TPU v7x, 128 devices: a whole 4x4x4 slice. The times are simulated.
128 devices in a mesh: logic: 8 (over z, core), slab: 16 (over y, x).
Axes of the slice: x: 4, y: 4, z: 4, core: 2. Of those that a mesh axis runs over, the one named last changes fastest.
Arguments:
- initial_heat_state: float32 [128, 512, 1024], P('slab', 'logic'), may hold values from 0 to 2
- dynamic_wattage: bfloat16 [262144, 256], P(('logic', 'slab')), may hold values from 0.099609375 to 1
- drain_multiplier: float32 [262144], P(('logic', 'slab')), may hold values from 0.2 to 2
- holder_processor: int32 [262144, 1], P(('logic', 'slab')), may hold values from 0 to 127; in each aligned block of 2048 rows (0 to 2047, 2048 to 4095, ...) at most 32 rows name the same one
- patch_target_slot: int32 [262144], P(('logic', 'slab')), may hold values from 0 to 2047
- active_patch_number: int32 [128], P(('logic', 'slab')), may hold values from 1024 to 2048, as said below
- prior_reduced_heat_map: float32 [128, 32, 4], replicated, may hold values from 0 to 2
- conductivity_lookup: float32 [8, 3], replicated, may hold values from 0.02 to 0.15
- substance_of_slab: int32 [128], replicated, may hold values from 0 to 7
Outputs:
- new_temperature: float32 [128, 512, 1024], P('slab', 'logic')
- coarse_map: float32 [128, 32, 4], replicated
Inputs may be any that keep to these rules, and one draw needn't show every extreme that they name: `holder_processor`: among the rows of one device, at most 32 name the same owner, a bound that some block reaches. `active_patch_number`: at least half the slots are live; some device has all 2048 live.
All inputs are finite; a program needn't handle non-finite values.
Results may differ from a plain program's by a relative error of at most 0.00069.
Values may be sent and summed in bfloat16 or wider, within the bound.
No kernel may reach another device: no remote copies, remote signals or barrier semaphores. Data moves between devices by JAX's collectives and lax.ppermute only.
A program may use at most 64 MiB of HBM per device.

v0:
```python
import jax
import jax.numpy as jnp
from jax import lax
from jax.sharding import PartitionSpec as P

STEPS = 4


LEAK_BETA = 0.7
THERMAL_FACTOR = 0.1


def padded(block, sides, width):
    for axis, dim in sides:
        count = lax.axis_size(axis)
        forward = [(i, i + 1) for i in range(count - 1)]
        backward = [(target, source) for source, target in forward]
        low = lax.ppermute(
            lax.slice_in_dim(block, block.shape[dim] - width, None, axis=dim), axis, forward
        )
        high = lax.ppermute(lax.slice_in_dim(block, 0, width, axis=dim), axis, backward)
        block = jnp.concatenate([low, block, high], axis=dim)
    return block


def conductances(conductivity_lookup, substance_of_slab, first, count, total):
    layers = first + jnp.arange(count, dtype=jnp.int32)

    def lookup(index):
        labels = substance_of_slab[jnp.clip(index, 0, total - 1)]
        match = (
            labels[:, None] == jnp.arange(conductivity_lookup.shape[0], dtype=jnp.int32)[None, :]
        )
        return jnp.sum(
            jnp.where(match[:, :, None], conductivity_lookup[None], jnp.float32(0.0)), axis=1
        )

    here = lookup(layers)
    above = lookup(layers + 1)
    below = lookup(layers - 1)
    higher_neighbour = 2.0 * here[:, 2] * above[:, 2] / (here[:, 2] + above[:, 2])
    lower_neighbour = 2.0 * here[:, 2] * below[:, 2] / (here[:, 2] + below[:, 2])
    shaped = lambda v: v.reshape(count, 1, 1)
    return (
        shaped(here[:, 0]),
        shaped(here[:, 1]),
        shaped(higher_neighbour),
        shaped(lower_neighbour),
    )


def march_forward(
    enlarged_slice,
    heat_input,
    horizontal_conductivity,
    vertical_conductivity,
    higher_neighbour,
    lower_neighbour,
    interior_part,
):
    center = enlarged_slice[1:-1, 1:-1]
    padded_x = jnp.pad(center, ((0, 0), (0, 0), (1, 1)))
    horizontal_flux = padded_x[:, :, 2:] + padded_x[:, :, :-2] - 2.0 * center
    vertical_flux = enlarged_slice[1:-1, 2:] + enlarged_slice[1:-1, :-2] - 2.0 * center
    heat_flow_higher = enlarged_slice[2:, 1:-1] - center
    heat_flow_lower = enlarged_slice[:-2, 1:-1] - center
    result = (
        center
        + horizontal_conductivity * horizontal_flux
        + vertical_conductivity * vertical_flux
        + higher_neighbour * heat_flow_higher
        + lower_neighbour * heat_flow_lower
        + THERMAL_FACTOR * heat_input
    )
    return jnp.where(interior_part, result, jnp.float32(0.0))


def per_device(
    initial_heat_state,
    dynamic_wattage,
    drain_multiplier,
    holder_processor,
    patch_target_slot,
    active_patch_number,
    prior_reduced_heat_map,
    conductivity_lookup,
    substance_of_slab,
):
    slab_count = lax.axis_size("slab")
    logic_count = lax.axis_size("logic")
    devices = slab_count * logic_count
    slab_thickness, owned_lines, line_span = initial_heat_state.shape
    partition_blocks = line_span // 256
    own_tiles = slab_thickness * owned_lines * partition_blocks
    total_layers = slab_thickness * slab_count
    total_rows = owned_lines * logic_count
    tiles = dynamic_wattage.shape[0]
    capacity = max(2, 2 * tiles // devices)
    owners = holder_processor[:, 0]
    live = jnp.arange(tiles, dtype=jnp.int32) < active_patch_number[0]
    slab_position = owners % slab_count * slab_thickness + patch_target_slot // (
        owned_lines * partition_blocks
    )
    line_position = (
        owners // slab_count * owned_lines + patch_target_slot // partition_blocks % owned_lines
    )
    column_position = patch_target_slot % partition_blocks
    reduced_current = prior_reduced_heat_map[slab_position, line_position // 16, column_position]
    power = (
        dynamic_wattage.astype(jnp.float32)
        * (1.0 + drain_multiplier * jnp.exp(LEAK_BETA * reduced_current))[:, None]
    ).astype(jnp.bfloat16)
    member = (owners[:, None] == jnp.arange(devices, dtype=jnp.int32)[None, :]) & live[:, None]
    member_int = member.astype(jnp.int32)
    rank = jnp.cumsum(member_int, axis=0) - 1
    slot = jnp.sum(rank * member_int, axis=1)
    destination = jnp.where(live, owners, devices)
    payload = (
        jnp.zeros((devices, capacity, 256), jnp.bfloat16)
        .at[destination, slot]
        .set(power, mode="drop")
    )
    labels = (
        jnp.full((devices, capacity), own_tiles, jnp.int32)
        .at[destination, slot]
        .set(patch_target_slot, mode="drop")
    )
    got_payload, got_labels = (
        lax.all_to_all(payload, ("logic", "slab"), split_axis=0, concat_axis=0, tiled=True),
        lax.all_to_all(labels, ("logic", "slab"), split_axis=0, concat_axis=0, tiled=True),
    )
    received = got_payload.reshape(devices * capacity, 256).astype(jnp.float32)
    received_labels = got_labels.reshape(devices * capacity)
    heat_input = jax.ops.segment_sum(received, received_labels, num_segments=own_tiles + 1)[
        :own_tiles
    ]
    heat_input = heat_input.reshape(slab_thickness, owned_lines, line_span)
    layer_start = lax.axis_index("slab") * slab_thickness
    row_start = lax.axis_index("logic") * owned_lines
    thermal_state = initial_heat_state
    for step in range(STEPS):
        enlarged_slice = padded(thermal_state, (("logic", 1), ("slab", 0)), 1)
        count = slab_thickness + 2 * 0
        first = layer_start - 0
        horizontal_conductivity, vertical_conductivity, higher_neighbour, lower_neighbour = (
            conductances(conductivity_lookup, substance_of_slab, first, count, total_layers)
        )
        layers = first + jnp.arange(count, dtype=jnp.int32)
        rows = row_start - 0 + jnp.arange(owned_lines + 2 * 0, dtype=jnp.int32)
        interior_part = ((layers >= 0) & (layers < total_layers))[:, None, None] & (
            (rows >= 0) & (rows < total_rows)
        )[None, :, None]
        thermal_state = march_forward(
            enlarged_slice,
            heat_input,
            horizontal_conductivity,
            vertical_conductivity,
            higher_neighbour,
            lower_neighbour,
            interior_part,
        )
    reduced_patch = thermal_state.reshape(
        slab_thickness, owned_lines // 16, 16, partition_blocks, 256
    ).mean(axis=(2, 4))
    gathered = lax.all_gather(reduced_patch.reshape(1, -1), ("logic", "slab"), axis=0, tiled=True)
    reduced_map = gathered.reshape(
        logic_count, slab_count, slab_thickness, owned_lines // 16, partition_blocks
    )
    reduced_map = jnp.transpose(reduced_map, (1, 2, 0, 3, 4)).reshape(
        total_layers, logic_count * owned_lines // 16, partition_blocks
    )
    return (thermal_state, reduced_map)


def solution(mesh):
    return jax.shard_map(
        per_device,
        mesh=mesh,
        in_specs=(
            P("slab", "logic", None),
            P(("logic", "slab"), None),
            P(("logic", "slab")),
            P(("logic", "slab"), None),
            P(("logic", "slab")),
            P(("logic", "slab")),
            P(),
            P(),
            P(),
        ),
        out_specs=(P("slab", "logic", None), P()),
        check_vma=False,
    )
```

profile of v0, /device:TPU:1, one launch (start us, length us, event | category | flops | bytes accessed | tf_op | source)
XLA Modules:
  0.0 275.2 jit_solution(5165405707344345658)
XLA Ops:
  1.8 4.9 %collective-permute-start.1 = (f32[8,1,1024]{2,1,0:T(1,128)S(1)}, f32[8,1,1024]{2,1,0:T(1,128)S(1)}, u32[]{:S(2)}, u32[]{:S(2)}) collective-permute-start(f32[8,1,1024]{2,1,0:T(1,128)S(1)} %get-tuple-element.29), channel_id=1, source_target_pairs={{0,16},{16,32},{32,48},{48,64},{64,80},{80,96},{96,112},{1,17},{17... | collective-permute-start | bytes 98312 | tf_op jit(solution)/shard_map/ppermute | solution.py:18
  12.9 8.1 %scatter_custom_fusion.1 = s32[4096]{0:T(1024)S(1)} fusion(s32[2048]{0:T(1024)S(1)} %get-tuple-element.36, s32[2048]{0:T(1024)S(1)} %copy-done.5, s32[]{:T(128)} %constant.118.clone.1), kind=kCustom, calls=%fused_computation.192 | custom fusion | bytes 16388
  21.7 10.2 %all-to-all-start = ((s32[128,1,32]{2,1,0:T(1,128)}), s32[128,1,32]{2,1,0:T(1,128)S(1)}, u32[]{:S(2)}, u32[]{:S(2)}) async-start(s32[128,1,32]{2,1,0:T(1,128)} %copy.36), calls=%async_computation | async-start | bytes 131072 | tf_op jit(solution)/shard_map/all_to_all | solution.py:130
  32.1 18.9 %gather_fusion.3 = f32[2048]{0:T(1024)S(1)} fusion(f32[128,32,4]{0,2,1:T(4,128)S(1)} %copy-done, s32[2048]{0:T(1024)S(1)} %fusion.88), kind=kCustom, calls=%fused_computation.3 | custom fusion | bytes 40960 | tf_op jit(solution)/shard_map/gather | solution.py:108
  51.0 11.8 %scatter_custom_fusion.2 = bf16[4096,256]{1,0:T(8,128)(2,1)} fusion(s32[2048]{0:T(1024)S(1)} %get-tuple-element.35, bf16[2048,256]{1,0:T(8,128)(2,1)S(1)} %copy-done.3, bf16[]{:T(256)} %constant.120.clone.1, f32[2048]{0:T(1024)S(1)} %multiply_add_fusion), kind=kCustom, calls=%fused_computation.116 | custom fusion | flops 1572864 | bytes 3153922
  62.8 10.2 %all-to-all-start.1 = ((bf16[128,32,256]{2,1,0:T(8,128)(2,1)}), bf16[128,32,256]{2,1,0:T(8,128)(2,1)}, u32[]{:S(2)}, u32[]{:S(2)}) async-start(bf16[128,32,256]{2,1,0:T(8,128)(2,1)} %bitcast.64), calls=%async_computation.1 | async-start | bytes 4194304 | tf_op jit(solution)/shard_map/all_to_all | solution.py:129
  78.3 4.0 %collective-permute-start.3 = (f32[1,66,1024]{2,1,0:T(8,128)S(1)}, f32[1,66,1024]{2,1,0:T(8,128)S(1)}, u32[]{:S(2)}, u32[]{:S(2)}) collective-permute-start(f32[1,66,1024]{2,1,0:T(8,128)S(1)} %get-tuple-element.22), channel_id=1, source_target_pairs={{0,1},{1,2},{2,3},{3,4},{4,5},{5,6},{6,7},{7,8},{8,9},{9,10},{10,1... | collective-permute-start | bytes 811016 | tf_op jit(solution)/shard_map/ppermute | solution.py:18
  82.3 20.6 %all-to-all-done.1 = bf16[128,32,256]{2,1,0:T(8,128)(2,1)} async-done(((bf16[128,32,256]{2,1,0:T(8,128)(2,1)}), bf16[128,32,256]{2,1,0:T(8,128)(2,1)}, u32[]{:S(2)}, u32[]{:S(2)}) %all-to-all-start.1) | async-done | bytes 2097184 | tf_op jit(solution)/shard_map/all_to_all | solution.py:129
  102.8 22.2 %scatter_custom_fusion = f32[2049,256]{1,0:T(8,128)S(1)} fusion(s32[4096]{0:T(1024)S(1)} %reshape.332, bf16[4096,256]{1,0:T(8,128)(2,1)} %bitcast.24, f32[]{:T(128)} %constant.114.clone.1), kind=kCustom, calls=%fused_computation.7 | custom fusion | flops 2097152 | bytes 4195332 | tf_op jit(solution)/shard_map/scatter-add | solution.py:134
  128.5 9.9 %fusion.10 = f32[8,64,1024]{2,1,0:T(8,128)S(1)} fusion(f32[8,64,1024]{2,1,0:T(8,128)S(1)} %mul.235, f32[8,64,1024]{2,1,0:T(8,128)} %param.9, f32[1,66,1024]{2,1,0:T(8,128)S(1)} %collective-permute-done.3, f32[8,1,1024]{2,1,0:T(1,128)S(1)} %collective-permute-done, f32[8,1,1024]{2,1,0:T(1,128)S(1)} %collective-permute-done.1, ...), kind=kLoop, calls=%fused_computation.25 | loop fusion | flops 13107200 | bytes 6898304 | tf_op jit(solution)/shard_map/jit(_where)/select_n | solution.py:75
  138.5 5.2 %collective-permute-start.5 = (f32[8,1,1024]{2,1,0:T(1,128)S(1)}, f32[8,1,1024]{2,1,0:T(1,128)S(1)}, u32[]{:S(2)}, u32[]{:S(2)}) collective-permute-start(f32[8,1,1024]{2,1,0:T(1,128)S(1)} %get-tuple-element.27), channel_id=1, source_target_pairs={{0,16},{16,32},{32,48},{48,64},{64,80},{80,96},{96,112},{1,17},{17... | collective-permute-start | bytes 98312 | tf_op jit(solution)/shard_map/ppermute | solution.py:18
  145.6 3.3 %collective-permute-done.4 = f32[8,1,1024]{2,1,0:T(1,128)S(1)} collective-permute-done((f32[8,1,1024]{2,1,0:T(1,128)S(1)}, f32[8,1,1024]{2,1,0:T(1,128)S(1)}, u32[]{:S(2)}, u32[]{:S(2)}) %collective-permute-start.4) | collective-permute-done | bytes 32800 | tf_op jit(solution)/shard_map/ppermute | solution.py:21
  150.3 4.0 %collective-permute-start.7 = (f32[1,66,1024]{2,1,0:T(8,128)S(1)}, f32[1,66,1024]{2,1,0:T(8,128)S(1)}, u32[]{:S(2)}, u32[]{:S(2)}) collective-permute-start(f32[1,66,1024]{2,1,0:T(8,128)S(1)} %get-tuple-element.20), channel_id=1, source_target_pairs={{0,1},{1,2},{2,3},{3,4},{4,5},{5,6},{6,7},{7,8},{8,9},{9,10},{10,1... | collective-permute-start | bytes 811016 | tf_op jit(solution)/shard_map/ppermute | solution.py:18
  154.3 3.7 %collective-permute-done.6 = f32[1,66,1024]{2,1,0:T(8,128)S(1)} collective-permute-done((f32[1,66,1024]{2,1,0:T(8,128)S(1)}, f32[1,66,1024]{2,1,0:T(8,128)S(1)}, u32[]{:S(2)}, u32[]{:S(2)}) %collective-permute-start.6) | collective-permute-done | bytes 270368 | tf_op jit(solution)/shard_map/ppermute | solution.py:21
  163.1 3.9 %collective-permute-start.9 = (f32[8,1,1024]{2,1,0:T(1,128)S(1)}, f32[8,1,1024]{2,1,0:T(1,128)S(1)}, u32[]{:S(2)}, u32[]{:S(2)}) collective-permute-start(f32[8,1,1024]{2,1,0:T(1,128)S(1)} %get-tuple-element.25), channel_id=1, source_target_pairs={{0,16},{16,32},{32,48},{48,64},{64,80},{80,96},{96,112},{1,17},{17... | collective-permute-start | bytes 98312 | tf_op jit(solution)/shard_map/ppermute | solution.py:18
  168.9 3.3 %collective-permute-done.8 = f32[8,1,1024]{2,1,0:T(1,128)S(1)} collective-permute-done((f32[8,1,1024]{2,1,0:T(1,128)S(1)}, f32[8,1,1024]{2,1,0:T(1,128)S(1)}, u32[]{:S(2)}, u32[]{:S(2)}) %collective-permute-start.8) | collective-permute-done | bytes 32800 | tf_op jit(solution)/shard_map/ppermute | solution.py:21
  173.6 4.8 %collective-permute-start.11 = (f32[1,66,1024]{2,1,0:T(8,128)S(1)}, f32[1,66,1024]{2,1,0:T(8,128)S(1)}, u32[]{:S(2)}, u32[]{:S(2)}) collective-permute-start(f32[1,66,1024]{2,1,0:T(8,128)S(1)} %get-tuple-element.18), channel_id=1, source_target_pairs={{0,1},{1,2},{2,3},{3,4},{4,5},{5,6},{6,7},{7,8},{8,9},{9,10},{10,1... | collective-permute-start | bytes 811016 | tf_op jit(solution)/shard_map/ppermute | solution.py:18
  178.3 3.4 %collective-permute-done.10 = f32[1,66,1024]{2,1,0:T(8,128)S(1)} collective-permute-done((f32[1,66,1024]{2,1,0:T(8,128)S(1)}, f32[1,66,1024]{2,1,0:T(8,128)S(1)}, u32[]{:S(2)}, u32[]{:S(2)}) %collective-permute-start.10) | collective-permute-done | bytes 270368 | tf_op jit(solution)/shard_map/ppermute | solution.py:21
  186.8 4.3 %collective-permute-start.13 = (f32[8,1,1024]{2,1,0:T(1,128)S(1)}, f32[8,1,1024]{2,1,0:T(1,128)S(1)}, u32[]{:S(2)}, u32[]{:S(2)}) collective-permute-start(f32[8,1,1024]{2,1,0:T(1,128)S(1)} %get-tuple-element.23), channel_id=1, source_target_pairs={{0,16},{16,32},{32,48},{48,64},{64,80},{80,96},{96,112},{1,17},{17... | collective-permute-start | bytes 98312 | tf_op jit(solution)/shard_map/ppermute | solution.py:18
  193.1 3.3 %collective-permute-done.12 = f32[8,1,1024]{2,1,0:T(1,128)S(1)} collective-permute-done((f32[8,1,1024]{2,1,0:T(1,128)S(1)}, f32[8,1,1024]{2,1,0:T(1,128)S(1)}, u32[]{:S(2)}, u32[]{:S(2)}) %collective-permute-start.12) | collective-permute-done | bytes 32800 | tf_op jit(solution)/shard_map/ppermute | solution.py:21
  197.8 5.9 %collective-permute-start.15 = (f32[1,66,1024]{2,1,0:T(8,128)S(1)}, f32[1,66,1024]{2,1,0:T(8,128)S(1)}, u32[]{:S(2)}, u32[]{:S(2)}) collective-permute-start(f32[1,66,1024]{2,1,0:T(8,128)S(1)} %get-tuple-element.16), channel_id=1, source_target_pairs={{0,1},{1,2},{2,3},{3,4},{4,5},{5,6},{6,7},{7,8},{8,9},{9,10},{10,1... | collective-permute-start | bytes 811016 | tf_op jit(solution)/shard_map/ppermute | solution.py:18
  203.7 3.4 %collective-permute-done.14 = f32[1,66,1024]{2,1,0:T(8,128)S(1)} collective-permute-done((f32[1,66,1024]{2,1,0:T(8,128)S(1)}, f32[1,66,1024]{2,1,0:T(8,128)S(1)}, u32[]{:S(2)}, u32[]{:S(2)}) %collective-permute-start.14) | collective-permute-done | bytes 270368 | tf_op jit(solution)/shard_map/ppermute | solution.py:21
  208.8 4.3 %fusion.37 = f32[8,64,1024]{2,1,0:T(8,128)} fusion(f32[8,64,1024]{2,1,0:T(8,128)S(1)} %mul.235, f32[8,64,1024]{2,1,0:T(8,128)S(1)} %fusion.28, f32[1,66,1024]{2,1,0:T(8,128)S(1)} %collective-permute-done.15, f32[8,1,1024]{2,1,0:T(1,128)S(1)} %collective-permute-done.12, f32[8,1,1024]{2,1,0:T(1,128)S(1)} %collective-permute-done.13, ...), kind=kLoop, calls=%fused_computation.52 | loop fusion | flops 13107200 | bytes 6898304 | tf_op jit(solution)/shard_map/jit(_where)/select_n | solution.py:75
  215.8 57.5 %all-gather = f32[128,1,128]{2,1,0:T(1,128)S(1)} all-gather(f32[1,1,128]{2,1,0:T(1,128)S(1)} %reshape.367), channel_id=1, replica_groups=mesh['logic'=8,'slab'=16] {'logic','slab'}, dimensions={0}, use_global_device_ids=true | all-gather | bytes 66048 | tf_op jit(solution)/shard_map/all_gather | solution.py:165
  (98 shorter events, 42.3 us)
Async XLA Ops:
  0.6 31.4 %copy-start = (f32[128,32,4]{0,2,1:T(4,128)S(1)}, f32[128,32,4]{0,2,1:T(4,128)}, u32[]{:S(2)}) copy-start(f32[128,32,4]{0,2,1:T(4,128)} %param.15) | copy-start | bytes 196612
  1.8 75.1 %collective-permute-start.1 = (f32[8,1,1024]{2,1,0:T(1,128)S(1)}, f32[8,1,1024]{2,1,0:T(1,128)S(1)}, u32[]{:S(2)}, u32[]{:S(2)}) collective-permute-start(f32[8,1,1024]{2,1,0:T(1,128)S(1)} %get-tuple-element.29), channel_id=1, source_target_pairs={{0,16},{16,32},{32,48},{48,64},{64,80},{80,96},{96,112},{1,17},{17... | collective-permute-start | bytes 98312 | tf_op jit(solution)/shard_map/ppermute | solution.py:18
  6.7 70.2 %collective-permute-start = (f32[8,1,1024]{2,1,0:T(1,128)S(1)}, f32[8,1,1024]{2,1,0:T(1,128)S(1)}, u32[]{:S(2)}, u32[]{:S(2)}) collective-permute-start(f32[8,1,1024]{2,1,0:T(1,128)S(1)} %get-tuple-element.30), channel_id=1, source_target_pairs={{16,0},{32,16},{48,32},{64,48},{80,64},{96,80},{112,96},{17,1},{33... | collective-permute-start | bytes 98312 | tf_op jit(solution)/shard_map/ppermute | solution.py:21
  21.7 41.0 %all-to-all-start = ((s32[128,1,32]{2,1,0:T(1,128)}), s32[128,1,32]{2,1,0:T(1,128)S(1)}, u32[]{:S(2)}, u32[]{:S(2)}) async-start(s32[128,1,32]{2,1,0:T(1,128)} %copy.36), calls=%async_computation | async-start | bytes 131072 | tf_op jit(solution)/shard_map/all_to_all | solution.py:130
  32.0 18.9 %copy-start.6 = (f32[2048]{0:T(1024)S(1)}, f32[2048]{0:T(1024)}, u32[]{:S(2)}) copy-start(f32[2048]{0:T(1024)} %param.11) | copy-start | bytes 24580
  32.1 18.9 %copy-start.3 = (bf16[2048,256]{1,0:T(8,128)(2,1)S(1)}, bf16[2048,256]{1,0:T(8,128)(2,1)}, u32[]{:S(2)}) copy-start(bf16[2048,256]{1,0:T(8,128)(2,1)} %param.10) | copy-start | bytes 3145732
  62.8 10.3 %copy-start.1 = (s32[128]{0:T(128)S(1)}, s32[128]{0:T(128)}, u32[]{:S(2)}) copy-start(s32[128]{0:T(128)} %param.17) | copy-start | bytes 1540
  62.8 12.5 %copy-start.7 = (f32[8,3]{0,1:T(4,128)S(1)}, f32[8,3]{0,1:T(4,128)}, u32[]{:S(2)}) copy-start(f32[8,3]{0,1:T(4,128)} %param.16) | copy-start | bytes 292
  62.8 14.1 %copy-start.2 = (f32[8,64,1024]{2,1,0:T(8,128)S(1)}, f32[8,64,1024]{2,1,0:T(8,128)}, u32[]{:S(2)}) copy-start(f32[8,64,1024]{2,1,0:T(8,128)} %param.9) | copy-start | bytes 6291460
  62.8 40.1 %all-to-all-start.1 = ((bf16[128,32,256]{2,1,0:T(8,128)(2,1)}), bf16[128,32,256]{2,1,0:T(8,128)(2,1)}, u32[]{:S(2)}, u32[]{:S(2)}) async-start(bf16[128,32,256]{2,1,0:T(8,128)(2,1)} %bitcast.64), calls=%async_computation.1 | async-start | bytes 4194304 | tf_op jit(solution)/shard_map/all_to_all | solution.py:129
  77.0 51.5 %collective-permute-start.2 = (f32[1,66,1024]{2,1,0:T(8,128)S(1)}, f32[1,66,1024]{2,1,0:T(8,128)S(1)}, u32[]{:S(2)}, u32[]{:S(2)}) collective-permute-start(f32[1,66,1024]{2,1,0:T(8,128)S(1)} %get-tuple-element.21), channel_id=1, source_target_pairs={{1,0},{2,1},{3,2},{4,3},{5,4},{6,5},{7,6},{8,7},{9,8},{10,9},{11,1... | collective-permute-start | bytes 811016 | tf_op jit(solution)/shard_map/ppermute | solution.py:21
  78.3 50.2 %collective-permute-start.3 = (f32[1,66,1024]{2,1,0:T(8,128)S(1)}, f32[1,66,1024]{2,1,0:T(8,128)S(1)}, u32[]{:S(2)}, u32[]{:S(2)}) collective-permute-start(f32[1,66,1024]{2,1,0:T(8,128)S(1)} %get-tuple-element.22), channel_id=1, source_target_pairs={{0,1},{1,2},{2,3},{3,4},{4,5},{5,6},{6,7},{7,8},{8,9},{9,10},{10,1... | collective-permute-start | bytes 811016 | tf_op jit(solution)/shard_map/ppermute | solution.py:18
  138.5 7.2 %collective-permute-start.5 = (f32[8,1,1024]{2,1,0:T(1,128)S(1)}, f32[8,1,1024]{2,1,0:T(1,128)S(1)}, u32[]{:S(2)}, u32[]{:S(2)}) collective-permute-start(f32[8,1,1024]{2,1,0:T(1,128)S(1)} %get-tuple-element.27), channel_id=1, source_target_pairs={{0,16},{16,32},{32,48},{48,64},{64,80},{80,96},{96,112},{1,17},{17... | collective-permute-start | bytes 98312 | tf_op jit(solution)/shard_map/ppermute | solution.py:18
  143.7 5.2 %collective-permute-start.4 = (f32[8,1,1024]{2,1,0:T(1,128)S(1)}, f32[8,1,1024]{2,1,0:T(1,128)S(1)}, u32[]{:S(2)}, u32[]{:S(2)}) collective-permute-start(f32[8,1,1024]{2,1,0:T(1,128)S(1)} %get-tuple-element.28), channel_id=1, source_target_pairs={{16,0},{32,16},{48,32},{64,48},{80,64},{96,80},{112,96},{17,1},{33... | collective-permute-start | bytes 98312 | tf_op jit(solution)/shard_map/ppermute | solution.py:21
  149.0 9.0 %collective-permute-start.6 = (f32[1,66,1024]{2,1,0:T(8,128)S(1)}, f32[1,66,1024]{2,1,0:T(8,128)S(1)}, u32[]{:S(2)}, u32[]{:S(2)}) collective-permute-start(f32[1,66,1024]{2,1,0:T(8,128)S(1)} %get-tuple-element.19), channel_id=1, source_target_pairs={{1,0},{2,1},{3,2},{4,3},{5,4},{6,5},{7,6},{8,7},{9,8},{10,9},{11,1... | collective-permute-start | bytes 811016 | tf_op jit(solution)/shard_map/ppermute | solution.py:21
  150.3 9.4 %collective-permute-start.7 = (f32[1,66,1024]{2,1,0:T(8,128)S(1)}, f32[1,66,1024]{2,1,0:T(8,128)S(1)}, u32[]{:S(2)}, u32[]{:S(2)}) collective-permute-start(f32[1,66,1024]{2,1,0:T(8,128)S(1)} %get-tuple-element.20), channel_id=1, source_target_pairs={{0,1},{1,2},{2,3},{3,4},{4,5},{5,6},{6,7},{7,8},{8,9},{9,10},{10,1... | collective-permute-start | bytes 811016 | tf_op jit(solution)/shard_map/ppermute | solution.py:18
  163.1 5.8 %collective-permute-start.9 = (f32[8,1,1024]{2,1,0:T(1,128)S(1)}, f32[8,1,1024]{2,1,0:T(1,128)S(1)}, u32[]{:S(2)}, u32[]{:S(2)}) collective-permute-start(f32[8,1,1024]{2,1,0:T(1,128)S(1)} %get-tuple-element.25), channel_id=1, source_target_pairs={{0,16},{16,32},{32,48},{48,64},{64,80},{80,96},{96,112},{1,17},{17... | collective-permute-start | bytes 98312 | tf_op jit(solution)/shard_map/ppermute | solution.py:18
  167.0 5.2 %collective-permute-start.8 = (f32[8,1,1024]{2,1,0:T(1,128)S(1)}, f32[8,1,1024]{2,1,0:T(1,128)S(1)}, u32[]{:S(2)}, u32[]{:S(2)}) collective-permute-start(f32[8,1,1024]{2,1,0:T(1,128)S(1)} %get-tuple-element.26), channel_id=1, source_target_pairs={{16,0},{32,16},{48,32},{64,48},{80,64},{96,80},{112,96},{17,1},{33... | collective-permute-start | bytes 98312 | tf_op jit(solution)/shard_map/ppermute | solution.py:21
  172.3 9.4 %collective-permute-start.10 = (f32[1,66,1024]{2,1,0:T(8,128)S(1)}, f32[1,66,1024]{2,1,0:T(8,128)S(1)}, u32[]{:S(2)}, u32[]{:S(2)}) collective-permute-start(f32[1,66,1024]{2,1,0:T(8,128)S(1)} %get-tuple-element.17), channel_id=1, source_target_pairs={{1,0},{2,1},{3,2},{4,3},{5,4},{6,5},{7,6},{8,7},{9,8},{10,9},{11,1... | collective-permute-start | bytes 811016 | tf_op jit(solution)/shard_map/ppermute | solution.py:21
  173.6 9.9 %collective-permute-start.11 = (f32[1,66,1024]{2,1,0:T(8,128)S(1)}, f32[1,66,1024]{2,1,0:T(8,128)S(1)}, u32[]{:S(2)}, u32[]{:S(2)}) collective-permute-start(f32[1,66,1024]{2,1,0:T(8,128)S(1)} %get-tuple-element.18), channel_id=1, source_target_pairs={{0,1},{1,2},{2,3},{3,4},{4,5},{5,6},{6,7},{7,8},{8,9},{9,10},{10,1... | collective-permute-start | bytes 811016 | tf_op jit(solution)/shard_map/ppermute | solution.py:18
  186.8 6.3 %collective-permute-start.13 = (f32[8,1,1024]{2,1,0:T(1,128)S(1)}, f32[8,1,1024]{2,1,0:T(1,128)S(1)}, u32[]{:S(2)}, u32[]{:S(2)}) collective-permute-start(f32[8,1,1024]{2,1,0:T(1,128)S(1)} %get-tuple-element.23), channel_id=1, source_target_pairs={{0,16},{16,32},{32,48},{48,64},{64,80},{80,96},{96,112},{1,17},{17... | collective-permute-start | bytes 98312 | tf_op jit(solution)/shard_map/ppermute | solution.py:18
  191.2 5.2 %collective-permute-start.12 = (f32[8,1,1024]{2,1,0:T(1,128)S(1)}, f32[8,1,1024]{2,1,0:T(1,128)S(1)}, u32[]{:S(2)}, u32[]{:S(2)}) collective-permute-start(f32[8,1,1024]{2,1,0:T(1,128)S(1)} %get-tuple-element.24), channel_id=1, source_target_pairs={{16,0},{32,16},{48,32},{64,48},{80,64},{96,80},{112,96},{17,1},{33... | collective-permute-start | bytes 98312 | tf_op jit(solution)/shard_map/ppermute | solution.py:21
  196.5 10.6 %collective-permute-start.14 = (f32[1,66,1024]{2,1,0:T(8,128)S(1)}, f32[1,66,1024]{2,1,0:T(8,128)S(1)}, u32[]{:S(2)}, u32[]{:S(2)}) collective-permute-start(f32[1,66,1024]{2,1,0:T(8,128)S(1)} %get-tuple-element.15), channel_id=1, source_target_pairs={{1,0},{2,1},{3,2},{4,3},{5,4},{6,5},{7,6},{8,7},{9,8},{10,9},{11,1... | collective-permute-start | bytes 811016 | tf_op jit(solution)/shard_map/ppermute | solution.py:21
  197.8 11.0 %collective-permute-start.15 = (f32[1,66,1024]{2,1,0:T(8,128)S(1)}, f32[1,66,1024]{2,1,0:T(8,128)S(1)}, u32[]{:S(2)}, u32[]{:S(2)}) collective-permute-start(f32[1,66,1024]{2,1,0:T(8,128)S(1)} %get-tuple-element.16), channel_id=1, source_target_pairs={{0,1},{1,2},{2,3},{3,4},{4,5},{5,6},{6,7},{7,8},{8,9},{9,10},{10,1... | collective-permute-start | bytes 811016 | tf_op jit(solution)/shard_map/ppermute | solution.py:18
  (5 other events, 8.3 us)
where the time goes:
time: 276 us; the launch traced here: 275 us
  starting transfers between devices  70.3 us (25%)
  other arithmetic  60.4 us (22%)
  blocking collectives  57.5 us (21%)
  waiting for transfers between devices  46.2 us (17%)
  local copies, waits for them, and re-layouts  38.9 us (14%)
    all_gather x1, blocking collectives, per_device(): lax.all_gather(reduced_patch.reshape(1, -1), ('logic', 'slab'), axis=0, t...  57.5 us
    ppermute x8, starting transfers between devices, padded(): lax.ppermute(lax.slice_in_dim(block, block.shape[dim] - width, None, axis...  37.1 us
    scatter-add x1, other arithmetic, per_device(): jax.ops.segment_sum(received, received_labels, num_segments=own_tiles + 1)  22.2 us
    select_n x4, other arithmetic, march_forward(): return jnp.where(interior_part, result, jnp.float32(0.0))  20.8 us
    all_to_all x1, waiting for transfers between devices, per_device(): lax.all_to_all(payload, ('logic', 'slab'), split_axis=0, concat_axis=0, t...  20.6 us
    ppermute x8, waiting for transfers between devices, padded(): lax.ppermute(lax.slice_in_dim(block, 0, width, axis=dim), axis, backward)  20.3 us
    gather x1, local copies, waits for them, and re-layouts, per_device(): prior_reduced_heat_map[slab_position, line_position // 16, column_position]  18.9 us
    ppermute x8, starting transfers between devices, padded(): lax.ppermute(lax.slice_in_dim(block, 0, width, axis=dim), axis, backward)  12.9 us
  transfers between devices with their start and end apart: 18, of which 10 were waited for; matrix products, arithmetic and copies ran while one was open for 26% of the time, Pallas kernels for 0%

commit v1 on v0

v1 whole, which is shorter than its diff:
```python
import functools

import jax
import jax.numpy as jnp
from jax import lax
from jax.experimental import pallas as pl
from jax.experimental.pallas import tpu as pltpu
from jax.sharding import PartitionSpec as P

LEAK_BETA = 0.7
THERMAL_FACTOR = 0.1

DEV = 128
CAP = 32
TILES = 2048
NZ = 8
NY = 64
LAYERS = 128
SLABS = 16
LOGICS = 8
ROWS = 72
GROUP = 16
VMEM = 48 * 1024 * 1024
F32 = jnp.float32
BF16 = jnp.bfloat16
I32 = jnp.int32


def iota(shape, dim):
    return lax.broadcasted_iota(I32, shape, dim)


def pack_kernel(
    count_ref, owner_ref, target_ref, drain_ref, prior_ref, watt_ref, out_ref,
    member_ref, pick_ref, high_ref, low_ref, power_ref,
):
    owner = owner_ref[...]
    target = target_ref[...]
    live = iota((1, TILES), 1) < count_ref[0]
    layer = (owner & (SLABS - 1)) * NZ + (target >> 8)
    column = (owner >> 4) * 16 + ((target >> 6) & 3) * 4 + (target & 3)
    at_layer = jnp.where(iota((LAYERS, TILES), 0) == layer, 1.0, 0.0).astype(BF16)
    prior = prior_ref[...]
    first = prior.astype(BF16)
    rest = prior - first.astype(F32)
    second = rest.astype(BF16)
    third = (rest - second.astype(F32)).astype(BF16)
    lookup = lambda part: lax.dot_general(
        part, at_layer, (((0,), (0,)), ((), ())), preferred_element_type=F32
    )
    picked = lookup(first) + lookup(second) + lookup(third)
    heat = jnp.sum(
        jnp.where(iota((LAYERS, TILES), 0) == column, picked, 0.0), axis=0, keepdims=True
    )
    scale = 1.0 + drain_ref[...] * jnp.exp(LEAK_BETA * heat)
    for b in range(TILES // 128):
        rows = pl.ds(128 * b, 128)
        spread = jnp.transpose(jnp.broadcast_to(scale[:, 128 * b : 128 * b + 128], (128, 128)))
        for h in range(2):
            cols = pl.ds(128 * h, 128)
            power_ref[rows, cols] = (watt_ref[rows, cols].astype(F32) * spread).astype(BF16)
    member = jnp.where(iota((DEV, TILES), 0) == jnp.where(live, owner, -1), 1.0, 0.0)
    member_ref[...] = member
    before = jnp.where(iota((256, 256), 0) < iota((256, 256), 1), 1.0, 0.0).astype(BF16)
    carry = jnp.zeros((DEV, 1), F32)
    ranks = []
    for b in range(TILES // 256):
        part = member[:, 256 * b : 256 * b + 256]
        earlier = jnp.dot(part.astype(BF16), before, preferred_element_type=F32) + carry
        ranks.append(jnp.sum(earlier * part, axis=0, keepdims=True))
        carry = carry + jnp.sum(part, axis=1, keepdims=True)
    rank = jnp.where(live, jnp.concatenate(ranks, axis=1).astype(I32), -1)
    pick_ref[...] = jnp.where(iota((CAP, TILES), 0) == rank, 1.0, 0.0).astype(BF16)
    slot = (iota((128, TILES), 0) & (CAP - 1)) == rank
    flat = member.astype(BF16)
    spot = lambda value: lax.dot_general(
        flat,
        jnp.where(slot, value.astype(F32), 0.0).astype(BF16),
        (((1,), (1,)), ((), ())),
        preferred_element_type=F32,
    )
    high_ref[...] = spot((target >> 6) + 1)
    low_ref[...] = spot(target & 63)
    row8 = iota((8, 128), 0)

    def group(g, _):
        pick = pick_ref[...]
        parts = []
        for j in range(GROUP):
            d = g * GROUP + j
            parts.append(pick * member_ref[pl.ds(d, 1), :].astype(BF16))
            label = jnp.where(
                row8 == 0,
                high_ref[pl.ds(d, 1), :],
                jnp.where(row8 == 1, low_ref[pl.ds(d, 1), :], 0.0),
            )
            out_ref[d, 64:72, :] = label.astype(BF16)
        packed = jnp.dot(
            jnp.concatenate(parts, axis=0), power_ref[...], preferred_element_type=F32
        ).astype(BF16)
        here = pl.ds(g * GROUP, GROUP)
        out_ref[here, 0:32, :] = packed[:, :128].reshape(GROUP, CAP, 128)
        out_ref[here, 32:64, :] = packed[:, 128:].reshape(GROUP, CAP, 128)
        return 0

    lax.fori_loop(0, DEV // GROUP, group, 0)


def scatter_kernel(got_ref, source_ref, low_ref, high_ref, front_ref, back_ref, label_ref):
    labels = got_ref[:, 64:72, :].reshape(DEV * 8, 128)
    row = iota((DEV * 8, 128), 0)
    lane = iota((DEV * 8, 128), 1)
    labels = jnp.where((lane >> 5) == ((row >> 3) & 3), labels.astype(F32), 0.0).astype(BF16)
    g = iota((32, DEV * 8), 0)
    col = iota((32, DEV * 8), 1)
    weight = jnp.where((col & 7) == 0, 64.0, jnp.where((col & 7) == 1, 1.0, 0.0))
    weight = jnp.where((col >> 5) == g, weight, 0.0).astype(BF16)
    target = jnp.dot(weight, labels, preferred_element_type=F32).astype(I32) - 64
    label_ref[...] = target
    left = got_ref[:, 0:32, :].reshape(DEV * CAP, 128)
    right = got_ref[:, 32:64, :].reshape(DEV * CAP, 128)
    both = jnp.concatenate([left, right], axis=1)
    wanted = iota((512, 128), 0) * 4
    for c in range(4):
        chosen = jnp.concatenate(
            [
                jnp.where(wanted == label_ref[k : k + 1, :] - c, 1.0, 0.0).astype(BF16)
                for k in range(32)
            ],
            axis=1,
        )
        total = THERMAL_FACTOR * jnp.dot(chosen, both, preferred_element_type=F32)
        for h in range(2):
            xb = 2 * c + h
            part = total[:, 128 * h : 128 * h + 128]
            cells = part.reshape(NZ * 8, 8, 128)
            source_ref[:, xb] = cells
            short = part.astype(BF16).reshape(NZ * 4, 16, 128)
            low_ref[:, xb] = short[:12]
            high_ref[:, xb] = short[20:]
            for z in range(NZ):
                front_ref[z, xb] = cells[8 * z].astype(BF16)
                back_ref[z, xb] = cells[8 * z + 7].astype(BF16)


def fill_coefficients(coef_ref, table_ref, label_ref, halo):
    base = lax.axis_index("slab") * NZ - halo
    spot = iota((8, 128), 0) * 128 + iota((8, 128), 1)

    def layer(i, _):
        z = base + i
        inside = jnp.where((z >= 0) & (z < LAYERS), 1.0, 0.0).astype(F32)
        material = lambda at: label_ref[jnp.clip(at, 0, LAYERS - 1)]
        here = material(z)
        splat = lambda m, k: jnp.full((8, 128), table_ref[m, k], F32)
        kx = splat(here, 0)
        ky = splat(here, 1)
        a = splat(here, 2)
        above = splat(material(z + 1), 2)
        below = splat(material(z - 1), 2)
        up = 2.0 * a * above / (a + above)
        down = 2.0 * a * below / (a + below)
        keep = jnp.full((8, 128), inside, F32)
        coef_ref[i, 0] = keep * (1.0 - 2.0 * kx - 2.0 * ky - up - down)
        coef_ref[i, 1] = keep * jnp.where(spot == 0, 0.0, kx)
        coef_ref[i, 2] = keep * jnp.where(spot == 1023, 0.0, kx)
        coef_ref[i, 3] = keep * ky
        coef_ref[i, 4] = keep * up
        coef_ref[i, 5] = keep * down
        return 0

    lax.fori_loop(0, NZ + 2 * halo, layer, 0)


def diffuse(coef_ref, read, write, layers, rows, low, high):
    lane = iota((8, 128), 1)

    def layer(z, _):
        coef = [coef_ref[z, j] for j in range(6)]
        before, cell = read(z, rows[0] - 1), read(z, rows[0])
        for y in range(rows[0], rows[1]):
            after = read(z, y + 1)
            step = pltpu.roll(cell, 127, 1)
            right = jnp.where(lane == 127, pltpu.roll(step, 7, 0), step)
            step = pltpu.roll(cell, 1, 1)
            left = jnp.where(lane == 0, pltpu.roll(step, 1, 0), step)
            value = (
                coef[0] * cell
                + coef[1] * left
                + coef[2] * right
                + coef[3] * (before + after)
                + coef[4] * read(z + 1, y)
                + coef[5] * read(z - 1, y)
            )
            if y < 0:
                value = value * low
            if y >= NY:
                value = value * high
            write(z, y, value)
            before, cell = cell, after
        return 0

    lax.fori_loop(layers[0], layers[1], layer, 0)


def edges():
    at = lax.axis_index("logic")
    low = jnp.full((8, 128), jnp.where(at > 0, 1.0, 0.0), F32)
    high = jnp.full((8, 128), jnp.where(at < LOGICS - 1, 1.0, 0.0), F32)
    return low, high


def row_of(z, y, halo):
    return pl.ds(pl.multiple_of((z * (NY + 8) + (y + 4)) * 8, 8), 8)


def temperature_kernel(
    table_ref, label_ref, state_ref, low_ref, high_ref, front_ref, back_ref,
    corner_low_ref, corner_high_ref, out_ref, coef_ref, cells_ref, a_ref, b_ref,
):
    halo = 4
    fill_coefficients(coef_ref, table_ref, label_ref, halo)

    def spread(z, block, value):
        for xb in range(8):
            cells_ref[z, block, pl.ds(xb * 8, 8), :] = value[:, 128 * xb : 128 * xb + 128]

    def gather(z, rows):
        for y in rows:
            block, at = (y + 8) // 8, (y + 8) % 8
            a_ref[row_of(z, y, halo), :] = cells_ref[z, block, pl.ds(at, 8, stride=8), :]

    def own(z, _):
        for block in range(8):
            spread(z + halo, block + 1, state_ref[z, 8 * block : 8 * block + 8, :])
        spread(z + halo, 0, front_ref[z].astype(F32))
        spread(z + halo, 9, back_ref[z].astype(F32))
        gather(z + halo, range(-4, NY + 4))
        return 0

    lax.fori_loop(0, NZ, own, 0)

    def outer(z, _):
        for base, body, corner in ((0, low_ref, corner_low_ref), (12, high_ref, corner_high_ref)):
            for block in range(4):
                two = body[z, 16 * block : 16 * block + 16, :].astype(F32)
                spread(z + base, 2 * block + 1, two[:8])
                spread(z + base, 2 * block + 2, two[8:])
            spread(z + base, 0, corner[0, z].astype(F32))
            spread(z + base, 9, corner[1, z].astype(F32))
            gather(z + base, range(-4, NY + 4))
        return 0

    lax.fori_loop(0, halo, outer, 0)
    low, high = edges()
    bufs = (a_ref, b_ref)
    for step in range(4):
        src, dst = bufs[step % 2], bufs[(step + 1) % 2]
        reach = 3 - step

        def read(z, y, src=src):
            return src[row_of(z, y, halo), :]

        def write(z, y, value, dst=dst, step=step):
            if step == 3:
                out_ref[pl.ds(pl.multiple_of(((z - halo) * NY + y) * 8, 8), 8), :] = value
            else:
                dst[row_of(z, y, halo), :] = value

        diffuse(
            coef_ref, read, write, (halo - reach, halo + NZ + reach), (-reach, NY + reach), low, high
        )


def source_kernel(
    table_ref, label_ref, source_ref, base_ref, low_ref, high_ref, front_ref, back_ref,
    corner_low_ref, corner_high_ref, out_ref, coarse_ref, coef_ref, cells_ref, s_ref, a_ref, b_ref,
    sums_ref,
):
    halo = 3
    fill_coefficients(coef_ref, table_ref, label_ref, halo)

    def gather(z, rows):
        for y in rows:
            block, at = (y + 8) // 8, (y + 8) % 8
            s_ref[row_of(z, y, halo), :] = cells_ref[z, block, pl.ds(at, 8, stride=8), :]

    def own(z, _):
        for y in range(NY):
            start = (z * 8 + y // 8) * 64 + y % 8
            s_ref[row_of(z + halo, y, halo), :] = source_ref[pl.ds(start, 8, stride=8), :]
        for xb in range(8):
            cells_ref[z + halo, 0, pl.ds(xb * 8, 8), :] = front_ref[z, xb].astype(F32)
            cells_ref[z + halo, 9, pl.ds(xb * 8, 8), :] = back_ref[z, xb].astype(F32)
        gather(z + halo, (-3, -2, -1, NY, NY + 1, NY + 2))
        return 0

    lax.fori_loop(0, NZ, own, 0)

    def outer(z, _):
        for base, body, corner in ((0, low_ref, corner_low_ref), (11, high_ref, corner_high_ref)):
            for xb in range(8):
                for block in range(4):
                    two = body[z * 4 + block, xb].astype(F32)
                    cells_ref[z + base, 2 * block + 1, pl.ds(xb * 8, 8), :] = two[:8]
                    cells_ref[z + base, 2 * block + 2, pl.ds(xb * 8, 8), :] = two[8:]
                cells_ref[z + base, 0, pl.ds(xb * 8, 8), :] = corner[0, z, xb].astype(F32)
                cells_ref[z + base, 9, pl.ds(xb * 8, 8), :] = corner[1, z, xb].astype(F32)
            gather(z + base, range(-3, NY + 3))
        return 0

    lax.fori_loop(0, halo, outer, 0)
    low, high = edges()
    for step in range(3):
        src = (s_ref, a_ref, b_ref)[step]
        dst = (a_ref, b_ref, None)[step]
        reach = 2 - step

        def read(z, y, src=src):
            return src[row_of(z, y, halo), :]

        def write(z, y, value, dst=dst, step=step):
            value = value + s_ref[row_of(z, y, halo), :]
            if step < 2:
                dst[row_of(z, y, halo), :] = value
                return
            own = z - halo
            value = value + base_ref[pl.ds(pl.multiple_of((own * NY + y) * 8, 8), 8), :]
            out_ref[own, y // 8, pl.ds(y % 8, 8, stride=8), :] = value
            here = pl.ds(pl.multiple_of((own * 4 + y // 16) * 8, 8), 8)
            if y % 16 == 0:
                sums_ref[here, :] = value
            else:
                sums_ref[here, :] = sums_ref[here, :] + value

        diffuse(
            coef_ref, read, write, (halo - reach, halo + NZ + reach), (-reach, NY + reach), low, high
        )
    exact = lax.Precision.HIGHEST
    lines = lax.dot_general(
        jnp.ones((8, 128), F32), sums_ref[...], (((1,), (1,)), ((), ())),
        precision=exact, preferred_element_type=F32,
    )
    pairs = jnp.where((iota((256, 128), 0) >> 1) == iota((256, 128), 1), 1.0 / 4096.0, 0.0)
    means = jnp.dot(lines, pairs, precision=exact, preferred_element_type=F32)
    coarse_ref[...] = jnp.broadcast_to(means[0:1, :], (DEV, 128))


def vmem(count):
    return [pl.BlockSpec(memory_space=pltpu.VMEM)] * count


def smem(count):
    return [pl.BlockSpec(memory_space=pltpu.SMEM)] * count


def params():
    return pltpu.CompilerParams(vmem_limit_bytes=VMEM)


def cost(flops, moved):
    return pl.CostEstimate(flops=flops, bytes_accessed=moved, transcendentals=0)


def shift(value, axis, by):
    count = lax.axis_size(axis)
    if by > 0:
        pairs = [(i, i + 1) for i in range(count - 1)]
    else:
        pairs = [(i + 1, i) for i in range(count - 1)]
    return lax.ppermute(value, axis, pairs)


def per_device(
    initial_heat_state,
    dynamic_wattage,
    drain_multiplier,
    holder_processor,
    patch_target_slot,
    active_patch_number,
    prior_reduced_heat_map,
    conductivity_lookup,
    substance_of_slab,
):
    state = initial_heat_state
    both = ("logic", "slab")
    shape = jax.ShapeDtypeStruct
    low = shift(state[4:].astype(BF16), "slab", 1)
    high = shift(state[:4].astype(BF16), "slab", -1)
    front = shift(state[:, 56:].astype(BF16), "logic", 1)
    back = shift(state[:, :8].astype(BF16), "logic", -1)
    corner_low = shift(jnp.stack([front[4:], back[4:]]), "slab", 1)
    corner_high = shift(jnp.stack([front[:4], back[:4]]), "slab", -1)

    packed = pl.pallas_call(
        pack_kernel,
        out_shape=shape((DEV, ROWS, 128), BF16),
        in_specs=smem(1) + vmem(5),
        out_specs=pl.BlockSpec(memory_space=pltpu.VMEM),
        scratch_shapes=[
            pltpu.VMEM((DEV, TILES), F32),
            pltpu.VMEM((CAP, TILES), BF16),
            pltpu.VMEM((DEV, 128), F32),
            pltpu.VMEM((DEV, 128), F32),
            pltpu.VMEM((TILES, 256), BF16),
        ],
        compiler_params=params(),
        cost_estimate=cost(5_000_000_000, 4_000_000),
        name="pack",
    )(
        active_patch_number,
        holder_processor.reshape(1, TILES),
        patch_target_slot.reshape(1, TILES),
        drain_multiplier.reshape(1, TILES),
        prior_reduced_heat_map.reshape(LAYERS, 128),
        dynamic_wattage,
    )
    got = lax.all_to_all(packed, both, split_axis=0, concat_axis=0, tiled=True)

    base = pl.pallas_call(
        temperature_kernel,
        out_shape=shape((NZ * NY * 8, 128), F32),
        in_specs=smem(2) + vmem(7),
        out_specs=pl.BlockSpec(memory_space=pltpu.VMEM),
        scratch_shapes=[
            pltpu.VMEM((16, 6, 8, 128), F32),
            pltpu.VMEM((16, 10, 64, 128), F32),
            pltpu.VMEM((16 * 72 * 8, 128), F32),
            pltpu.VMEM((16 * 72 * 8, 128), F32),
        ],
        compiler_params=params(),
        cost_estimate=cost(100_000_000, 20_000_000),
        name="diffuse_temperature",
    )(
        conductivity_lookup, substance_of_slab, state, low, high, front, back, corner_low, corner_high
    )

    source, lower, upper, first, last = pl.pallas_call(
        scatter_kernel,
        out_shape=[
            shape((64, 8, 8, 128), F32),
            shape((12, 8, 16, 128), BF16),
            shape((12, 8, 16, 128), BF16),
            shape((8, 8, 8, 128), BF16),
            shape((8, 8, 8, 128), BF16),
        ],
        in_specs=vmem(1),
        out_specs=vmem(5),
        scratch_shapes=[pltpu.VMEM((32, 128), I32)],
        compiler_params=params(),
        cost_estimate=cost(5_000_000_000, 6_000_000),
        name="place_tiles",
    )(got)
    s_low = shift(upper, "slab", 1)
    s_high = shift(lower, "slab", -1)
    s_front = shift(last, "logic", 1)
    s_back = shift(first, "logic", -1)
    s_corner_low = shift(jnp.stack([s_front[5:], s_back[5:]]), "slab", 1)
    s_corner_high = shift(jnp.stack([s_front[:3], s_back[:3]]), "slab", -1)

    new_state, coarse = pl.pallas_call(
        source_kernel,
        out_shape=[shape((NZ, 8, 64, 128), F32), shape((DEV, 128), F32)],
        in_specs=smem(2) + vmem(8),
        out_specs=vmem(2),
        scratch_shapes=[
            pltpu.VMEM((14, 6, 8, 128), F32),
            pltpu.VMEM((14, 10, 64, 128), F32),
            pltpu.VMEM((14 * 72 * 8, 128), F32),
            pltpu.VMEM((14 * 72 * 8, 128), F32),
            pltpu.VMEM((14 * 72 * 8, 128), F32),
            pltpu.VMEM((256, 128), F32),
        ],
        compiler_params=params(),
        cost_estimate=cost(100_000_000, 20_000_000),
        name="diffuse_source",
    )(
        conductivity_lookup, substance_of_slab, source.reshape(4096, 128), base,
        s_low, s_high, s_front, s_back, s_corner_low, s_corner_high,
    )
    thermal_state = (
        new_state.reshape(NZ, 8, 8, 8, 128).transpose(0, 1, 3, 2, 4).reshape(NZ, NY, 1024)
    )
    gathered = lax.all_to_all(coarse, both, split_axis=0, concat_axis=0, tiled=True)
    reduced_map = gathered.reshape(LOGICS, SLABS, NZ, 4, 4)
    reduced_map = jnp.transpose(reduced_map, (1, 2, 0, 3, 4)).reshape(LAYERS, 32, 4)
    return (thermal_state, reduced_map)


def solution(mesh):
    return jax.shard_map(
        per_device,
        mesh=mesh,
        in_specs=(
            P("slab", "logic", None),
            P(("logic", "slab"), None),
            P(("logic", "slab")),
            P(("logic", "slab"), None),
            P(("logic", "slab")),
            P(("logic", "slab")),
            P(),
            P(),
            P(),
        ),
        out_specs=(P("slab", "logic", None), P()),
        check_vma=False,
    )
```

time: 276 us -> 154 us (0.56)
  other arithmetic: 60.4 us -> 1.49 us
  Pallas kernels: 0 us -> 36.7 us
  blocking collectives: 57.5 us -> 21.4 us
  starting transfers between devices: 70.3 us -> 41.3 us
  local copies, waits for them, and re-layouts: 38.9 us -> 14 us
  waiting for transfers between devices: 46.2 us -> 36.6 us
    all_gather x1 -> x0, blocking collectives: 57.5 us -> none  [per_device(): lax.all_gather(reduced_patch.reshape(1, -1), ('logic', 'slab'), axis=0, t...]
    pallas_call x0 -> x4, Pallas kernels: none -> 36.7 us  [the longest x1 11.8 us: per_device(): pl.pallas_call(temperature_kernel, out_shape=shape((NZ * NY * 8, 128), F3...]
    scatter-add x1 -> x0, other arithmetic: 22.2 us -> none  [per_device(): jax.ops.segment_sum(received, received_labels, num_segments=own_tiles + 1)]
    all_to_all x0 -> x1, blocking collectives: none -> 21.4 us  [per_device(): lax.all_to_all(coarse, both, split_axis=0, concat_axis=0, tiled=True)]
    select_n x7 -> x0, other arithmetic: 20.8 us -> none  [the longest x4 20.8 us: march_forward(): return jnp.where(interior_part, result, jnp.float32(0.0))]
    gather x4 -> x0, local copies, waits for them, and re-layouts: 20.8 us -> none  [the longest x1 18.9 us: per_device(): prior_reduced_heat_map[slab_position, line_position // 16, column_position]]
    ppermute x16 -> x12, starting transfers between devices: 49.9 us -> 29.4 us  [shift(): return lax.ppermute(value, axis, pairs)]
    all_to_all x2 -> x1, waiting for transfers between devices: 20.6 us -> 6.92 us  [per_device(): got = lax.all_to_all(packed, both, split_axis=0, concat_axis=0, tiled=True)]
  transfers between devices with their start and end apart: 18 -> 13, of which waited for: 10 -> 4; matrix products, arithmetic and copies ran while one was open for 26% -> 3% of each run, Pallas kernels for 0% -> 12%
where the time goes in v1:
time: 154 us; the launch traced here: 153 us
  starting transfers between devices  41.3 us (27%)
  Pallas kernels  36.7 us (24%)
  waiting for transfers between devices  36.6 us (24%)
  blocking collectives  21.4 us (14%)
  local copies, waits for them, and re-layouts  14 us (9%)
  between operations  1.62 us (1%)
    ppermute x12, waiting for transfers between devices, shift(): return lax.ppermute(value, axis, pairs)  29.7 us
    ppermute x12, starting transfers between devices, shift(): return lax.ppermute(value, axis, pairs)  29.4 us
    all_to_all x1, blocking collectives, per_device(): lax.all_to_all(coarse, both, split_axis=0, concat_axis=0, tiled=True)  21.4 us
    all_to_all x1, starting transfers between devices, per_device(): got = lax.all_to_all(packed, both, split_axis=0, concat_axis=0, tiled=True)  11.9 us
    pallas_call x1, Pallas kernels, per_device(): pl.pallas_call(temperature_kernel, out_shape=shape((NZ * NY * 8, 128), F3...  11.8 us
    pallas_call x1, Pallas kernels, per_device(): pl.pallas_call(source_kernel, out_shape=[shape((NZ, 8, 64, 128), F32), sh...  10.5 us
    unnamed x43, local copies, waits for them, and re-layouts  10.3 us
    pallas_call x1, Pallas kernels, per_device(): pl.pallas_call(pack_kernel, out_shape=shape((DEV, ROWS, 128), BF16), in_s...  7.28 us
  transfers between devices with their start and end apart: 13, of which 4 were waited for; matrix products, arithmetic and copies ran while one was open for 3% of the time, Pallas kernels for 12%

profile of v1, /device:TPU:1, one launch (start us, length us, event | category | flops | bytes accessed | tf_op | source)
XLA Modules:
  0.0 153.1 jit_solution(6026587311716921189)
XLA Ops:
  5.5 7.3 %pack.1 = bf16[128,72,128]{2,1,0:T(8,128)(2,1)S(1)} custom-call(s32[1]{0:T(128)S(6)} %copy.30.count_ref, s32[1,2048]{1,0:T(1,128)S(1)} %bitcast.38, s32[1,2048]{1,0:T(1,128)S(1)} %bitcast.39, f32[1,2048]{1,0:T(1,128)S(1)} %bitcast.40, f32[128,128]{1,0:T(8,128)S(1)} %copy.21.prior_ref, bf16[2048,256]{1,0:T(8,128)(2,1)S(1)} %copy-done.11), custom_call_target="tpu_custom_call" | custom-call | flops 5000000000 | bytes 4000000 | tf_op jit(solution)/shard_map/pack/pallas_call | solution.py:395
  12.8 1.4 copy-done.1
  14.2 11.9 %all-to-all-start = ((bf16[128,72,128]{2,1,0:T(8,128)(2,1)}), bf16[128,72,128]{2,1,0:T(8,128)(2,1)}, u32[]{:S(2)}, u32[]{:S(2)}) async-start(bf16[128,72,128]{2,1,0:T(8,128)(2,1)} %copy-done.1), calls=%async_computation | async-start | bytes 4718592 | tf_op jit(solution)/shard_map/all_to_all | solution.py:418
  26.3 3.0 %collective-permute-start.3 = (bf16[8,8,1024]{2,1,0:T(8,128)(2,1)S(1)}, bf16[8,8,1024]{2,1,0:T(8,128)(2,1)S(1)}, u32[]{:S(2)}, u32[]{:S(2)}) collective-permute-start(bf16[8,8,1024]{2,1,0:T(8,128)(2,1)S(1)} %get-tuple-element.20), channel_id=1, source_target_pairs={{16,0},{32,16},{48,32},{64,48},{80,64},{96,80},{112,96},{17,1},{33... | collective-permute-start | bytes 393224 | tf_op jit(solution)/shard_map/ppermute | solution.py:371
  29.4 2.5 %collective-permute-start.2 = (bf16[8,8,1024]{2,1,0:T(8,128)(2,1)S(1)}, bf16[8,8,1024]{2,1,0:T(8,128)(2,1)S(1)}, u32[]{:S(2)}, u32[]{:S(2)}) collective-permute-start(bf16[8,8,1024]{2,1,0:T(8,128)(2,1)S(1)} %get-tuple-element.21), channel_id=1, source_target_pairs={{0,16},{16,32},{32,48},{48,64},{64,80},{80,96},{96,112},{1,17},{17... | collective-permute-start | bytes 393224 | tf_op jit(solution)/shard_map/ppermute | solution.py:371
  33.1 1.3 collective-permute-start.1
  34.3 4.0 %collective-permute-start = (bf16[4,64,1024]{2,1,0:T(8,128)(2,1)}, bf16[4,64,1024]{2,1,0:T(8,128)(2,1)S(1)}, u32[]{:S(2)}, u32[]{:S(2)}) collective-permute-start(bf16[4,64,1024]{2,1,0:T(8,128)(2,1)} %get-tuple-element.23), channel_id=1, source_target_pairs={{0,1},{1,2},{2,3},{3,4},{4,5},{5,6},{6,7},{7,8},{8,9},{9,10},{10,1... | collective-permute-start | bytes 1572872 | tf_op jit(solution)/shard_map/ppermute | solution.py:371
  38.4 12.2 %collective-permute-done.3.back_ref = bf16[8,8,1024]{2,1,0:T(8,128)(2,1)S(1)} collective-permute-done((bf16[8,8,1024]{2,1,0:T(8,128)(2,1)S(1)}, bf16[8,8,1024]{2,1,0:T(8,128)(2,1)S(1)}, u32[]{:S(2)}, u32[]{:S(2)}) %collective-permute-start.3) | collective-permute-done | bytes 131104 | tf_op jit(solution)/shard_map/ppermute | solution.py:371
  51.9 6.9 %all-to-all-done.got_ref = bf16[128,72,128]{2,1,0:T(8,128)(2,1)} async-done(((bf16[128,72,128]{2,1,0:T(8,128)(2,1)}), bf16[128,72,128]{2,1,0:T(8,128)(2,1)}, u32[]{:S(2)}, u32[]{:S(2)}) %all-to-all-start) | async-done | bytes 2359328 | tf_op jit(solution)/shard_map/all_to_all | solution.py:418
  58.8 7.2 %place_tiles.1 = (f32[64,8,8,128]{3,2,1,0:T(8,128)S(1)}, bf16[12,8,16,128]{3,2,1,0:T(8,128)(2,1)}, bf16[12,8,16,128]{3,2,1,0:T(8,128)(2,1)}, bf16[8,8,8,128]{3,2...) custom-call(bf16[128,72,128]{2,1,0:T(8,128)(2,1)} %all-to-all-done.got_ref), custom_call_target="tpu_custom_call" | custom-call | flops 5000000000 | bytes 6000000 | tf_op jit(solution)/shard_map/place_tiles/pallas_call | solution.py:438
  66.1 1.3 copy-done.2
  67.4 2.7 %collective-permute-start.8 = (bf16[8,8,8,128]{3,2,1,0:T(8,128)(2,1)S(1)}, bf16[8,8,8,128]{3,2,1,0:T(8,128)(2,1)S(1)}, u32[]{:S(2)}, u32[]{:S(2)}) collective-permute-start(bf16[8,8,8,128]{3,2,1,0:T(8,128)(2,1)S(1)} %get-tuple-element.12), channel_id=1, source_target_pairs={{0,16},{16,32},{32,48},{48,64},{64,80},{80,96},{96,112},{1,17},{17... | collective-permute-start | bytes 393224 | tf_op jit(solution)/shard_map/ppermute | solution.py:371
  70.2 2.6 %collective-permute-start.4 = (bf16[2,4,8,1024]{3,2,1,0:T(8,128)(2,1)S(1)}, bf16[2,4,8,1024]{3,2,1,0:T(8,128)(2,1)S(1)}, u32[]{:S(2)}, u32[]{:S(2)}) collective-permute-start(bf16[2,4,8,1024]{3,2,1,0:T(8,128)(2,1)S(1)} %pad_maximum_fusion), channel_id=1, source_target_pairs={{0,1},{1,2},{2,3},{3,4},{4,5},{5,6},{6,7},{7,8},{8,9},{9,10},{10,1... | collective-permute-start | bytes 393224 | tf_op jit(solution)/shard_map/ppermute | solution.py:371
  72.8 1.9 %collective-permute-start.9 = (bf16[8,8,8,128]{3,2,1,0:T(8,128)(2,1)S(1)}, bf16[8,8,8,128]{3,2,1,0:T(8,128)(2,1)S(1)}, u32[]{:S(2)}, u32[]{:S(2)}) collective-permute-start(bf16[8,8,8,128]{3,2,1,0:T(8,128)(2,1)S(1)} %get-tuple-element.13), channel_id=1, source_target_pairs={{16,0},{32,16},{48,32},{64,48},{80,64},{96,80},{112,96},{17,1},{33... | collective-permute-start | bytes 393224 | tf_op jit(solution)/shard_map/ppermute | solution.py:371
  74.8 3.1 %collective-permute-start.6 = (bf16[12,8,16,128]{3,2,1,0:T(8,128)(2,1)}, bf16[12,8,16,128]{3,2,1,0:T(8,128)(2,1)}, u32[]{:S(2)}, u32[]{:S(2)}) collective-permute-start(bf16[12,8,16,128]{3,2,1,0:T(8,128)(2,1)} %get-tuple-element.10), channel_id=1, source_target_pairs={{0,1},{1,2},{2,3},{3,4},{4,5},{5,6},{6,7},{7,8},{8,9},{9,10},{10,1... | collective-permute-start | bytes 1179656 | tf_op jit(solution)/shard_map/ppermute | solution.py:371
  77.9 1.2 collective-permute-done.9.back_ref
  79.1 1.3 collective-permute-start.7
  80.4 1.3 collective-permute-start.5
  83.1 16.2 %collective-permute-done.5.corner_high_ref = bf16[2,4,8,1024]{3,2,1,0:T(8,128)(2,1)S(1)} collective-permute-done((bf16[2,4,8,1024]{3,2,1,0:T(8,128)(2,1)S(1)}, bf16[2,4,8,1024]{3,2,1,0:T(8,128)(2,1)S(1)}, u32[]{:S(2)}, u32[]{:S(2)}) %collective-permute-start.5) | collective-permute-done | bytes 131104 | tf_op jit(solution)/shard_map/ppermute | solution.py:371
  99.9 4.3 %collective-permute-start.10 = (bf16[2,3,8,8,128]{4,3,2,1,0:T(8,128)(2,1)}, bf16[2,3,8,8,128]{4,3,2,1,0:T(8,128)(2,1)}, u32[]{:S(2)}, u32[]{:S(2)}) collective-permute-start(bf16[2,3,8,8,128]{4,3,2,1,0:T(8,128)(2,1)} %pad_maximum_fusion.2), channel_id=1, source_target_pairs={{0,1},{1,2},{2,3},{3,4},{4,5},{5,6},{6,7},{7,8},{8,9},{9,10},{10,1... | collective-permute-start | bytes 294920 | tf_op jit(solution)/shard_map/ppermute | solution.py:371
  104.2 1.3 collective-permute-start.11
  107.5 11.8 %diffuse_temperature.1.base_ref = f32[4096,128]{1,0:T(8,128)S(1)} custom-call(f32[8,3]{1,0:T(8,128)S(1)} %copy.23.table_ref, s32[128]{0:T(128)S(1)} %copy-done.10, f32[8,64,1024]{2,1,0:T(8,128)S(1)} %copy-done, bf16[4,64,1024]{2,1,0:T(8,128)(2,1)S(1)} %collective-permute-done.low_ref, bf16[4,64,1024]{2,1,0:T(8,128)(2,1)S(1)} %collective-permute-done.1.high_ref, ...), custom_call_target="tpu_custom_call" | custom-call | flops 100000000 | bytes 20000000 | tf_op jit(solution)/shard_map/diffuse_temperature/pallas_call | solution.py:420
  119.4 10.5 %diffuse_source.1 = (f32[8,8,64,128]{3,2,1,0:T(8,128)}, f32[128,128]{1,0:T(8,128)S(1)}) custom-call(f32[8,3]{1,0:T(8,128)S(1)} %copy.23.table_ref, s32[128]{0:T(128)S(1)} %copy-done.10, f32[4096,128]{1,0:T(8,128)S(1)} %bitcast.36, f32[4096,128]{1,0:T(8,128)S(1)} %diffuse_temperature.1.base_ref, bf16[12,8,16,128]{3,2,1,0:T(8,128)(2,1)} %collective-permute-done.6.low_ref, ...), custom_call_target="tpu_custom_call" | custom-call | flops 100000000 | bytes 20000000 | tf_op jit(solution)/shard_map/diffuse_source/pallas_call | solution.py:461
  129.8 21.4 %all_to_all.14 = f32[128,1,128]{2,1,0:T(1,128)S(1)} all-to-all(f32[128,1,128]{2,1,0:T(1,128)S(1)} %bitcast.37), channel_id=1, replica_groups=mesh['logic'=8,'slab'=16] {'logic','slab'}, dimensions={0} | all-to-all | bytes 131072 | tf_op jit(solution)/shard_map/all_to_all | solution.py:484
  (64 shorter events, 12.8 us)
Async XLA Ops:
  14.2 11.9 %copy-start = (f32[8,64,1024]{2,1,0:T(8,128)S(1)}, f32[8,64,1024]{2,1,0:T(8,128)}, u32[]{:S(2)}) copy-start(f32[8,64,1024]{2,1,0:T(8,128)} %state_ref.1) | copy-start | bytes 6291460
  14.2 44.6 %all-to-all-start = ((bf16[128,72,128]{2,1,0:T(8,128)(2,1)}), bf16[128,72,128]{2,1,0:T(8,128)(2,1)}, u32[]{:S(2)}, u32[]{:S(2)}) async-start(bf16[128,72,128]{2,1,0:T(8,128)(2,1)} %copy-done.1), calls=%async_computation | async-start | bytes 4718592 | tf_op jit(solution)/shard_map/all_to_all | solution.py:418
  26.3 24.3 %collective-permute-start.3 = (bf16[8,8,1024]{2,1,0:T(8,128)(2,1)S(1)}, bf16[8,8,1024]{2,1,0:T(8,128)(2,1)S(1)}, u32[]{:S(2)}, u32[]{:S(2)}) collective-permute-start(bf16[8,8,1024]{2,1,0:T(8,128)(2,1)S(1)} %get-tuple-element.20), channel_id=1, source_target_pairs={{16,0},{32,16},{48,32},{64,48},{80,64},{96,80},{112,96},{17,1},{33... | collective-permute-start | bytes 393224 | tf_op jit(solution)/shard_map/ppermute | solution.py:371
  29.4 21.9 %collective-permute-start.2 = (bf16[8,8,1024]{2,1,0:T(8,128)(2,1)S(1)}, bf16[8,8,1024]{2,1,0:T(8,128)(2,1)S(1)}, u32[]{:S(2)}, u32[]{:S(2)}) collective-permute-start(bf16[8,8,1024]{2,1,0:T(8,128)(2,1)S(1)} %get-tuple-element.21), channel_id=1, source_target_pairs={{0,16},{16,32},{32,48},{48,64},{64,80},{80,96},{96,112},{1,17},{17... | collective-permute-start | bytes 393224 | tf_op jit(solution)/shard_map/ppermute | solution.py:371
  33.1 71.1 %collective-permute-start.1 = (bf16[4,64,1024]{2,1,0:T(8,128)(2,1)}, bf16[4,64,1024]{2,1,0:T(8,128)(2,1)S(1)}, u32[]{:S(2)}, u32[]{:S(2)}) collective-permute-start(bf16[4,64,1024]{2,1,0:T(8,128)(2,1)} %get-tuple-element.22), channel_id=1, source_target_pairs={{1,0},{2,1},{3,2},{4,3},{5,4},{6,5},{7,6},{8,7},{9,8},{10,9},{11,1... | collective-permute-start | bytes 1572872 | tf_op jit(solution)/shard_map/ppermute | solution.py:371
  34.3 71.2 %collective-permute-start = (bf16[4,64,1024]{2,1,0:T(8,128)(2,1)}, bf16[4,64,1024]{2,1,0:T(8,128)(2,1)S(1)}, u32[]{:S(2)}, u32[]{:S(2)}) collective-permute-start(bf16[4,64,1024]{2,1,0:T(8,128)(2,1)} %get-tuple-element.23), channel_id=1, source_target_pairs={{0,1},{1,2},{2,3},{3,4},{4,5},{5,6},{6,7},{7,8},{8,9},{9,10},{10,1... | collective-permute-start | bytes 1572872 | tf_op jit(solution)/shard_map/ppermute | solution.py:371
  51.9 53.6 %copy-start.19 = (f32[8,3]{0,1:T(4,128)S(1)}, f32[8,3]{0,1:T(4,128)}, u32[]{:S(2)}) copy-start(f32[8,3]{0,1:T(4,128)} %param.16) | copy-start | bytes 292
  51.9 53.7 %copy-start.10 = (s32[128]{0:T(128)S(1)}, s32[128]{0:T(128)}, u32[]{:S(2)}) copy-start(s32[128]{0:T(128)} %label_ref.3) | copy-start | bytes 1540
  58.8 11.3 %copy-start.17 = (bf16[1,4,8,1024]{3,2,1,0:T(8,128)(2,1)S(1)}, bf16[1,4,8,1024]{3,2,1,0:T(8,128)(2,1)}, u32[]{:S(2)}) copy-start(bf16[1,4,8,1024]{3,2,1,0:T(8,128)(2,1)} %get-tuple-element.31) | copy-start | bytes 196612
  58.8 11.3 %copy-start.18 = (bf16[1,4,8,1024]{3,2,1,0:T(8,128)(2,1)S(1)}, bf16[1,4,8,1024]{3,2,1,0:T(8,128)(2,1)}, u32[]{:S(2)}) copy-start(bf16[1,4,8,1024]{3,2,1,0:T(8,128)(2,1)} %get-tuple-element.29) | copy-start | bytes 196612
  58.8 13.9 %copy-start.15 = (bf16[1,4,8,1024]{3,2,1,0:T(8,128)(2,1)S(1)}, bf16[1,4,8,1024]{3,2,1,0:T(8,128)(2,1)}, u32[]{:S(2)}) copy-start(bf16[1,4,8,1024]{3,2,1,0:T(8,128)(2,1)} %get-tuple-element.30) | copy-start | bytes 196612
  58.8 14.0 %copy-start.16 = (bf16[1,4,8,1024]{3,2,1,0:T(8,128)(2,1)S(1)}, bf16[1,4,8,1024]{3,2,1,0:T(8,128)(2,1)}, u32[]{:S(2)}) copy-start(bf16[1,4,8,1024]{3,2,1,0:T(8,128)(2,1)} %get-tuple-element.28) | copy-start | bytes 196612
  67.4 7.4 %collective-permute-start.8 = (bf16[8,8,8,128]{3,2,1,0:T(8,128)(2,1)S(1)}, bf16[8,8,8,128]{3,2,1,0:T(8,128)(2,1)S(1)}, u32[]{:S(2)}, u32[]{:S(2)}) collective-permute-start(bf16[8,8,8,128]{3,2,1,0:T(8,128)(2,1)S(1)} %get-tuple-element.12), channel_id=1, source_target_pairs={{0,16},{16,32},{32,48},{48,64},{64,80},{80,96},{96,112},{1,17},{17... | collective-permute-start | bytes 393224 | tf_op jit(solution)/shard_map/ppermute | solution.py:371
  70.2 10.3 %collective-permute-start.4 = (bf16[2,4,8,1024]{3,2,1,0:T(8,128)(2,1)S(1)}, bf16[2,4,8,1024]{3,2,1,0:T(8,128)(2,1)S(1)}, u32[]{:S(2)}, u32[]{:S(2)}) collective-permute-start(bf16[2,4,8,1024]{3,2,1,0:T(8,128)(2,1)S(1)} %pad_maximum_fusion), channel_id=1, source_target_pairs={{0,1},{1,2},{2,3},{3,4},{4,5},{5,6},{6,7},{7,8},{8,9},{9,10},{10,1... | collective-permute-start | bytes 393224 | tf_op jit(solution)/shard_map/ppermute | solution.py:371
  72.8 6.3 %collective-permute-start.9 = (bf16[8,8,8,128]{3,2,1,0:T(8,128)(2,1)S(1)}, bf16[8,8,8,128]{3,2,1,0:T(8,128)(2,1)S(1)}, u32[]{:S(2)}, u32[]{:S(2)}) collective-permute-start(bf16[8,8,8,128]{3,2,1,0:T(8,128)(2,1)S(1)} %get-tuple-element.13), channel_id=1, source_target_pairs={{16,0},{32,16},{48,32},{64,48},{80,64},{96,80},{112,96},{17,1},{33... | collective-permute-start | bytes 393224 | tf_op jit(solution)/shard_map/ppermute | solution.py:371
  74.8 44.6 %collective-permute-start.6 = (bf16[12,8,16,128]{3,2,1,0:T(8,128)(2,1)}, bf16[12,8,16,128]{3,2,1,0:T(8,128)(2,1)}, u32[]{:S(2)}, u32[]{:S(2)}) collective-permute-start(bf16[12,8,16,128]{3,2,1,0:T(8,128)(2,1)} %get-tuple-element.10), channel_id=1, source_target_pairs={{0,1},{1,2},{2,3},{3,4},{4,5},{5,6},{6,7},{7,8},{8,9},{9,10},{10,1... | collective-permute-start | bytes 1179656 | tf_op jit(solution)/shard_map/ppermute | solution.py:371
  79.1 25.1 %copy-start.4 = (bf16[8,8,8,128]{3,2,1,0:T(8,128)(2,1)}, bf16[8,8,8,128]{3,2,1,0:T(8,128)(2,1)S(1)}, u32[]{:S(2)}) copy-start(bf16[8,8,8,128]{3,2,1,0:T(8,128)(2,1)S(1)} %collective-permute-done.9.back_ref) | copy-start | bytes 393220
  79.1 40.2 %collective-permute-start.7 = (bf16[12,8,16,128]{3,2,1,0:T(8,128)(2,1)}, bf16[12,8,16,128]{3,2,1,0:T(8,128)(2,1)}, u32[]{:S(2)}, u32[]{:S(2)}) collective-permute-start(bf16[12,8,16,128]{3,2,1,0:T(8,128)(2,1)} %get-tuple-element.11), channel_id=1, source_target_pairs={{1,0},{2,1},{3,2},{4,3},{5,4},{6,5},{7,6},{8,7},{9,8},{10,9},{11,1... | collective-permute-start | bytes 1179656 | tf_op jit(solution)/shard_map/ppermute | solution.py:371
  80.4 23.7 %copy-start.6 = (bf16[2,4,8,1024]{3,2,1,0:T(8,128)(2,1)}, bf16[2,4,8,1024]{3,2,1,0:T(8,128)(2,1)S(1)}, u32[]{:S(2)}) copy-start(bf16[2,4,8,1024]{3,2,1,0:T(8,128)(2,1)S(1)} %collective-permute-done.4.corner_low_ref) | copy-start | bytes 393220
  80.4 18.8 %collective-permute-start.5 = (bf16[2,4,8,1024]{3,2,1,0:T(8,128)(2,1)S(1)}, bf16[2,4,8,1024]{3,2,1,0:T(8,128)(2,1)S(1)}, u32[]{:S(2)}, u32[]{:S(2)}) collective-permute-start(bf16[2,4,8,1024]{3,2,1,0:T(8,128)(2,1)S(1)} %pad_maximum_fusion.1), channel_id=1, source_target_pairs={{1,0},{2,1},{3,2},{4,3},{5,4},{6,5},{7,6},{8,7},{9,8},{10,9},{11,1... | collective-permute-start | bytes 393224 | tf_op jit(solution)/shard_map/ppermute | solution.py:371
  99.9 19.4 %collective-permute-start.10 = (bf16[2,3,8,8,128]{4,3,2,1,0:T(8,128)(2,1)}, bf16[2,3,8,8,128]{4,3,2,1,0:T(8,128)(2,1)}, u32[]{:S(2)}, u32[]{:S(2)}) collective-permute-start(bf16[2,3,8,8,128]{4,3,2,1,0:T(8,128)(2,1)} %pad_maximum_fusion.2), channel_id=1, source_target_pairs={{0,1},{1,2},{2,3},{3,4},{4,5},{5,6},{6,7},{7,8},{8,9},{9,10},{10,1... | collective-permute-start | bytes 294920 | tf_op jit(solution)/shard_map/ppermute | solution.py:371
  104.2 15.1 %collective-permute-start.11 = (bf16[2,3,8,8,128]{4,3,2,1,0:T(8,128)(2,1)}, bf16[2,3,8,8,128]{4,3,2,1,0:T(8,128)(2,1)}, u32[]{:S(2)}, u32[]{:S(2)}) collective-permute-start(bf16[2,3,8,8,128]{4,3,2,1,0:T(8,128)(2,1)} %pad_maximum_fusion.3), channel_id=1, source_target_pairs={{1,0},{2,1},{3,2},{4,3},{5,4},{6,5},{7,6},{8,7},{9,8},{10,9},{11,1... | collective-permute-start | bytes 294920 | tf_op jit(solution)/shard_map/ppermute | solution.py:371
  105.6 13.8 %copy-start.3 = (f32[64,8,8,128]{3,2,1,0:T(8,128)S(1)}, f32[64,8,8,128]{3,2,1,0:T(8,128)}, u32[]{:S(2)}) copy-start(f32[64,8,8,128]{3,2,1,0:T(8,128)} %copy-done.2) | copy-start | bytes 6291460
  105.6 13.8 %copy-start.5 = (bf16[8,8,8,128]{3,2,1,0:T(8,128)(2,1)S(1)}, bf16[8,8,8,128]{3,2,1,0:T(8,128)(2,1)}, u32[]{:S(2)}) copy-start(bf16[8,8,8,128]{3,2,1,0:T(8,128)(2,1)} %copy-done.4) | copy-start | bytes 393220
  (9 other events, 8.7 us)

commit v2 on v1

--- a/solution.py
+++ b/solution.py
@@ -20,7 +20,7 @@
 LOGICS = 8
 ROWS = 72
 GROUP = 16
-VMEM = 48 * 1024 * 1024
+VMEM = 28 * 1024 * 1024
 F32 = jnp.float32
 BF16 = jnp.bfloat16
 I32 = jnp.int32
@@ -30,10 +30,44 @@
     return lax.broadcasted_iota(I32, shape, dim)
 
 
+def edge_kernel(lower_ref, upper_ref, to_high_ref, to_low_ref, first_ref, last_ref):
+    to_low_ref[...] = lower_ref[...].astype(BF16)
+    to_high_ref[...] = upper_ref[...].astype(BF16)
+    for half, ref in ((0, lower_ref), (1, upper_ref)):
+        for xb in range(8):
+            cols = slice(128 * xb, 128 * xb + 128)
+            first_ref[half, 0, xb] = ref[0, :8, cols].astype(BF16)
+            last_ref[half, 0, xb] = ref[0, NY - 8 :, cols].astype(BF16)
+
+
+def corner_kernel(front_ref, back_ref, low_ref, high_ref):
+    for side, ref in ((0, front_ref), (1, back_ref)):
+        for kind in range(2):
+            low_ref[side, kind] = ref[kind, NZ - 3 :]
+            high_ref[side, kind] = ref[kind, :3]
+
+
 def pack_kernel(
-    count_ref, owner_ref, target_ref, drain_ref, prior_ref, watt_ref, out_ref,
-    member_ref, pick_ref, high_ref, low_ref, power_ref,
+    count_ref, owner_hbm, target_hbm, drain_hbm, prior_hbm, watt_hbm, out_hbm,
+    owner_ref, target_ref, drain_ref, prior_ref, watt_ref, out_ref,
+    member_ref, pick_ref, high_ref, low_ref, power_ref, in_sems, out_sems,
 ):
+    loads = [
+        pltpu.make_async_copy(src, dst, in_sems.at[i])
+        for i, (src, dst) in enumerate(
+            (
+                (owner_hbm, owner_ref),
+                (target_hbm, target_ref),
+                (prior_hbm, prior_ref),
+                (drain_hbm, drain_ref),
+                (watt_hbm, watt_ref),
+            )
+        )
+    ]
+    for load in loads:
+        load.start()
+    for load in loads[:4]:
+        load.wait()
     owner = owner_ref[...]
     target = target_ref[...]
     live = iota((1, TILES), 1) < count_ref[0]
@@ -46,19 +80,13 @@
     second = rest.astype(BF16)
     third = (rest - second.astype(F32)).astype(BF16)
     lookup = lambda part: lax.dot_general(
-        part, at_layer, (((0,), (0,)), ((), ())), preferred_element_type=F32
+        part, at_layer, (((1,), (0,)), ((), ())), preferred_element_type=F32
     )
     picked = lookup(first) + lookup(second) + lookup(third)
     heat = jnp.sum(
         jnp.where(iota((LAYERS, TILES), 0) == column, picked, 0.0), axis=0, keepdims=True
     )
     scale = 1.0 + drain_ref[...] * jnp.exp(LEAK_BETA * heat)
-    for b in range(TILES // 128):
-        rows = pl.ds(128 * b, 128)
-        spread = jnp.transpose(jnp.broadcast_to(scale[:, 128 * b : 128 * b + 128], (128, 128)))
-        for h in range(2):
-            cols = pl.ds(128 * h, 128)
-            power_ref[rows, cols] = (watt_ref[rows, cols].astype(F32) * spread).astype(BF16)
     member = jnp.where(iota((DEV, TILES), 0) == jnp.where(live, owner, -1), 1.0, 0.0)
     member_ref[...] = member
     before = jnp.where(iota((256, 256), 0) < iota((256, 256), 1), 1.0, 0.0).astype(BF16)
@@ -82,6 +110,17 @@
     high_ref[...] = spot((target >> 6) + 1)
     low_ref[...] = spot(target & 63)
     row8 = iota((8, 128), 0)
+    loads[4].wait()
+    for b in range(TILES // 128):
+        rows = pl.ds(128 * b, 128)
+        spread = jnp.transpose(jnp.broadcast_to(scale[:, 128 * b : 128 * b + 128], (128, 128)))
+        for h in range(2):
+            cols = pl.ds(128 * h, 128)
+            power_ref[rows, cols] = (watt_ref[rows, cols].astype(F32) * spread).astype(BF16)
+
+    def store(g):
+        here = pl.ds(g * GROUP, GROUP)
+        return pltpu.make_async_copy(out_ref.at[here], out_hbm.at[here], out_sems.at[g])
 
     def group(g, _):
         pick = pick_ref[...]
@@ -101,12 +140,17 @@
         here = pl.ds(g * GROUP, GROUP)
         out_ref[here, 0:32, :] = packed[:, :128].reshape(GROUP, CAP, 128)
         out_ref[here, 32:64, :] = packed[:, 128:].reshape(GROUP, CAP, 128)
+        store(g).start()
         return 0
 
     lax.fori_loop(0, DEV // GROUP, group, 0)
-
-
-def scatter_kernel(got_ref, source_ref, low_ref, high_ref, front_ref, back_ref, label_ref):
+    for g in range(DEV // GROUP):
+        store(g).wait()
+
+
+def scatter_kernel(
+    got_ref, first_ref, last_ref, source_ref, low_ref, high_ref, front_ref, back_ref, label_ref,
+):
     labels = got_ref[:, 64:72, :].reshape(DEV * 8, 128)
     row = iota((DEV * 8, 128), 0)
     lane = iota((DEV * 8, 128), 1)
@@ -139,8 +183,10 @@
             low_ref[:, xb] = short[:12]
             high_ref[:, xb] = short[20:]
             for z in range(NZ):
-                front_ref[z, xb] = cells[8 * z].astype(BF16)
-                back_ref[z, xb] = cells[8 * z + 7].astype(BF16)
+                front_ref[0, z, xb] = cells[8 * z].astype(BF16)
+                back_ref[0, z, xb] = cells[8 * z + 7].astype(BF16)
+    front_ref[1] = first_ref[...]
+    back_ref[1] = last_ref[...]
 
 
 def fill_coefficients(coef_ref, table_ref, label_ref, halo):
@@ -215,8 +261,7 @@
 
 
 def temperature_kernel(
-    table_ref, label_ref, state_ref, low_ref, high_ref, front_ref, back_ref,
-    corner_low_ref, corner_high_ref, out_ref, coef_ref, cells_ref, a_ref, b_ref,
+    table_ref, label_ref, state_ref, low_ref, high_ref, out_ref, coef_ref, cells_ref, a_ref, b_ref,
 ):
     halo = 4
     fill_coefficients(coef_ref, table_ref, label_ref, halo)
@@ -225,30 +270,33 @@
         for xb in range(8):
             cells_ref[z, block, pl.ds(xb * 8, 8), :] = value[:, 128 * xb : 128 * xb + 128]
 
-    def gather(z, rows):
-        for y in rows:
-            block, at = (y + 8) // 8, (y + 8) % 8
-            a_ref[row_of(z, y, halo), :] = cells_ref[z, block, pl.ds(at, 8, stride=8), :]
+    def gather(z):
+        for y in range(NY):
+            a_ref[row_of(z, y, halo), :] = cells_ref[z, y // 8, pl.ds(y % 8, 8, stride=8), :]
+
+    def clear(z, _):
+        for y in (-3, -2, -1, NY, NY + 1, NY + 2):
+            a_ref[row_of(z, y, halo), :] = jnp.zeros((8, 128), F32)
+            b_ref[row_of(z, y, halo), :] = jnp.zeros((8, 128), F32)
+        return 0
+
+    lax.fori_loop(0, NZ + 2 * halo, clear, 0)
 
     def own(z, _):
         for block in range(8):
-            spread(z + halo, block + 1, state_ref[z, 8 * block : 8 * block + 8, :])
-        spread(z + halo, 0, front_ref[z].astype(F32))
-        spread(z + halo, 9, back_ref[z].astype(F32))
-        gather(z + halo, range(-4, NY + 4))
+            spread(z + halo, block, state_ref[z, 8 * block : 8 * block + 8, :])
+        gather(z + halo)
         return 0
 
     lax.fori_loop(0, NZ, own, 0)
 
     def outer(z, _):
-        for base, body, corner in ((0, low_ref, corner_low_ref), (12, high_ref, corner_high_ref)):
+        for base, body in ((0, low_ref), (12, high_ref)):
             for block in range(4):
                 two = body[z, 16 * block : 16 * block + 16, :].astype(F32)
-                spread(z + base, 2 * block + 1, two[:8])
-                spread(z + base, 2 * block + 2, two[8:])
-            spread(z + base, 0, corner[0, z].astype(F32))
-            spread(z + base, 9, corner[1, z].astype(F32))
-            gather(z + base, range(-4, NY + 4))
+                spread(z + base, 2 * block, two[:8])
+                spread(z + base, 2 * block + 1, two[8:])
+            gather(z + base)
         return 0
 
     lax.fori_loop(0, halo, outer, 0)
@@ -257,6 +305,7 @@
     for step in range(4):
         src, dst = bufs[step % 2], bufs[(step + 1) % 2]
         reach = 3 - step
+        wide = (1, 2, 1, 0)[step]
 
         def read(z, y, src=src):
             return src[row_of(z, y, halo), :]
@@ -268,55 +317,102 @@
                 dst[row_of(z, y, halo), :] = value
 
         diffuse(
-            coef_ref, read, write, (halo - reach, halo + NZ + reach), (-reach, NY + reach), low, high
+            coef_ref, read, write, (halo - reach, halo + NZ + reach), (-wide, NY + wide), low, high
         )
 
 
 def source_kernel(
     table_ref, label_ref, source_ref, base_ref, low_ref, high_ref, front_ref, back_ref,
-    corner_low_ref, corner_high_ref, out_ref, coarse_ref, coef_ref, cells_ref, s_ref, a_ref, b_ref,
-    sums_ref,
+    corner_low_ref, corner_high_ref, out_ref, coarse_ref,
+    coef_ref, cells_ref, s_ref, a_ref, b_ref, rim_ref, edge_ref, sums_ref,
 ):
     halo = 3
     fill_coefficients(coef_ref, table_ref, label_ref, halo)
-
-    def gather(z, rows):
-        for y in rows:
-            block, at = (y + 8) // 8, (y + 8) % 8
-            s_ref[row_of(z, y, halo), :] = cells_ref[z, block, pl.ds(at, 8, stride=8), :]
+    zero = jnp.zeros((8, 128), F32)
+
+    def rim_at(z, y):
+        slot = y + 4 if y < 1 else y - NY + 6
+        return pl.ds(pl.multiple_of(((z + 1) * 10 + slot) * 8, 8), 8)
+
+    def edge_at(z, y):
+        slot = y + 3 if y < 1 else y - NY + 5
+        return pl.ds(pl.multiple_of((z * 8 + slot) * 8, 8), 8)
+
+    def strips(z, front, back):
+        for xb in range(8):
+            for kind in range(2):
+                cells_ref[kind, pl.ds(xb * 8, 8), :] = front(kind, xb).astype(F32)
+                cells_ref[2 + kind, pl.ds(xb * 8, 8), :] = back(kind, xb).astype(F32)
+        for at in range(4):
+            if at:
+                s_ref[row_of(z, at - 4, halo), :] = cells_ref[0, pl.ds(4 + at, 8, stride=8), :]
+            rim_ref[rim_at(z, at - 4), :] = cells_ref[1, pl.ds(4 + at, 8, stride=8), :]
+            if at < 3:
+                s_ref[row_of(z, NY + at, halo), :] = cells_ref[2, pl.ds(at, 8, stride=8), :]
+            rim_ref[rim_at(z, NY + at), :] = cells_ref[3, pl.ds(at, 8, stride=8), :]
+
+    rim_ref[pl.ds(0, 80), :] = jnp.zeros((80, 128), F32)
+    rim_ref[pl.ds(15 * 80, 80), :] = jnp.zeros((80, 128), F32)
 
     def own(z, _):
         for y in range(NY):
             start = (z * 8 + y // 8) * 64 + y % 8
             s_ref[row_of(z + halo, y, halo), :] = source_ref[pl.ds(start, 8, stride=8), :]
-        for xb in range(8):
-            cells_ref[z + halo, 0, pl.ds(xb * 8, 8), :] = front_ref[z, xb].astype(F32)
-            cells_ref[z + halo, 9, pl.ds(xb * 8, 8), :] = back_ref[z, xb].astype(F32)
-        gather(z + halo, (-3, -2, -1, NY, NY + 1, NY + 2))
+        strips(
+            z + halo, lambda kind, xb: front_ref[kind, z, xb], lambda kind, xb: back_ref[kind, z, xb]
+        )
         return 0
 
     lax.fori_loop(0, NZ, own, 0)
 
     def outer(z, _):
         for base, body, corner in ((0, low_ref, corner_low_ref), (11, high_ref, corner_high_ref)):
-            for xb in range(8):
-                for block in range(4):
+            for block in range(4):
+                for xb in range(8):
                     two = body[z * 4 + block, xb].astype(F32)
-                    cells_ref[z + base, 2 * block + 1, pl.ds(xb * 8, 8), :] = two[:8]
-                    cells_ref[z + base, 2 * block + 2, pl.ds(xb * 8, 8), :] = two[8:]
-                cells_ref[z + base, 0, pl.ds(xb * 8, 8), :] = corner[0, z, xb].astype(F32)
-                cells_ref[z + base, 9, pl.ds(xb * 8, 8), :] = corner[1, z, xb].astype(F32)
-            gather(z + base, range(-3, NY + 3))
+                    cells_ref[4, pl.ds(xb * 8, 8), :] = two[:8]
+                    cells_ref[5, pl.ds(xb * 8, 8), :] = two[8:]
+                for y in range(16):
+                    s_ref[row_of(z + base, 16 * block + y, halo), :] = cells_ref[
+                        4 + y // 8, pl.ds(y % 8, 8, stride=8), :
+                    ]
+            strips(
+                z + base,
+                lambda kind, xb: corner[0, kind, z, xb],
+                lambda kind, xb: corner[1, kind, z, xb],
+            )
         return 0
 
     lax.fori_loop(0, halo, outer, 0)
     low, high = edges()
+
+    def read_rim(z, y):
+        return rim_ref[rim_at(z, y), :]
+
+    def write_edge(z, y, value):
+        edge_ref[edge_at(z, y), :] = value + s_ref[row_of(z, y, halo), :]
+
+    def sides(z, _):
+        rim_ref[rim_at(z, 0), :] = zero
+        rim_ref[rim_at(z, NY - 1), :] = zero
+        ky = coef_ref[z, 3]
+        write_edge(z, 0, ky * read_rim(z, -1))
+        write_edge(z, NY - 1, ky * read_rim(z, NY))
+        return 0
+
+    lax.fori_loop(0, NZ + 2 * halo, sides, 0)
+    diffuse(coef_ref, read_rim, write_edge, (0, NZ + 2 * halo), (-3, 0), low, high)
+    diffuse(coef_ref, read_rim, write_edge, (0, NZ + 2 * halo), (NY, NY + 3), low, high)
     for step in range(3):
-        src = (s_ref, a_ref, b_ref)[step]
+        src = (None, a_ref, b_ref)[step]
         dst = (a_ref, b_ref, None)[step]
         reach = 2 - step
 
         def read(z, y, src=src):
+            if src is None:
+                if 1 <= y < NY - 1:
+                    return s_ref[row_of(z, y, halo), :]
+                return edge_ref[edge_at(z, y), :]
             return src[row_of(z, y, halo), :]
 
         def write(z, y, value, dst=dst, step=step):
@@ -385,24 +481,51 @@
     state = initial_heat_state
     both = ("logic", "slab")
     shape = jax.ShapeDtypeStruct
-    low = shift(state[4:].astype(BF16), "slab", 1)
-    high = shift(state[:4].astype(BF16), "slab", -1)
-    front = shift(state[:, 56:].astype(BF16), "logic", 1)
-    back = shift(state[:, :8].astype(BF16), "logic", -1)
-    corner_low = shift(jnp.stack([front[4:], back[4:]]), "slab", 1)
-    corner_high = shift(jnp.stack([front[:4], back[:4]]), "slab", -1)
+    to_high, to_low, t_first, t_last = pl.pallas_call(
+        edge_kernel,
+        grid=(NZ // 2,),
+        out_shape=[
+            shape((4, NY, 1024), BF16),
+            shape((4, NY, 1024), BF16),
+            shape((2, 4, 8, 8, 128), BF16),
+            shape((2, 4, 8, 8, 128), BF16),
+        ],
+        in_specs=[
+            pl.BlockSpec((1, NY, 1024), lambda i: (i, 0, 0)),
+            pl.BlockSpec((1, NY, 1024), lambda i: (i + NZ // 2, 0, 0)),
+        ],
+        out_specs=[
+            pl.BlockSpec((1, NY, 1024), lambda i: (i, 0, 0)),
+            pl.BlockSpec((1, NY, 1024), lambda i: (i, 0, 0)),
+            pl.BlockSpec((2, 1, 8, 8, 128), lambda i: (0, i, 0, 0, 0)),
+            pl.BlockSpec((2, 1, 8, 8, 128), lambda i: (0, i, 0, 0, 0)),
+        ],
+        compiler_params=params(),
+        cost_estimate=cost(1_000_000, 5_000_000),
+        name="edges",
+    )(state, state)
+    low = shift(to_high, "slab", 1)
+    high = shift(to_low, "slab", -1)
 
     packed = pl.pallas_call(
         pack_kernel,
         out_shape=shape((DEV, ROWS, 128), BF16),
-        in_specs=smem(1) + vmem(5),
-        out_specs=pl.BlockSpec(memory_space=pltpu.VMEM),
+        in_specs=smem(1) + [pl.BlockSpec(memory_space=pltpu.HBM)] * 5,
+        out_specs=pl.BlockSpec(memory_space=pltpu.HBM),
         scratch_shapes=[
+            pltpu.VMEM((1, TILES), I32),
+            pltpu.VMEM((1, TILES), I32),
+            pltpu.VMEM((1, TILES), F32),
+            pltpu.VMEM((LAYERS, 128), F32),
+            pltpu.VMEM((TILES, 256), BF16),
+            pltpu.VMEM((DEV, ROWS, 128), BF16),
             pltpu.VMEM((DEV, TILES), F32),
             pltpu.VMEM((CAP, TILES), BF16),
             pltpu.VMEM((DEV, 128), F32),
             pltpu.VMEM((DEV, 128), F32),
             pltpu.VMEM((TILES, 256), BF16),
+            pltpu.SemaphoreType.DMA((5,)),
+            pltpu.SemaphoreType.DMA((DEV // GROUP,)),
         ],
         compiler_params=params(),
         cost_estimate=cost(5_000_000_000, 4_000_000),
@@ -412,28 +535,28 @@
         holder_processor.reshape(1, TILES),
         patch_target_slot.reshape(1, TILES),
         drain_multiplier.reshape(1, TILES),
-        prior_reduced_heat_map.reshape(LAYERS, 128),
+        prior_reduced_heat_map.transpose(1, 2, 0).reshape(128, LAYERS),
         dynamic_wattage,
     )
+    packed, low, high = lax.optimization_barrier((packed, low, high))
     got = lax.all_to_all(packed, both, split_axis=0, concat_axis=0, tiled=True)
 
     base = pl.pallas_call(
         temperature_kernel,
         out_shape=shape((NZ * NY * 8, 128), F32),
-        in_specs=smem(2) + vmem(7),
+        in_specs=smem(2) + vmem(3),
         out_specs=pl.BlockSpec(memory_space=pltpu.VMEM),
         scratch_shapes=[
             pltpu.VMEM((16, 6, 8, 128), F32),
-            pltpu.VMEM((16, 10, 64, 128), F32),
+            pltpu.VMEM((16, 8, 64, 128), F32),
             pltpu.VMEM((16 * 72 * 8, 128), F32),
             pltpu.VMEM((16 * 72 * 8, 128), F32),
         ],
         compiler_params=params(),
         cost_estimate=cost(100_000_000, 20_000_000),
         name="diffuse_temperature",
-    )(
-        conductivity_lookup, substance_of_slab, state, low, high, front, back, corner_low, corner_high
-    )
+    )(conductivity_lookup, substance_of_slab, state, low, high)
+    got, base = lax.optimization_barrier((got, base))
 
     source, lower, upper, first, last = pl.pallas_call(
         scatter_kernel,
@@ -441,22 +564,31 @@
             shape((64, 8, 8, 128), F32),
             shape((12, 8, 16, 128), BF16),
             shape((12, 8, 16, 128), BF16),
-            shape((8, 8, 8, 128), BF16),
-            shape((8, 8, 8, 128), BF16),
+            shape((2, NZ, 8, 8, 128), BF16),
+            shape((2, NZ, 8, 8, 128), BF16),
         ],
-        in_specs=vmem(1),
+        in_specs=vmem(3),
         out_specs=vmem(5),
         scratch_shapes=[pltpu.VMEM((32, 128), I32)],
         compiler_params=params(),
         cost_estimate=cost(5_000_000_000, 6_000_000),
         name="place_tiles",
-    )(got)
+    )(got, t_first.reshape(NZ, 8, 8, 128), t_last.reshape(NZ, 8, 8, 128))
     s_low = shift(upper, "slab", 1)
     s_high = shift(lower, "slab", -1)
     s_front = shift(last, "logic", 1)
     s_back = shift(first, "logic", -1)
-    s_corner_low = shift(jnp.stack([s_front[5:], s_back[5:]]), "slab", 1)
-    s_corner_high = shift(jnp.stack([s_front[:3], s_back[:3]]), "slab", -1)
+    to_high, to_low = pl.pallas_call(
+        corner_kernel,
+        out_shape=[shape((2, 2, 3, 8, 8, 128), BF16)] * 2,
+        in_specs=vmem(2),
+        out_specs=vmem(2),
+        compiler_params=params(),
+        cost_estimate=cost(1_000_000, 1_000_000),
+        name="corners",
+    )(s_front, s_back)
+    s_corner_low = shift(to_high, "slab", 1)
+    s_corner_high = shift(to_low, "slab", -1)
 
     new_state, coarse = pl.pallas_call(
         source_kernel,
@@ -465,10 +597,12 @@
         out_specs=vmem(2),
         scratch_shapes=[
             pltpu.VMEM((14, 6, 8, 128), F32),
-            pltpu.VMEM((14, 10, 64, 128), F32),
+            pltpu.VMEM((6, 64, 128), F32),
             pltpu.VMEM((14 * 72 * 8, 128), F32),
             pltpu.VMEM((14 * 72 * 8, 128), F32),
             pltpu.VMEM((14 * 72 * 8, 128), F32),
+            pltpu.VMEM((16 * 80, 128), F32),
+            pltpu.VMEM((14 * 64, 128), F32),
             pltpu.VMEM((256, 128), F32),
         ],
         compiler_params=params(),

time: 154 us -> 131 us (0.85)
  starting transfers between devices: 41.3 us -> 32.4 us
  local copies, waits for them, and re-layouts: 14 us -> 6.28 us
  waiting for transfers between devices: 36.6 us -> 32.3 us
  blocking collectives: 21.4 us -> 18.8 us
  Pallas kernels: 36.7 us -> 39.1 us
    ppermute x12 -> x8, waiting for transfers between devices: 29.7 us -> 13 us  [shift(): return lax.ppermute(value, axis, pairs)]
    all_to_all x1, waiting for transfers between devices: 6.92 us -> 19.2 us  [per_device(): got = lax.all_to_all(packed, both, split_axis=0, concat_axis=0, tiled=True)]
    ppermute x12 -> x8, starting transfers between devices: 29.4 us -> 18.7 us  [shift(): return lax.ppermute(value, axis, pairs)]
    unnamed x43 -> x27, local copies, waits for them, and re-layouts: 10.3 us -> 6 us
    all_to_all x1, blocking collectives: 21.4 us -> 18.8 us  [per_device(): lax.all_to_all(coarse, both, split_axis=0, concat_axis=0, tiled=True)]
    pallas_call x1, Pallas kernels: 10.5 us -> 12.4 us  [per_device(): pl.pallas_call(source_kernel, out_shape=[shape((NZ, 8, 64, 128), F32), sh...]
    all_to_all x1, starting transfers between devices: 11.9 us -> 13.8 us  [per_device(): got = lax.all_to_all(packed, both, split_axis=0, concat_axis=0, tiled=True)]
  transfers between devices with their start and end apart: 13 -> 9, of which waited for: 4 -> 6; matrix products, arithmetic and copies ran while one was open for 3% -> 0% of each run, Pallas kernels for 12% -> 15%
where the time goes in v2:
time: 131 us; the launch traced here: 130 us
  Pallas kernels  39.1 us (30%)
  starting transfers between devices  32.4 us (25%)
  waiting for transfers between devices  32.3 us (25%)
  blocking collectives  18.8 us (14%)
  local copies, waits for them, and re-layouts  6.28 us (5%)
  between operations  1.51 us (1%)
    all_to_all x1, waiting for transfers between devices, per_device(): got = lax.all_to_all(packed, both, split_axis=0, concat_axis=0, tiled=True)  19.2 us
    all_to_all x1, blocking collectives, per_device(): lax.all_to_all(coarse, both, split_axis=0, concat_axis=0, tiled=True)  18.8 us
    ppermute x8, starting transfers between devices, shift(): return lax.ppermute(value, axis, pairs)  18.7 us
    all_to_all x1, starting transfers between devices, per_device(): got = lax.all_to_all(packed, both, split_axis=0, concat_axis=0, tiled=True)  13.8 us
    ppermute x8, waiting for transfers between devices, shift(): return lax.ppermute(value, axis, pairs)  13 us
    pallas_call x1, Pallas kernels, per_device(): pl.pallas_call(source_kernel, out_shape=[shape((NZ, 8, 64, 128), F32), sh...  12.4 us
    pallas_call x1, Pallas kernels, per_device(): pl.pallas_call(temperature_kernel, out_shape=shape((NZ * NY * 8, 128), F3...  11.6 us
    pallas_call x1, Pallas kernels, per_device(): pl.pallas_call(pack_kernel, out_shape=shape((DEV, ROWS, 128), BF16), in_s...  8.33 us
  transfers between devices with their start and end apart: 9, of which 6 were waited for; matrix products, arithmetic and copies ran while one was open for 0% of the time, Pallas kernels for 15%

profile of v2, /device:TPU:1, one launch (start us, length us, event | category | flops | bytes accessed | tf_op | source)
XLA Modules:
  0.0 130.4 jit_solution(11439410468214639734)
XLA Ops:
  0.6 1.6 %copy-done = f32[8,64,1024]{2,1,0:T(8,128)S(1)} copy-done((f32[8,64,1024]{2,1,0:T(8,128)S(1)}, f32[8,64,1024]{2,1,0:T(8,128)}, u32[]{:S(2)}) %copy-start) | copy-done | bytes 2097176
  2.5 4.1 %collective-permute-start = (bf16[4,64,1024]{2,1,0:T(8,128)(2,1)S(1)}, bf16[4,64,1024]{2,1,0:T(8,128)(2,1)S(1)}, u32[]{:S(2)}, u32[]{:S(2)}) collective-permute-start(bf16[4,64,1024]{2,1,0:T(8,128)(2,1)S(1)} %get-tuple-element.20), channel_id=1, source_target_pairs={{0,1},{1,2},{2,3},{3,4},{4,5},{5,6},{6,7},{7,8},{8,9},{9,10},{10,1... | collective-permute-start | bytes 1572872 | tf_op jit(solution)/shard_map/ppermute | solution.py:467
  6.6 1.3 collective-permute-start.1
  8.6 8.3 %pack.1 = bf16[128,72,128]{2,1,0:T(8,128)(2,1)S(1)} custom-call(s32[1]{0:T(128)S(6)} %copy.27.count_ref, s32[1,2048]{1,0:T(1,128)S(1)} %bitcast.29, s32[1,2048]{1,0:T(1,128)S(1)} %bitcast.30, f32[1,2048]{1,0:T(1,128)S(1)} %bitcast.31, f32[128,128]{1,0:T(8,128)S(1)} %bitcast.28, bf16[2048,256]{1,0:T(8,128)(2,1)S(1)} %copy-done.6), custom_call_target="tpu_custom_call" | custom-call | flops 5000000000 | bytes 4000000 | tf_op jit(solution)/shard_map/pack/pallas_call | solution.py:510
  17.0 1.4 %copy-done.4 = bf16[128,72,128]{2,1,0:T(8,128)(2,1)} copy-done((bf16[128,72,128]{2,1,0:T(8,128)(2,1)}, bf16[128,72,128]{2,1,0:T(8,128)(2,1)S(1)}, u32[]{:S(2)}) %copy-start.4) | copy-done | bytes 2359320
  18.4 2.6 %collective-permute-done.1.high_ref = bf16[4,64,1024]{2,1,0:T(8,128)(2,1)S(1)} collective-permute-done((bf16[4,64,1024]{2,1,0:T(8,128)(2,1)S(1)}, bf16[4,64,1024]{2,1,0:T(8,128)(2,1)S(1)}, u32[]{:S(2)}, u32[]{:S(2)}) %collective-permute-start.1) | collective-permute-done | bytes 524320 | tf_op jit(solution)/shard_map/ppermute | solution.py:467
  21.0 13.8 %all-to-all-start = ((bf16[128,72,128]{2,1,0:T(8,128)(2,1)}), bf16[128,72,128]{2,1,0:T(8,128)(2,1)}, u32[]{:S(2)}, u32[]{:S(2)}) async-start(bf16[128,72,128]{2,1,0:T(8,128)(2,1)} %copy-done.4), calls=%async_computation | async-start | bytes 4718592 | tf_op jit(solution)/shard_map/all_to_all | solution.py:542
  34.9 11.6 %diffuse_temperature.1.base_ref = f32[4096,128]{1,0:T(8,128)S(1)} custom-call(f32[8,3]{1,0:T(8,128)S(1)} %copy.20.table_ref, s32[128]{0:T(128)S(1)} %copy-done.5, f32[8,64,1024]{2,1,0:T(8,128)S(1)} %copy-done.1, bf16[4,64,1024]{2,1,0:T(8,128)(2,1)S(1)} %collective-permute-done.low_ref, bf16[4,64,1024]{2,1,0:T(8,128)(2,1)S(1)} %collective-permute-done.1.high_ref), custom_call_target="tpu_custom_call" | custom-call | flops 100000000 | bytes 20000000 | tf_op jit(solution)/shard_map/diffuse_temperature/pallas_call | solution.py:544
  46.4 1.3 %copy-done.2 = f32[4096,128]{1,0:T(8,128)} copy-done((f32[4096,128]{1,0:T(8,128)}, f32[4096,128]{1,0:T(8,128)S(1)}, u32[]{:S(2)}) %copy-start.2) | copy-done | bytes 2097176
  47.8 19.2 %all-to-all-done.got_ref = bf16[128,72,128]{2,1,0:T(8,128)(2,1)} async-done(((bf16[128,72,128]{2,1,0:T(8,128)(2,1)}), bf16[128,72,128]{2,1,0:T(8,128)(2,1)}, u32[]{:S(2)}, u32[]{:S(2)}) %all-to-all-start) | async-done | bytes 2359328 | tf_op jit(solution)/shard_map/all_to_all | solution.py:542
  67.0 6.5 %place_tiles.1 = (f32[64,8,8,128]{3,2,1,0:T(8,128)S(1)}, bf16[12,8,16,128]{3,2,1,0:T(8,128)(2,1)S(1)}, bf16[12,8,16,128]{3,2,1,0:T(8,128)(2,1)S(1)}, bf16[2,8,8,...) custom-call(bf16[128,72,128]{2,1,0:T(8,128)(2,1)} %all-to-all-done.got_ref, bf16[8,8,8,128]{3,2,1,0:T(8,128)(2,1)S(1)} %bitcast.26, ...), custom_call_target="tpu_custom_call" | custom-call | flops 5000000000 | bytes 6000000 | tf_op jit(solution)/shard_map/place_tiles/pallas_call | solution.py:561
  73.5 3.2 %collective-permute-start.4 = (bf16[2,8,8,8,128]{4,3,2,1,0:T(8,128)(2,1)S(1)}, bf16[2,8,8,8,128]{4,3,2,1,0:T(8,128)(2,1)S(1)}, u32[]{:S(2)}, u32[]{:S(2)}) collective-permute-start(bf16[2,8,8,8,128]{4,3,2,1,0:T(8,128)(2,1)S(1)} %get-tuple-element.32), channel_id=1, source_target_pairs={{0,16},{16,32},{32,48},{48,64},{64,80},{80,96},{96,112},{1,17},{17... | collective-permute-start | bytes 786440 | tf_op jit(solution)/shard_map/ppermute | solution.py:467
  76.7 1.9 %collective-permute-start.5 = (bf16[2,8,8,8,128]{4,3,2,1,0:T(8,128)(2,1)S(1)}, bf16[2,8,8,8,128]{4,3,2,1,0:T(8,128)(2,1)S(1)}, u32[]{:S(2)}, u32[]{:S(2)}) collective-permute-start(bf16[2,8,8,8,128]{4,3,2,1,0:T(8,128)(2,1)S(1)} %get-tuple-element.33), channel_id=1, source_target_pairs={{16,0},{32,16},{48,32},{64,48},{80,64},{96,80},{112,96},{17,1},{33... | collective-permute-start | bytes 786440 | tf_op jit(solution)/shard_map/ppermute | solution.py:467
  78.7 2.6 %collective-permute-start.2 = (bf16[12,8,16,128]{3,2,1,0:T(8,128)(2,1)S(1)}, bf16[12,8,16,128]{3,2,1,0:T(8,128)(2,1)S(1)}, u32[]{:S(2)}, u32[]{:S(2)}) collective-permute-start(bf16[12,8,16,128]{3,2,1,0:T(8,128)(2,1)S(1)} %get-tuple-element.30), channel_id=1, source_target_pairs={{0,1},{1,2},{2,3},{3,4},{4,5},{5,6},{6,7},{7,8},{8,9},{9,10},{10,1... | collective-permute-start | bytes 1179656 | tf_op jit(solution)/shard_map/ppermute | solution.py:467
  81.3 1.3 collective-permute-start.3
  82.6 1.8 %collective-permute-done.5.back_ref = bf16[2,8,8,8,128]{4,3,2,1,0:T(8,128)(2,1)S(1)} collective-permute-done((bf16[2,8,8,8,128]{4,3,2,1,0:T(8,128)(2,1)S(1)}, bf16[2,8,8,8,128]{4,3,2,1,0:T(8,128)(2,1)S(1)}, u32[]{:S(2)}, u32[]{:S(2)}) %collective-permute-start.5) | collective-permute-done | bytes 262176 | tf_op jit(solution)/shard_map/ppermute | solution.py:467
  84.5 2.9 %collective-permute-start.6 = (bf16[2,2,3,8,8,128]{5,4,3,2,1,0:T(8,128)(2,1)S(1)}, bf16[2,2,3,8,8,128]{5,4,3,2,1,0:T(8,128)(2,1)S(1)}, u32[]{:S(2)}, u32[]{:S(2)}) collective-permute-start(bf16[2,2,3,8,8,128]{5,4,3,2,1,0:T(8,128)(2,1)S(1)} %get-tuple-element.34), channel_id=1, source_target_pairs={{0,1},{1,2},{2,3},{3,4},{4,5},{5,6},{6,7},{7,8},{8,9},{9,10},{10,1... | collective-permute-start | bytes 589832 | tf_op jit(solution)/shard_map/ppermute | solution.py:467
  87.4 1.3 collective-permute-start.7
  88.7 1.5 %collective-permute-done.2.low_ref = bf16[12,8,16,128]{3,2,1,0:T(8,128)(2,1)S(1)} collective-permute-done((bf16[12,8,16,128]{3,2,1,0:T(8,128)(2,1)S(1)}, bf16[12,8,16,128]{3,2,1,0:T(8,128)(2,1)S(1)}, u32[]{:S(2)}, u32[]{:S(2)}) %collective-permute-start.2) | collective-permute-done | bytes 393248 | tf_op jit(solution)/shard_map/ppermute | solution.py:467
  90.2 4.1 %collective-permute-done.3.high_ref = bf16[12,8,16,128]{3,2,1,0:T(8,128)(2,1)S(1)} collective-permute-done((bf16[12,8,16,128]{3,2,1,0:T(8,128)(2,1)S(1)}, bf16[12,8,16,128]{3,2,1,0:T(8,128)(2,1)S(1)}, u32[]{:S(2)}, u32[]{:S(2)}) %collective-permute-start.3) | collective-permute-done | bytes 393248 | tf_op jit(solution)/shard_map/ppermute | solution.py:467
  94.3 3.0 %collective-permute-done.7.corner_high_ref = bf16[2,2,3,8,8,128]{5,4,3,2,1,0:T(8,128)(2,1)S(1)} collective-permute-done((bf16[2,2,3,8,8,128]{5,4,3,2,1,0:T(8,128)(2,1)S(1)}, bf16[2,2,3,8,8,128]{5,4,3,2,1,0:T(8,128)(2,1)S(1)}, u32[]{:S(2)}, u32[]{:S(2)}) %collective-permute-start.7) | collective-permute-done | bytes 196640 | tf_op jit(solution)/shard_map/ppermute | solution.py:467
  97.3 12.4 %diffuse_source.1 = (f32[8,8,64,128]{3,2,1,0:T(8,128)}, f32[128,128]{1,0:T(8,128)S(1)}) custom-call(f32[8,3]{1,0:T(8,128)S(1)} %copy.20.table_ref, s32[128]{0:T(128)S(1)} %copy-done.5, f32[4096,128]{1,0:T(8,128)S(1)} %bitcast.24, f32[4096,128]{1,0:T(8,128)S(1)} %copy-done.3, bf16[12,8,16,128]{3,2,1,0:T(8,128)(2,1)S(1)} %collective-permute-done.2.low_ref, ...), custom_call_target="tpu_custom_call" | custom-call | flops 100000000 | bytes 20000000 | tf_op jit(solution)/shard_map/diffuse_source/pallas_call | solution.py:593
  109.8 18.8 %all_to_all.14 = f32[128,1,128]{2,1,0:T(1,128)S(1)} all-to-all(f32[128,1,128]{2,1,0:T(1,128)S(1)} %bitcast.25), channel_id=1, replica_groups=mesh['logic'=8,'slab'=16] {'logic','slab'}, dimensions={0} | all-to-all | bytes 131072 | tf_op jit(solution)/shard_map/all_to_all | solution.py:618
  129.3 1.1 reshape.51
  (30 shorter events, 1.1 us)
Async XLA Ops:
  0.6 1.6 %copy-start = (f32[8,64,1024]{2,1,0:T(8,128)S(1)}, f32[8,64,1024]{2,1,0:T(8,128)}, u32[]{:S(2)}) copy-start(f32[8,64,1024]{2,1,0:T(8,128)} %state_ref.1) | copy-start | bytes 6291460
  2.2 6.3 %copy-start.6 = (bf16[2048,256]{1,0:T(8,128)(2,1)S(1)}, bf16[2048,256]{1,0:T(8,128)(2,1)}, u32[]{:S(2)}) copy-start(bf16[2048,256]{1,0:T(8,128)(2,1)} %watt_hbm.1) | copy-start | bytes 3145732
  2.2 6.3 %copy-start.7 = (f32[128,32,4]{0,2,1:T(4,128)S(1)}, f32[128,32,4]{0,2,1:T(4,128)}, u32[]{:S(2)}) copy-start(f32[128,32,4]{0,2,1:T(4,128)} %param.15) | copy-start | bytes 196612
  2.2 6.3 %copy-start.8 = (s32[2048,1]{0,1:T(1,128)S(1)}, s32[2048,1]{0,1:T(1,128)}, u32[]{:S(2)}) copy-start(s32[2048,1]{0,1:T(1,128)} %param.12) | copy-start | bytes 24580
  2.2 6.4 %copy-start.9 = (s32[2048]{0:T(1024)S(1)}, s32[2048]{0:T(1024)}, u32[]{:S(2)}) copy-start(s32[2048]{0:T(1024)} %param.13) | copy-start | bytes 24580
  2.2 6.4 %copy-start.10 = (f32[2048]{0:T(1024)S(1)}, f32[2048]{0:T(1024)}, u32[]{:S(2)}) copy-start(f32[2048]{0:T(1024)} %param.11) | copy-start | bytes 24580
  2.5 15.9 %collective-permute-start = (bf16[4,64,1024]{2,1,0:T(8,128)(2,1)S(1)}, bf16[4,64,1024]{2,1,0:T(8,128)(2,1)S(1)}, u32[]{:S(2)}, u32[]{:S(2)}) collective-permute-start(bf16[4,64,1024]{2,1,0:T(8,128)(2,1)S(1)} %get-tuple-element.20), channel_id=1, source_target_pairs={{0,1},{1,2},{2,3},{3,4},{4,5},{5,6},{6,7},{7,8},{8,9},{9,10},{10,1... | collective-permute-start | bytes 1572872 | tf_op jit(solution)/shard_map/ppermute | solution.py:467
  6.6 14.4 %collective-permute-start.1 = (bf16[4,64,1024]{2,1,0:T(8,128)(2,1)S(1)}, bf16[4,64,1024]{2,1,0:T(8,128)(2,1)S(1)}, u32[]{:S(2)}, u32[]{:S(2)}) collective-permute-start(bf16[4,64,1024]{2,1,0:T(8,128)(2,1)S(1)} %get-tuple-element.21), channel_id=1, source_target_pairs={{1,0},{2,1},{3,2},{4,3},{5,4},{6,5},{7,6},{8,7},{9,8},{10,9},{11,1... | collective-permute-start | bytes 1572872 | tf_op jit(solution)/shard_map/ppermute | solution.py:467
  16.9 1.4 %copy-start.4 = (bf16[128,72,128]{2,1,0:T(8,128)(2,1)}, bf16[128,72,128]{2,1,0:T(8,128)(2,1)S(1)}, u32[]{:S(2)}) copy-start(bf16[128,72,128]{2,1,0:T(8,128)(2,1)S(1)} %pack.1) | copy-start | bytes 7077892
  18.4 16.4 %copy-start.11 = (f32[8,3]{0,1:T(4,128)S(1)}, f32[8,3]{0,1:T(4,128)}, u32[]{:S(2)}) copy-start(f32[8,3]{0,1:T(4,128)} %param.16) | copy-start | bytes 292
  18.4 16.5 %copy-start.1 = (f32[8,64,1024]{2,1,0:T(8,128)S(1)}, f32[8,64,1024]{2,1,0:T(8,128)}, u32[]{:S(2)}) copy-start(f32[8,64,1024]{2,1,0:T(8,128)} %state_ref.1) | copy-start | bytes 6291460
  18.4 16.5 %copy-start.5 = (s32[128]{0:T(128)S(1)}, s32[128]{0:T(128)}, u32[]{:S(2)}) copy-start(s32[128]{0:T(128)} %label_ref.3) | copy-start | bytes 1540
  21.0 46.0 %all-to-all-start = ((bf16[128,72,128]{2,1,0:T(8,128)(2,1)}), bf16[128,72,128]{2,1,0:T(8,128)(2,1)}, u32[]{:S(2)}, u32[]{:S(2)}) async-start(bf16[128,72,128]{2,1,0:T(8,128)(2,1)} %copy-done.4), calls=%async_computation | async-start | bytes 4718592 | tf_op jit(solution)/shard_map/all_to_all | solution.py:542
  46.4 1.3 %copy-start.2 = (f32[4096,128]{1,0:T(8,128)}, f32[4096,128]{1,0:T(8,128)S(1)}, u32[]{:S(2)}) copy-start(f32[4096,128]{1,0:T(8,128)S(1)} %diffuse_temperature.1.base_ref) | copy-start | bytes 6291460
  67.0 30.3 %copy-start.3 = (f32[4096,128]{1,0:T(8,128)S(1)}, f32[4096,128]{1,0:T(8,128)}, u32[]{:S(2)}) copy-start(f32[4096,128]{1,0:T(8,128)} %copy-done.2) | copy-start | bytes 6291460
  73.5 9.1 %collective-permute-start.4 = (bf16[2,8,8,8,128]{4,3,2,1,0:T(8,128)(2,1)S(1)}, bf16[2,8,8,8,128]{4,3,2,1,0:T(8,128)(2,1)S(1)}, u32[]{:S(2)}, u32[]{:S(2)}) collective-permute-start(bf16[2,8,8,8,128]{4,3,2,1,0:T(8,128)(2,1)S(1)} %get-tuple-element.32), channel_id=1, source_target_pairs={{0,16},{16,32},{32,48},{48,64},{64,80},{80,96},{96,112},{1,17},{17... | collective-permute-start | bytes 786440 | tf_op jit(solution)/shard_map/ppermute | solution.py:467
  76.7 7.7 %collective-permute-start.5 = (bf16[2,8,8,8,128]{4,3,2,1,0:T(8,128)(2,1)S(1)}, bf16[2,8,8,8,128]{4,3,2,1,0:T(8,128)(2,1)S(1)}, u32[]{:S(2)}, u32[]{:S(2)}) collective-permute-start(bf16[2,8,8,8,128]{4,3,2,1,0:T(8,128)(2,1)S(1)} %get-tuple-element.33), channel_id=1, source_target_pairs={{16,0},{32,16},{48,32},{64,48},{80,64},{96,80},{112,96},{17,1},{33... | collective-permute-start | bytes 786440 | tf_op jit(solution)/shard_map/ppermute | solution.py:467
  78.7 11.5 %collective-permute-start.2 = (bf16[12,8,16,128]{3,2,1,0:T(8,128)(2,1)S(1)}, bf16[12,8,16,128]{3,2,1,0:T(8,128)(2,1)S(1)}, u32[]{:S(2)}, u32[]{:S(2)}) collective-permute-start(bf16[12,8,16,128]{3,2,1,0:T(8,128)(2,1)S(1)} %get-tuple-element.30), channel_id=1, source_target_pairs={{0,1},{1,2},{2,3},{3,4},{4,5},{5,6},{6,7},{7,8},{8,9},{9,10},{10,1... | collective-permute-start | bytes 1179656 | tf_op jit(solution)/shard_map/ppermute | solution.py:467
  81.3 13.0 %collective-permute-start.3 = (bf16[12,8,16,128]{3,2,1,0:T(8,128)(2,1)S(1)}, bf16[12,8,16,128]{3,2,1,0:T(8,128)(2,1)S(1)}, u32[]{:S(2)}, u32[]{:S(2)}) collective-permute-start(bf16[12,8,16,128]{3,2,1,0:T(8,128)(2,1)S(1)} %get-tuple-element.31), channel_id=1, source_target_pairs={{1,0},{2,1},{3,2},{4,3},{5,4},{6,5},{7,6},{8,7},{9,8},{10,9},{11,1... | collective-permute-start | bytes 1179656 | tf_op jit(solution)/shard_map/ppermute | solution.py:467
  84.5 9.9 %collective-permute-start.6 = (bf16[2,2,3,8,8,128]{5,4,3,2,1,0:T(8,128)(2,1)S(1)}, bf16[2,2,3,8,8,128]{5,4,3,2,1,0:T(8,128)(2,1)S(1)}, u32[]{:S(2)}, u32[]{:S(2)}) collective-permute-start(bf16[2,2,3,8,8,128]{5,4,3,2,1,0:T(8,128)(2,1)S(1)} %get-tuple-element.34), channel_id=1, source_target_pairs={{0,1},{1,2},{2,3},{3,4},{4,5},{5,6},{6,7},{7,8},{8,9},{9,10},{10,1... | collective-permute-start | bytes 589832 | tf_op jit(solution)/shard_map/ppermute | solution.py:467
  87.4 9.9 %collective-permute-start.7 = (bf16[2,2,3,8,8,128]{5,4,3,2,1,0:T(8,128)(2,1)S(1)}, bf16[2,2,3,8,8,128]{5,4,3,2,1,0:T(8,128)(2,1)S(1)}, u32[]{:S(2)}, u32[]{:S(2)}) collective-permute-start(bf16[2,2,3,8,8,128]{5,4,3,2,1,0:T(8,128)(2,1)S(1)} %get-tuple-element.35), channel_id=1, source_target_pairs={{1,0},{2,1},{3,2},{4,3},{5,4},{6,5},{7,6},{8,7},{9,8},{10,9},{11,1... | collective-permute-start | bytes 589832 | tf_op jit(solution)/shard_map/ppermute | solution.py:467

commit v3 on v2

--- a/solution.py
+++ b/solution.py
@@ -41,10 +41,12 @@
 
 
 def corner_kernel(front_ref, back_ref, low_ref, high_ref):
-    for side, ref in ((0, front_ref), (1, back_ref)):
-        for kind in range(2):
-            low_ref[side, kind] = ref[kind, NZ - 3 :]
-            high_ref[side, kind] = ref[kind, :3]
+    for out, first in ((low_ref, NZ - 3), (high_ref, 0)):
+        for z in range(3):
+            for xb in range(8):
+                out[z, xb] = jnp.concatenate(
+                    [front_ref[first + z, xb].astype(F32), back_ref[first + z, xb].astype(F32)], axis=0
+                ).astype(BF16)
 
 
 def pack_kernel(
@@ -165,6 +167,7 @@
     right = got_ref[:, 32:64, :].reshape(DEV * CAP, 128)
     both = jnp.concatenate([left, right], axis=1)
     wanted = iota((512, 128), 0) * 4
+    upper = iota((8, 128), 0) < 4
     for c in range(4):
         chosen = jnp.concatenate(
             [
@@ -183,10 +186,12 @@
             low_ref[:, xb] = short[:12]
             high_ref[:, xb] = short[20:]
             for z in range(NZ):
-                front_ref[0, z, xb] = cells[8 * z].astype(BF16)
-                back_ref[0, z, xb] = cells[8 * z + 7].astype(BF16)
-    front_ref[1] = first_ref[...]
-    back_ref[1] = last_ref[...]
+                front_ref[z, xb] = jnp.where(
+                    upper, first_ref[z, xb].astype(F32), pltpu.roll(cells[8 * z], 4, 0)
+                ).astype(BF16)
+                back_ref[z, xb] = jnp.where(
+                    upper, pltpu.roll(cells[8 * z + 7], 4, 0), last_ref[z, xb].astype(F32)
+                ).astype(BF16)
 
 
 def fill_coefficients(coef_ref, table_ref, label_ref, halo):
@@ -249,10 +254,10 @@
     lax.fori_loop(layers[0], layers[1], layer, 0)
 
 
-def edges():
-    at = lax.axis_index("logic")
+def edges(axis, count):
+    at = lax.axis_index(axis)
     low = jnp.full((8, 128), jnp.where(at > 0, 1.0, 0.0), F32)
-    high = jnp.full((8, 128), jnp.where(at < LOGICS - 1, 1.0, 0.0), F32)
+    high = jnp.full((8, 128), jnp.where(at < count - 1, 1.0, 0.0), F32)
     return low, high
 
 
@@ -270,9 +275,10 @@
         for xb in range(8):
             cells_ref[z, block, pl.ds(xb * 8, 8), :] = value[:, 128 * xb : 128 * xb + 128]
 
-    def gather(z):
+    def gather(z, keep=None):
         for y in range(NY):
-            a_ref[row_of(z, y, halo), :] = cells_ref[z, y // 8, pl.ds(y % 8, 8, stride=8), :]
+            value = cells_ref[z, y // 8, pl.ds(y % 8, 8, stride=8), :]
+            a_ref[row_of(z, y, halo), :] = value if keep is None else value * keep
 
     def clear(z, _):
         for y in (-3, -2, -1, NY, NY + 1, NY + 2):
@@ -290,17 +296,19 @@
 
     lax.fori_loop(0, NZ, own, 0)
 
+    below, above = edges("slab", SLABS)
+
     def outer(z, _):
-        for base, body in ((0, low_ref), (12, high_ref)):
+        for base, body, keep in ((0, low_ref, below), (12, high_ref, above)):
             for block in range(4):
                 two = body[z, 16 * block : 16 * block + 16, :].astype(F32)
                 spread(z + base, 2 * block, two[:8])
                 spread(z + base, 2 * block + 1, two[8:])
-            gather(z + base)
+            gather(z + base, keep)
         return 0
 
     lax.fori_loop(0, halo, outer, 0)
-    low, high = edges()
+    low, high = edges("logic", LOGICS)
     bufs = (a_ref, b_ref)
     for step in range(4):
         src, dst = bufs[step % 2], bufs[(step + 1) % 2]
@@ -338,18 +346,24 @@
         slot = y + 3 if y < 1 else y - NY + 5
         return pl.ds(pl.multiple_of((z * 8 + slot) * 8, 8), 8)
 
-    def strips(z, front, back):
+    low, high = edges("logic", LOGICS)
+    below, above = edges("slab", SLABS)
+
+    def strips(z, front, back, keep_front, keep_back):
         for xb in range(8):
-            for kind in range(2):
-                cells_ref[kind, pl.ds(xb * 8, 8), :] = front(kind, xb).astype(F32)
-                cells_ref[2 + kind, pl.ds(xb * 8, 8), :] = back(kind, xb).astype(F32)
-        for at in range(4):
-            if at:
-                s_ref[row_of(z, at - 4, halo), :] = cells_ref[0, pl.ds(4 + at, 8, stride=8), :]
-            rim_ref[rim_at(z, at - 4), :] = cells_ref[1, pl.ds(4 + at, 8, stride=8), :]
-            if at < 3:
-                s_ref[row_of(z, NY + at, halo), :] = cells_ref[2, pl.ds(at, 8, stride=8), :]
-            rim_ref[rim_at(z, NY + at), :] = cells_ref[3, pl.ds(at, 8, stride=8), :]
+            cells_ref[0, pl.ds(xb * 8, 8), :] = front(xb).astype(F32)
+            cells_ref[1, pl.ds(xb * 8, 8), :] = back(xb).astype(F32)
+        for at in range(8):
+            before = cells_ref[0, pl.ds(at, 8, stride=8), :] * keep_front
+            after = cells_ref[1, pl.ds(at, 8, stride=8), :] * keep_back
+            if at < 4:
+                rim_ref[rim_at(z, NY + at), :] = after
+                if at:
+                    s_ref[row_of(z, at - 4, halo), :] = before
+            else:
+                rim_ref[rim_at(z, at - 8), :] = before
+                if at < 7:
+                    s_ref[row_of(z, NY + at - 4, halo), :] = after
 
     rim_ref[pl.ds(0, 80), :] = jnp.zeros((80, 128), F32)
     rim_ref[pl.ds(15 * 80, 80), :] = jnp.zeros((80, 128), F32)
@@ -358,33 +372,35 @@
         for y in range(NY):
             start = (z * 8 + y // 8) * 64 + y % 8
             s_ref[row_of(z + halo, y, halo), :] = source_ref[pl.ds(start, 8, stride=8), :]
-        strips(
-            z + halo, lambda kind, xb: front_ref[kind, z, xb], lambda kind, xb: back_ref[kind, z, xb]
-        )
+        strips(z + halo, lambda xb: front_ref[z, xb], lambda xb: back_ref[z, xb], low, high)
         return 0
 
     lax.fori_loop(0, NZ, own, 0)
 
     def outer(z, _):
-        for base, body, corner in ((0, low_ref, corner_low_ref), (11, high_ref, corner_high_ref)):
+        for base, body, corner, keep in (
+            (0, low_ref, corner_low_ref, below),
+            (11, high_ref, corner_high_ref, above),
+        ):
             for block in range(4):
                 for xb in range(8):
                     two = body[z * 4 + block, xb].astype(F32)
                     cells_ref[4, pl.ds(xb * 8, 8), :] = two[:8]
                     cells_ref[5, pl.ds(xb * 8, 8), :] = two[8:]
                 for y in range(16):
-                    s_ref[row_of(z + base, 16 * block + y, halo), :] = cells_ref[
-                        4 + y // 8, pl.ds(y % 8, 8, stride=8), :
-                    ]
+                    s_ref[row_of(z + base, 16 * block + y, halo), :] = (
+                        cells_ref[4 + y // 8, pl.ds(y % 8, 8, stride=8), :] * keep
+                    )
             strips(
                 z + base,
-                lambda kind, xb: corner[0, kind, z, xb],
-                lambda kind, xb: corner[1, kind, z, xb],
+                lambda xb: corner[z, xb].astype(F32)[:8],
+                lambda xb: corner[z, xb].astype(F32)[8:],
+                keep * low,
+                keep * high,
             )
         return 0
 
     lax.fori_loop(0, halo, outer, 0)
-    low, high = edges()
 
     def read_rim(z, y):
         return rim_ref[rim_at(z, y), :]
@@ -460,11 +476,7 @@
 
 def shift(value, axis, by):
     count = lax.axis_size(axis)
-    if by > 0:
-        pairs = [(i, i + 1) for i in range(count - 1)]
-    else:
-        pairs = [(i + 1, i) for i in range(count - 1)]
-    return lax.ppermute(value, axis, pairs)
+    return lax.ppermute(value, axis, [(i, (i + by) % count) for i in range(count)])
 
 
 def per_device(
@@ -509,7 +521,7 @@
 
     packed = pl.pallas_call(
         pack_kernel,
-        out_shape=shape((DEV, ROWS, 128), BF16),
+        out_shape=pltpu.HBM((DEV, ROWS, 128), BF16),
         in_specs=smem(1) + [pl.BlockSpec(memory_space=pltpu.HBM)] * 5,
         out_specs=pl.BlockSpec(memory_space=pltpu.HBM),
         scratch_shapes=[
@@ -543,7 +555,7 @@
 
     base = pl.pallas_call(
         temperature_kernel,
-        out_shape=shape((NZ * NY * 8, 128), F32),
+        out_shape=pltpu.VMEM((NZ * NY * 8, 128), F32),
         in_specs=smem(2) + vmem(3),
         out_specs=pl.BlockSpec(memory_space=pltpu.VMEM),
         scratch_shapes=[
@@ -564,8 +576,8 @@
             shape((64, 8, 8, 128), F32),
             shape((12, 8, 16, 128), BF16),
             shape((12, 8, 16, 128), BF16),
-            shape((2, NZ, 8, 8, 128), BF16),
-            shape((2, NZ, 8, 8, 128), BF16),
+            shape((NZ, 8, 8, 128), BF16),
+            shape((NZ, 8, 8, 128), BF16),
         ],
         in_specs=vmem(3),
         out_specs=vmem(5),
@@ -580,7 +592,7 @@
     s_back = shift(first, "logic", -1)
     to_high, to_low = pl.pallas_call(
         corner_kernel,
-        out_shape=[shape((2, 2, 3, 8, 8, 128), BF16)] * 2,
+        out_shape=[shape((3, 8, 16, 128), BF16)] * 2,
         in_specs=vmem(2),
         out_specs=vmem(2),
         compiler_params=params(),

time: 131 us -> 121 us (0.924)
  starting transfers between devices: 32.4 us -> 28.7 us
  waiting for transfers between devices: 32.3 us -> 28.6 us
  local copies, waits for them, and re-layouts: 6.28 us -> 4.84 us
    ppermute x8, waiting for transfers between devices: 13 us -> 9.34 us  [shift(): lax.ppermute(value, axis, [(i, (i + by) % count) for i in range(count)])]
    all_to_all x1, starting transfers between devices: 13.8 us -> 11.2 us  [per_device(): got = lax.all_to_all(packed, both, split_axis=0, concat_axis=0, tiled=True)]
    unnamed x27 -> x25, local copies, waits for them, and re-layouts: 6 us -> 4.57 us
  transfers between devices with their start and end apart: 9 -> 9, of which waited for: 6 -> 5; matrix products, arithmetic and copies ran while one was open for 0% -> 0% of each run, Pallas kernels for 15% -> 17%
where the time goes in v3:
time: 121 us
  Pallas kernels  39.2 us (32%)
  starting transfers between devices  28.7 us (24%)
  waiting for transfers between devices  28.6 us (24%)
  blocking collectives  18.1 us (15%)
  local copies, waits for them, and re-layouts  4.84 us (4%)
  between operations  1.48 us (1%)
    all_to_all x1, waiting for transfers between devices, per_device(): got = lax.all_to_all(packed, both, split_axis=0, concat_axis=0, tiled=True)  19.2 us
    all_to_all x1, blocking collectives, per_device(): lax.all_to_all(coarse, both, split_axis=0, concat_axis=0, tiled=True)  18.1 us
    ppermute x8, starting transfers between devices, shift(): lax.ppermute(value, axis, [(i, (i + by) % count) for i in range(count)])  17.5 us
    pallas_call x1, Pallas kernels, per_device(): pl.pallas_call(source_kernel, out_shape=[shape((NZ, 8, 64, 128), F32), sh...  12.4 us
    pallas_call x1, Pallas kernels, per_device(): pl.pallas_call(temperature_kernel, out_shape=pltpu.VMEM((NZ * NY * 8, 128...  11.6 us
    all_to_all x1, starting transfers between devices, per_device(): got = lax.all_to_all(packed, both, split_axis=0, concat_axis=0, tiled=True)  11.2 us
    ppermute x8, waiting for transfers between devices, shift(): lax.ppermute(value, axis, [(i, (i + by) % count) for i in range(count)])  9.34 us
    pallas_call x1, Pallas kernels, per_device(): pl.pallas_call(pack_kernel, out_shape=pltpu.HBM((DEV, ROWS, 128), BF16),...  8.54 us
  transfers between devices with their start and end apart: 9, of which 5 were waited for; matrix products, arithmetic and copies ran while one was open for 0% of the time, Pallas kernels for 17%

profile of v3, /device:TPU:1, one launch (start us, length us, event | category | flops | bytes accessed | tf_op | source)
XLA Modules:
  0.0 120.8 jit_solution(9895266172020989401)
XLA Ops:
  0.6 1.6 %copy-done = f32[8,64,1024]{2,1,0:T(8,128)S(1)} copy-done((f32[8,64,1024]{2,1,0:T(8,128)S(1)}, f32[8,64,1024]{2,1,0:T(8,128)}, u32[]{:S(2)}) %copy-start) | copy-done | bytes 2097176
  2.2 0.2 edges.1
  2.5 2.1 %collective-permute-start = (bf16[4,64,1024]{2,1,0:T(8,128)(2,1)S(1)}, bf16[4,64,1024]{2,1,0:T(8,128)(2,1)S(1)}, u32[]{:S(2)}, u32[]{:S(2)}) collective-permute-start(bf16[4,64,1024]{2,1,0:T(8,128)(2,1)S(1)} %get-tuple-element.20), channel_id=1, source_target_pairs={{0,1},{1,2},{2,3},{3,4},{4,5},{5,6},{6,7},{7,8},{8,9},{9,10},{10,1... | collective-permute-start | bytes 1572872 | tf_op jit(solution)/shard_map/ppermute | solution.py:479
  4.6 3.8 %collective-permute-start.1 = (bf16[4,64,1024]{2,1,0:T(8,128)(2,1)S(1)}, bf16[4,64,1024]{2,1,0:T(8,128)(2,1)S(1)}, u32[]{:S(2)}, u32[]{:S(2)}) collective-permute-start(bf16[4,64,1024]{2,1,0:T(8,128)(2,1)S(1)} %get-tuple-element.21), channel_id=1, source_target_pairs={{0,15},{1,0},{2,1},{3,2},{4,3},{5,4},{6,5},{7,6},{8,7},{9,8},{10,9... | collective-permute-start | bytes 1572872 | tf_op jit(solution)/shard_map/ppermute | solution.py:479
  9.1 8.5 %pack.1 = bf16[128,72,128]{2,1,0:T(8,128)(2,1)} custom-call(s32[1]{0:T(128)S(6)} %copy.27.count_ref, s32[1,2048]{1,0:T(1,128)S(1)} %bitcast.29, s32[1,2048]{1,0:T(1,128)S(1)} %bitcast.30, f32[1,2048]{1,0:T(1,128)S(1)} %bitcast.31, f32[128,128]{1,0:T(8,128)S(1)} %bitcast.28, bf16[2048,256]{1,0:T(8,128)(2,1)S(1)} %copy-done.5), custom_call_target="tpu_custom_call" | custom-call | flops 5000000000 | bytes 4000000 | tf_op jit(solution)/shard_map/pack/pallas_call | solution.py:522
  17.7 2.2 %collective-permute-done.low_ref = bf16[4,64,1024]{2,1,0:T(8,128)(2,1)S(1)} collective-permute-done((bf16[4,64,1024]{2,1,0:T(8,128)(2,1)S(1)}, bf16[4,64,1024]{2,1,0:T(8,128)(2,1)S(1)}, u32[]{:S(2)}, u32[]{:S(2)}) %collective-permute-start) | collective-permute-done | bytes 524320 | tf_op jit(solution)/shard_map/ppermute | solution.py:479
  19.9 11.2 %all-to-all-start = ((bf16[128,72,128]{2,1,0:T(8,128)(2,1)}), bf16[128,72,128]{2,1,0:T(8,128)(2,1)}, u32[]{:S(2)}, u32[]{:S(2)}) async-start(bf16[128,72,128]{2,1,0:T(8,128)(2,1)} %pack.1), calls=%async_computation | async-start | bytes 4718592 | tf_op jit(solution)/shard_map/all_to_all | solution.py:554
  31.2 11.6 %diffuse_temperature.1.base_ref = f32[4096,128]{1,0:T(8,128)S(1)} custom-call(f32[8,3]{1,0:T(8,128)S(1)} %copy.20.table_ref, s32[128]{0:T(128)S(1)} %copy-done.4, f32[8,64,1024]{2,1,0:T(8,128)S(1)} %copy-done.1, bf16[4,64,1024]{2,1,0:T(8,128)(2,1)S(1)} %collective-permute-done.low_ref, bf16[4,64,1024]{2,1,0:T(8,128)(2,1)S(1)} %collective-permute-done.1.high_ref), custom_call_target="tpu_custom_call" | custom-call | flops 100000000 | bytes 20000000 | tf_op jit(solution)/shard_map/diffuse_temperature/pallas_call | solution.py:556
  42.8 1.3 %copy-done.2 = f32[4096,128]{1,0:T(8,128)} copy-done((f32[4096,128]{1,0:T(8,128)}, f32[4096,128]{1,0:T(8,128)S(1)}, u32[]{:S(2)}) %copy-start.2) | copy-done | bytes 2097176
  44.1 19.2 %all-to-all-done.got_ref = bf16[128,72,128]{2,1,0:T(8,128)(2,1)} async-done(((bf16[128,72,128]{2,1,0:T(8,128)(2,1)}), bf16[128,72,128]{2,1,0:T(8,128)(2,1)}, u32[]{:S(2)}, u32[]{:S(2)}) %all-to-all-start) | async-done | bytes 2359328 | tf_op jit(solution)/shard_map/all_to_all | solution.py:554
  63.3 6.5 %place_tiles.1 = (f32[64,8,8,128]{3,2,1,0:T(8,128)S(1)}, bf16[12,8,16,128]{3,2,1,0:T(8,128)(2,1)S(1)}, bf16[12,8,16,128]{3,2,1,0:T(8,128)(2,1)S(1)}, bf16[8,8,8,...) custom-call(bf16[128,72,128]{2,1,0:T(8,128)(2,1)} %all-to-all-done.got_ref, bf16[8,8,8,128]{3,2,1,0:T(8,128)(2,1)S(1)} %bitcast.26, ...), custom_call_target="tpu_custom_call" | custom-call | flops 5000000000 | bytes 6000000 | tf_op jit(solution)/shard_map/place_tiles/pallas_call | solution.py:573
  69.8 0.4 collective-permute-start.2
  70.2 4.5 %collective-permute-start.3 = (bf16[12,8,16,128]{3,2,1,0:T(8,128)(2,1)S(1)}, bf16[12,8,16,128]{3,2,1,0:T(8,128)(2,1)S(1)}, u32[]{:S(2)}, u32[]{:S(2)}) collective-permute-start(bf16[12,8,16,128]{3,2,1,0:T(8,128)(2,1)S(1)} %get-tuple-element.31), channel_id=1, source_target_pairs={{0,15},{1,0},{2,1},{3,2},{4,3},{5,4},{6,5},{7,6},{8,7},{9,8},{10,9... | collective-permute-start | bytes 1179656 | tf_op jit(solution)/shard_map/ppermute | solution.py:479
  74.7 1.9 %collective-permute-start.4 = (bf16[8,8,8,128]{3,2,1,0:T(8,128)(2,1)S(1)}, bf16[8,8,8,128]{3,2,1,0:T(8,128)(2,1)S(1)}, u32[]{:S(2)}, u32[]{:S(2)}) collective-permute-start(bf16[8,8,8,128]{3,2,1,0:T(8,128)(2,1)S(1)} %get-tuple-element.32), channel_id=1, source_target_pairs={{0,16},{16,32},{32,48},{48,64},{64,80},{80,96},{96,112},{112,0},{1... | collective-permute-start | bytes 393224 | tf_op jit(solution)/shard_map/ppermute | solution.py:479
  76.5 1.9 %collective-permute-done.4.front_ref = bf16[8,8,8,128]{3,2,1,0:T(8,128)(2,1)S(1)} collective-permute-done((bf16[8,8,8,128]{3,2,1,0:T(8,128)(2,1)S(1)}, bf16[8,8,8,128]{3,2,1,0:T(8,128)(2,1)S(1)}, u32[]{:S(2)}, u32[]{:S(2)}) %collective-permute-start.4) | collective-permute-done | bytes 131104 | tf_op jit(solution)/shard_map/ppermute | solution.py:479
  78.5 2.7 %collective-permute-done.5.back_ref = bf16[8,8,8,128]{3,2,1,0:T(8,128)(2,1)S(1)} collective-permute-done((bf16[8,8,8,128]{3,2,1,0:T(8,128)(2,1)S(1)}, bf16[8,8,8,128]{3,2,1,0:T(8,128)(2,1)S(1)}, u32[]{:S(2)}, u32[]{:S(2)}) %collective-permute-start.5) | collective-permute-done | bytes 131104 | tf_op jit(solution)/shard_map/ppermute | solution.py:479
  81.4 4.8 %collective-permute-start.7 = (bf16[3,8,16,128]{3,2,1,0:T(8,128)(2,1)S(1)}, bf16[3,8,16,128]{3,2,1,0:T(8,128)(2,1)S(1)}, u32[]{:S(2)}, u32[]{:S(2)}) collective-permute-start(bf16[3,8,16,128]{3,2,1,0:T(8,128)(2,1)S(1)} %get-tuple-element.35), channel_id=1, source_target_pairs={{0,15},{1,0},{2,1},{3,2},{4,3},{5,4},{6,5},{7,6},{8,7},{9,8},{10,9... | collective-permute-start | bytes 294920 | tf_op jit(solution)/shard_map/ppermute | solution.py:479
  86.1 2.4 %collective-permute-done.6.corner_low_ref = bf16[3,8,16,128]{3,2,1,0:T(8,128)(2,1)S(1)} collective-permute-done((bf16[3,8,16,128]{3,2,1,0:T(8,128)(2,1)S(1)}, bf16[3,8,16,128]{3,2,1,0:T(8,128)(2,1)S(1)}, u32[]{:S(2)}, u32[]{:S(2)}) %collective-permute-start.6) | collective-permute-done | bytes 98336 | tf_op jit(solution)/shard_map/ppermute | solution.py:479
  88.6 12.4 %diffuse_source.1 = (f32[8,8,64,128]{3,2,1,0:T(8,128)}, f32[128,128]{1,0:T(8,128)S(1)}) custom-call(f32[8,3]{1,0:T(8,128)S(1)} %copy.20.table_ref, s32[128]{0:T(128)S(1)} %copy-done.4, f32[4096,128]{1,0:T(8,128)S(1)} %bitcast.24, f32[4096,128]{1,0:T(8,128)S(1)} %copy-done.3, bf16[12,8,16,128]{3,2,1,0:T(8,128)(2,1)S(1)} %collective-permute-done.2.low_ref, ...), custom_call_target="tpu_custom_call" | custom-call | flops 100000000 | bytes 20000000 | tf_op jit(solution)/shard_map/diffuse_source/pallas_call | solution.py:605
  100.9 18.1 %all_to_all.14 = f32[128,1,128]{2,1,0:T(1,128)S(1)} all-to-all(f32[128,1,128]{2,1,0:T(1,128)S(1)} %bitcast.25), channel_id=1, replica_groups=mesh['logic'=8,'slab'=16] {'logic','slab'}, dimensions={0} | all-to-all | bytes 131072 | tf_op jit(solution)/shard_map/all_to_all | solution.py:630
  119.0 0.1 copy.22
  119.1 0.2 reshape.49
  119.3 0.4 copy.25
  119.7 1.1 reshape.51
  (28 shorter events, 0.3 us)
Async XLA Ops:
  0.6 1.6 %copy-start = (f32[8,64,1024]{2,1,0:T(8,128)S(1)}, f32[8,64,1024]{2,1,0:T(8,128)}, u32[]{:S(2)}) copy-start(f32[8,64,1024]{2,1,0:T(8,128)} %state_ref.1) | copy-start | bytes 6291460
  2.2 6.8 %copy-start.5 = (bf16[2048,256]{1,0:T(8,128)(2,1)S(1)}, bf16[2048,256]{1,0:T(8,128)(2,1)}, u32[]{:S(2)}) copy-start(bf16[2048,256]{1,0:T(8,128)(2,1)} %watt_hbm.1) | copy-start | bytes 3145732
  2.2 6.8 %copy-start.6 = (f32[128,32,4]{0,2,1:T(4,128)S(1)}, f32[128,32,4]{0,2,1:T(4,128)}, u32[]{:S(2)}) copy-start(f32[128,32,4]{0,2,1:T(4,128)} %param.15) | copy-start | bytes 196612
  2.2 6.8 %copy-start.7 = (s32[2048,1]{0,1:T(1,128)S(1)}, s32[2048,1]{0,1:T(1,128)}, u32[]{:S(2)}) copy-start(s32[2048,1]{0,1:T(1,128)} %param.12) | copy-start | bytes 24580
  2.2 6.9 %copy-start.8 = (s32[2048]{0:T(1024)S(1)}, s32[2048]{0:T(1024)}, u32[]{:S(2)}) copy-start(s32[2048]{0:T(1024)} %param.13) | copy-start | bytes 24580
  2.2 6.9 %copy-start.9 = (f32[2048]{0:T(1024)S(1)}, f32[2048]{0:T(1024)}, u32[]{:S(2)}) copy-start(f32[2048]{0:T(1024)} %param.11) | copy-start | bytes 24580
  2.5 17.4 %collective-permute-start = (bf16[4,64,1024]{2,1,0:T(8,128)(2,1)S(1)}, bf16[4,64,1024]{2,1,0:T(8,128)(2,1)S(1)}, u32[]{:S(2)}, u32[]{:S(2)}) collective-permute-start(bf16[4,64,1024]{2,1,0:T(8,128)(2,1)S(1)} %get-tuple-element.20), channel_id=1, source_target_pairs={{0,1},{1,2},{2,3},{3,4},{4,5},{5,6},{6,7},{7,8},{8,9},{9,10},{10,1... | collective-permute-start | bytes 1572872 | tf_op jit(solution)/shard_map/ppermute | solution.py:479
  4.6 15.3 %collective-permute-start.1 = (bf16[4,64,1024]{2,1,0:T(8,128)(2,1)S(1)}, bf16[4,64,1024]{2,1,0:T(8,128)(2,1)S(1)}, u32[]{:S(2)}, u32[]{:S(2)}) collective-permute-start(bf16[4,64,1024]{2,1,0:T(8,128)(2,1)S(1)} %get-tuple-element.21), channel_id=1, source_target_pairs={{0,15},{1,0},{2,1},{3,2},{4,3},{5,4},{6,5},{7,6},{8,7},{9,8},{10,9... | collective-permute-start | bytes 1572872 | tf_op jit(solution)/shard_map/ppermute | solution.py:479
  17.6 13.4 %copy-start.10 = (f32[8,3]{0,1:T(4,128)S(1)}, f32[8,3]{0,1:T(4,128)}, u32[]{:S(2)}) copy-start(f32[8,3]{0,1:T(4,128)} %param.16) | copy-start | bytes 292
  17.7 13.5 %copy-start.1 = (f32[8,64,1024]{2,1,0:T(8,128)S(1)}, f32[8,64,1024]{2,1,0:T(8,128)}, u32[]{:S(2)}) copy-start(f32[8,64,1024]{2,1,0:T(8,128)} %state_ref.1) | copy-start | bytes 6291460
  17.7 13.5 %copy-start.4 = (s32[128]{0:T(128)S(1)}, s32[128]{0:T(128)}, u32[]{:S(2)}) copy-start(s32[128]{0:T(128)} %label_ref.3) | copy-start | bytes 1540
  19.9 43.4 %all-to-all-start = ((bf16[128,72,128]{2,1,0:T(8,128)(2,1)}), bf16[128,72,128]{2,1,0:T(8,128)(2,1)}, u32[]{:S(2)}, u32[]{:S(2)}) async-start(bf16[128,72,128]{2,1,0:T(8,128)(2,1)} %pack.1), calls=%async_computation | async-start | bytes 4718592 | tf_op jit(solution)/shard_map/all_to_all | solution.py:554
  42.8 1.3 %copy-start.2 = (f32[4096,128]{1,0:T(8,128)}, f32[4096,128]{1,0:T(8,128)S(1)}, u32[]{:S(2)}) copy-start(f32[4096,128]{1,0:T(8,128)S(1)} %diffuse_temperature.1.base_ref) | copy-start | bytes 6291460
  63.3 25.2 %copy-start.3 = (f32[4096,128]{1,0:T(8,128)S(1)}, f32[4096,128]{1,0:T(8,128)}, u32[]{:S(2)}) copy-start(f32[4096,128]{1,0:T(8,128)} %copy-done.2) | copy-start | bytes 6291460
  69.8 18.7 %collective-permute-start.2 = (bf16[12,8,16,128]{3,2,1,0:T(8,128)(2,1)S(1)}, bf16[12,8,16,128]{3,2,1,0:T(8,128)(2,1)S(1)}, u32[]{:S(2)}, u32[]{:S(2)}) collective-permute-start(bf16[12,8,16,128]{3,2,1,0:T(8,128)(2,1)S(1)} %get-tuple-element.30), channel_id=1, source_target_pairs={{0,1},{1,2},{2,3},{3,4},{4,5},{5,6},{6,7},{7,8},{8,9},{9,10},{10,1... | collective-permute-start | bytes 1179656 | tf_op jit(solution)/shard_map/ppermute | solution.py:479
  70.2 18.4 %collective-permute-start.3 = (bf16[12,8,16,128]{3,2,1,0:T(8,128)(2,1)S(1)}, bf16[12,8,16,128]{3,2,1,0:T(8,128)(2,1)S(1)}, u32[]{:S(2)}, u32[]{:S(2)}) collective-permute-start(bf16[12,8,16,128]{3,2,1,0:T(8,128)(2,1)S(1)} %get-tuple-element.31), channel_id=1, source_target_pairs={{0,15},{1,0},{2,1},{3,2},{4,3},{5,4},{6,5},{7,6},{8,7},{9,8},{10,9... | collective-permute-start | bytes 1179656 | tf_op jit(solution)/shard_map/ppermute | solution.py:479
  74.7 3.8 %collective-permute-start.4 = (bf16[8,8,8,128]{3,2,1,0:T(8,128)(2,1)S(1)}, bf16[8,8,8,128]{3,2,1,0:T(8,128)(2,1)S(1)}, u32[]{:S(2)}, u32[]{:S(2)}) collective-permute-start(bf16[8,8,8,128]{3,2,1,0:T(8,128)(2,1)S(1)} %get-tuple-element.32), channel_id=1, source_target_pairs={{0,16},{16,32},{32,48},{48,64},{64,80},{80,96},{96,112},{112,0},{1... | collective-permute-start | bytes 393224 | tf_op jit(solution)/shard_map/ppermute | solution.py:479
  76.5 4.7 %collective-permute-start.5 = (bf16[8,8,8,128]{3,2,1,0:T(8,128)(2,1)S(1)}, bf16[8,8,8,128]{3,2,1,0:T(8,128)(2,1)S(1)}, u32[]{:S(2)}, u32[]{:S(2)}) collective-permute-start(bf16[8,8,8,128]{3,2,1,0:T(8,128)(2,1)S(1)} %get-tuple-element.33), channel_id=1, source_target_pairs={{0,112},{16,0},{32,16},{48,32},{64,48},{80,64},{96,80},{112,96},{1... | collective-permute-start | bytes 393224 | tf_op jit(solution)/shard_map/ppermute | solution.py:479
  81.3 7.3 %collective-permute-start.6 = (bf16[3,8,16,128]{3,2,1,0:T(8,128)(2,1)S(1)}, bf16[3,8,16,128]{3,2,1,0:T(8,128)(2,1)S(1)}, u32[]{:S(2)}, u32[]{:S(2)}) collective-permute-start(bf16[3,8,16,128]{3,2,1,0:T(8,128)(2,1)S(1)} %get-tuple-element.34), channel_id=1, source_target_pairs={{0,1},{1,2},{2,3},{3,4},{4,5},{5,6},{6,7},{7,8},{8,9},{9,10},{10,1... | collective-permute-start | bytes 294920 | tf_op jit(solution)/shard_map/ppermute | solution.py:479
  81.4 7.2 %collective-permute-start.7 = (bf16[3,8,16,128]{3,2,1,0:T(8,128)(2,1)S(1)}, bf16[3,8,16,128]{3,2,1,0:T(8,128)(2,1)S(1)}, u32[]{:S(2)}, u32[]{:S(2)}) collective-permute-start(bf16[3,8,16,128]{3,2,1,0:T(8,128)(2,1)S(1)} %get-tuple-element.35), channel_id=1, source_target_pairs={{0,15},{1,0},{2,1},{3,2},{4,3},{5,4},{6,5},{7,6},{8,7},{9,8},{10,9... | collective-permute-start | bytes 294920 | tf_op jit(solution)/shard_map/ppermute | solution.py:479

commit v4 on v3

--- a/solution.py
+++ b/solution.py
@@ -19,7 +19,7 @@
 SLABS = 16
 LOGICS = 8
 ROWS = 72
-GROUP = 16
+GROUP = 32
 VMEM = 28 * 1024 * 1024
 F32 = jnp.float32
 BF16 = jnp.bfloat16
@@ -223,32 +223,33 @@
     lax.fori_loop(0, NZ + 2 * halo, layer, 0)
 
 
-def diffuse(coef_ref, read, write, layers, rows, low, high):
+def diffuse(coef, read, write, layers, ranges, low, high):
     lane = iota((8, 128), 1)
 
     def layer(z, _):
-        coef = [coef_ref[z, j] for j in range(6)]
-        before, cell = read(z, rows[0] - 1), read(z, rows[0])
-        for y in range(rows[0], rows[1]):
-            after = read(z, y + 1)
-            step = pltpu.roll(cell, 127, 1)
-            right = jnp.where(lane == 127, pltpu.roll(step, 7, 0), step)
-            step = pltpu.roll(cell, 1, 1)
-            left = jnp.where(lane == 0, pltpu.roll(step, 1, 0), step)
-            value = (
-                coef[0] * cell
-                + coef[1] * left
-                + coef[2] * right
-                + coef[3] * (before + after)
-                + coef[4] * read(z + 1, y)
-                + coef[5] * read(z - 1, y)
-            )
-            if y < 0:
-                value = value * low
-            if y >= NY:
-                value = value * high
-            write(z, y, value)
-            before, cell = cell, after
+        c = [coef(z, j) for j in range(6)]
+        for rows in ranges:
+            before, cell = read(z, rows[0] - 1), read(z, rows[0])
+            for y in range(rows[0], rows[1]):
+                after = read(z, y + 1)
+                step = pltpu.roll(cell, 127, 1)
+                right = jnp.where(lane == 127, pltpu.roll(step, 7, 0), step)
+                step = pltpu.roll(cell, 1, 1)
+                left = jnp.where(lane == 0, pltpu.roll(step, 1, 0), step)
+                value = (
+                    c[0] * cell
+                    + c[1] * left
+                    + c[2] * right
+                    + c[3] * (before + after)
+                    + c[4] * read(z + 1, y)
+                    + c[5] * read(z - 1, y)
+                )
+                if y < 0:
+                    value = value * low
+                if y >= NY:
+                    value = value * high
+                write(z, y, value)
+                before, cell = cell, after
         return 0
 
     lax.fori_loop(layers[0], layers[1], layer, 0)
@@ -325,18 +326,61 @@
                 dst[row_of(z, y, halo), :] = value
 
         diffuse(
-            coef_ref, read, write, (halo - reach, halo + NZ + reach), (-wide, NY + wide), low, high
+            lambda z, j: coef_ref[z, j],
+            read,
+            write,
+            (halo - reach, halo + NZ + reach),
+            [(-wide, NY + wide)],
+            low,
+            high,
         )
 
 
-def source_kernel(
-    table_ref, label_ref, source_ref, base_ref, low_ref, high_ref, front_ref, back_ref,
-    corner_low_ref, corner_high_ref, out_ref, coarse_ref,
-    coef_ref, cells_ref, s_ref, a_ref, b_ref, rim_ref, edge_ref, sums_ref,
+def inner_kernel(coef_ref, source_ref, s_ref, a_ref, b_ref):
+    halo = 3
+
+    def own(z, _):
+        for y in range(NY):
+            start = (z * 8 + y // 8) * 64 + y % 8
+            s_ref[row_of(z + halo, y, halo), :] = source_ref[pl.ds(start, 8, stride=8), :]
+        return 0
+
+    lax.fori_loop(0, NZ, own, 0)
+    for step, (src, dst) in enumerate(((s_ref, a_ref), (a_ref, b_ref))):
+
+        def read(z, y, src=src):
+            return src[row_of(z, y, halo), :]
+
+        def write(z, y, value, dst=dst):
+            dst[row_of(z, y, halo), :] = value + s_ref[row_of(z, y, halo), :]
+
+        diffuse(
+            lambda z, j: coef_ref[z + 1, j],
+            read,
+            write,
+            (halo + 1 + step, halo + NZ - 1 - step),
+            [(2 + step, NY - 2 - step)],
+            None,
+            None,
+        )
+
+
+def outer_kernel(
+    s_in, a_in, b_in, coef_ref, base_ref, low_ref, high_ref, front_ref, back_ref,
+    corner_low_ref, corner_high_ref, out_hbm, coarse_ref,
+    s_ref, a_ref, b_ref, out_ref, cells_ref, rim_ref, edge_ref, sums_ref, sems, in_sems,
 ):
     halo = 3
-    fill_coefficients(coef_ref, table_ref, label_ref, halo)
     zero = jnp.zeros((8, 128), F32)
+    coef = lambda z, j: coef_ref[z + 1, j]
+    loads = []
+    for step, (src, dst) in enumerate(((s_in, s_ref), (a_in, a_ref), (b_in, b_ref))):
+        skip = (0, 2, 3)[step]
+        for z in range(halo + step, halo + NZ - step):
+            rows = pl.ds((z * (NY + 8) + 4 + skip) * 8, (NY - 2 * skip) * 8)
+            loads.append(pltpu.make_async_copy(src.at[rows], dst.at[rows], in_sems.at[len(loads)]))
+    for load in loads:
+        load.start()
 
     def rim_at(z, y):
         slot = y + 4 if y < 1 else y - NY + 6
@@ -349,13 +393,15 @@
     low, high = edges("logic", LOGICS)
     below, above = edges("slab", SLABS)
 
-    def strips(z, front, back, keep_front, keep_back):
+    def strips(z, slot, front, back, keep_front, keep_back):
         for xb in range(8):
-            cells_ref[0, pl.ds(xb * 8, 8), :] = front(xb).astype(F32)
-            cells_ref[1, pl.ds(xb * 8, 8), :] = back(xb).astype(F32)
+            cells_ref[slot, pl.ds(xb * 8, 8), :] = front(xb).astype(F32)
+            cells_ref[slot + 1, pl.ds(xb * 8, 8), :] = back(xb).astype(F32)
+        rim_ref[rim_at(z, 0), :] = zero
+        rim_ref[rim_at(z, NY - 1), :] = zero
         for at in range(8):
-            before = cells_ref[0, pl.ds(at, 8, stride=8), :] * keep_front
-            after = cells_ref[1, pl.ds(at, 8, stride=8), :] * keep_back
+            before = cells_ref[slot, pl.ds(at, 8, stride=8), :] * keep_front
+            after = cells_ref[slot + 1, pl.ds(at, 8, stride=8), :] * keep_back
             if at < 4:
                 rim_ref[rim_at(z, NY + at), :] = after
                 if at:
@@ -368,31 +414,33 @@
     rim_ref[pl.ds(0, 80), :] = jnp.zeros((80, 128), F32)
     rim_ref[pl.ds(15 * 80, 80), :] = jnp.zeros((80, 128), F32)
 
-    def own(z, _):
-        for y in range(NY):
-            start = (z * 8 + y // 8) * 64 + y % 8
-            s_ref[row_of(z + halo, y, halo), :] = source_ref[pl.ds(start, 8, stride=8), :]
-        strips(z + halo, lambda xb: front_ref[z, xb], lambda xb: back_ref[z, xb], low, high)
-        return 0
-
-    lax.fori_loop(0, NZ, own, 0)
+    def own(i, _):
+        for half in range(2):
+            z = 2 * i + half
+            strips(
+                z + halo, 2 * half, lambda xb: front_ref[z, xb], lambda xb: back_ref[z, xb], low, high
+            )
+        return 0
+
+    lax.fori_loop(0, NZ // 2, own, 0)
 
     def outer(z, _):
-        for base, body, corner, keep in (
-            (0, low_ref, corner_low_ref, below),
-            (11, high_ref, corner_high_ref, above),
+        for side, (base, body, corner, keep) in enumerate(
+            ((0, low_ref, corner_low_ref, below), (11, high_ref, corner_high_ref, above))
         ):
             for block in range(4):
+                slot = 8 * side + 2 * block
                 for xb in range(8):
                     two = body[z * 4 + block, xb].astype(F32)
-                    cells_ref[4, pl.ds(xb * 8, 8), :] = two[:8]
-                    cells_ref[5, pl.ds(xb * 8, 8), :] = two[8:]
+                    cells_ref[slot, pl.ds(xb * 8, 8), :] = two[:8]
+                    cells_ref[slot + 1, pl.ds(xb * 8, 8), :] = two[8:]
                 for y in range(16):
                     s_ref[row_of(z + base, 16 * block + y, halo), :] = (
-                        cells_ref[4 + y // 8, pl.ds(y % 8, 8, stride=8), :] * keep
+                        cells_ref[slot + y // 8, pl.ds(y % 8, 8, stride=8), :] * keep
                     )
             strips(
                 z + base,
+                16 + 2 * side,
                 lambda xb: corner[z, xb].astype(F32)[:8],
                 lambda xb: corner[z, xb].astype(F32)[8:],
                 keep * low,
@@ -401,53 +449,69 @@
         return 0
 
     lax.fori_loop(0, halo, outer, 0)
+    for load in loads[:8]:
+        load.wait()
 
     def read_rim(z, y):
         return rim_ref[rim_at(z, y), :]
 
     def write_edge(z, y, value):
         edge_ref[edge_at(z, y), :] = value + s_ref[row_of(z, y, halo), :]
-
-    def sides(z, _):
-        rim_ref[rim_at(z, 0), :] = zero
-        rim_ref[rim_at(z, NY - 1), :] = zero
-        ky = coef_ref[z, 3]
-        write_edge(z, 0, ky * read_rim(z, -1))
-        write_edge(z, NY - 1, ky * read_rim(z, NY))
-        return 0
-
-    lax.fori_loop(0, NZ + 2 * halo, sides, 0)
-    diffuse(coef_ref, read_rim, write_edge, (0, NZ + 2 * halo), (-3, 0), low, high)
-    diffuse(coef_ref, read_rim, write_edge, (0, NZ + 2 * halo), (NY, NY + 3), low, high)
-    for step in range(3):
-        src = (None, a_ref, b_ref)[step]
-        dst = (a_ref, b_ref, None)[step]
-        reach = 2 - step
-
-        def read(z, y, src=src):
-            if src is None:
-                if 1 <= y < NY - 1:
-                    return s_ref[row_of(z, y, halo), :]
-                return edge_ref[edge_at(z, y), :]
-            return src[row_of(z, y, halo), :]
-
-        def write(z, y, value, dst=dst, step=step):
-            value = value + s_ref[row_of(z, y, halo), :]
-            if step < 2:
-                dst[row_of(z, y, halo), :] = value
-                return
-            own = z - halo
-            value = value + base_ref[pl.ds(pl.multiple_of((own * NY + y) * 8, 8), 8), :]
-            out_ref[own, y // 8, pl.ds(y % 8, 8, stride=8), :] = value
-            here = pl.ds(pl.multiple_of((own * 4 + y // 16) * 8, 8), 8)
-            if y % 16 == 0:
-                sums_ref[here, :] = value
-            else:
-                sums_ref[here, :] = sums_ref[here, :] + value
-
-        diffuse(
-            coef_ref, read, write, (halo - reach, halo + NZ + reach), (-reach, NY + reach), low, high
-        )
+        if y == -1:
+            edge_ref[edge_at(z, 0), :] = (
+                coef(z, 3) * read_rim(z, -1) + s_ref[row_of(z, 0, halo), :]
+            )
+        if y == NY:
+            edge_ref[edge_at(z, NY - 1), :] = (
+                coef(z, 3) * read_rim(z, NY) + s_ref[row_of(z, NY - 1, halo), :]
+            )
+
+    diffuse(coef, read_rim, write_edge, (0, NZ + 2 * halo), [(-3, 0), (NY, NY + 3)], low, high)
+
+    def first(z, y):
+        if 1 <= y < NY - 1:
+            return s_ref[row_of(z, y, halo), :]
+        return edge_ref[edge_at(z, y), :]
+
+    def second(z, y):
+        return a_ref[row_of(z, y, halo), :]
+
+    def third(z, y):
+        return b_ref[row_of(z, y, halo), :]
+
+    def to(ref):
+        def write(z, y, value):
+            ref[row_of(z, y, halo), :] = value + s_ref[row_of(z, y, halo), :]
+
+        return write
+
+    every = lambda reach: [(-reach, NY + reach)]
+    diffuse(coef, first, to(a_ref), (1, 4), every(2), low, high)
+    diffuse(coef, first, to(a_ref), (10, 13), every(2), low, high)
+    diffuse(coef, first, to(a_ref), (4, 10), [(-2, 2), (NY - 2, NY + 2)], low, high)
+    for load in loads[8:]:
+        load.wait()
+    diffuse(coef, second, to(b_ref), (2, 5), every(1), low, high)
+    diffuse(coef, second, to(b_ref), (9, 12), every(1), low, high)
+    diffuse(coef, second, to(b_ref), (5, 9), [(-1, 3), (NY - 3, NY + 1)], low, high)
+
+    def store(z):
+        return pltpu.make_async_copy(out_ref.at[z], out_hbm.at[z], sems.at[z])
+
+    def write_out(z, y, value):
+        own = z - halo
+        value = value + s_ref[row_of(z, y, halo), :]
+        value = value + base_ref[pl.ds(pl.multiple_of((own * NY + y) * 8, 8), 8), :]
+        out_ref[own, y // 8, pl.ds(y % 8, 8, stride=8), :] = value
+        here = pl.ds(pl.multiple_of((own * 4 + y // 16) * 8, 8), 8)
+        if y % 16 == 0:
+            sums_ref[here, :] = value
+        else:
+            sums_ref[here, :] = sums_ref[here, :] + value
+        if y == NY - 1:
+            store(own).start()
+
+    diffuse(coef, third, write_out, (halo, halo + NZ), every(0), low, high)
     exact = lax.Precision.HIGHEST
     lines = lax.dot_general(
         jnp.ones((8, 128), F32), sums_ref[...], (((1,), (1,)), ((), ())),
@@ -456,6 +520,8 @@
     pairs = jnp.where((iota((256, 128), 0) >> 1) == iota((256, 128), 1), 1.0 / 4096.0, 0.0)
     means = jnp.dot(lines, pairs, precision=exact, preferred_element_type=F32)
     coarse_ref[...] = jnp.broadcast_to(means[0:1, :], (DEV, 128))
+    for z in range(NZ):
+        store(z).wait()
 
 
 def vmem(count):
@@ -553,13 +619,12 @@
     packed, low, high = lax.optimization_barrier((packed, low, high))
     got = lax.all_to_all(packed, both, split_axis=0, concat_axis=0, tiled=True)
 
-    base = pl.pallas_call(
+    base, coef = pl.pallas_call(
         temperature_kernel,
-        out_shape=pltpu.VMEM((NZ * NY * 8, 128), F32),
+        out_shape=[shape((NZ * NY * 8, 128), F32), shape((16, 6, 8, 128), F32)],
         in_specs=smem(2) + vmem(3),
-        out_specs=pl.BlockSpec(memory_space=pltpu.VMEM),
+        out_specs=vmem(2),
         scratch_shapes=[
-            pltpu.VMEM((16, 6, 8, 128), F32),
             pltpu.VMEM((16, 8, 64, 128), F32),
             pltpu.VMEM((16 * 72 * 8, 128), F32),
             pltpu.VMEM((16 * 72 * 8, 128), F32),
@@ -568,7 +633,7 @@
         cost_estimate=cost(100_000_000, 20_000_000),
         name="diffuse_temperature",
     )(conductivity_lookup, substance_of_slab, state, low, high)
-    got, base = lax.optimization_barrier((got, base))
+    got, base, coef = lax.optimization_barrier((got, base, coef))
 
     source, lower, upper, first, last = pl.pallas_call(
         scatter_kernel,
@@ -602,28 +667,37 @@
     s_corner_low = shift(to_high, "slab", 1)
     s_corner_high = shift(to_low, "slab", -1)
 
+    rows = shape((14 * 72 * 8, 128), F32)
+    parts = pl.pallas_call(
+        inner_kernel,
+        out_shape=[rows] * 3,
+        in_specs=vmem(2),
+        out_specs=vmem(3),
+        compiler_params=params(),
+        cost_estimate=cost(20_000_000, 10_000_000),
+        name="diffuse_inner",
+    )(coef, source.reshape(4096, 128))
     new_state, coarse = pl.pallas_call(
-        source_kernel,
-        out_shape=[shape((NZ, 8, 64, 128), F32), shape((DEV, 128), F32)],
-        in_specs=smem(2) + vmem(8),
-        out_specs=vmem(2),
+        outer_kernel,
+        out_shape=[pltpu.HBM((NZ, 8, 64, 128), F32), shape((DEV, 128), F32)],
+        in_specs=[pl.BlockSpec(memory_space=pl.ANY)] * 3 + vmem(8),
+        out_specs=[pl.BlockSpec(memory_space=pltpu.HBM)] + vmem(1),
         scratch_shapes=[
-            pltpu.VMEM((14, 6, 8, 128), F32),
-            pltpu.VMEM((6, 64, 128), F32),
             pltpu.VMEM((14 * 72 * 8, 128), F32),
             pltpu.VMEM((14 * 72 * 8, 128), F32),
             pltpu.VMEM((14 * 72 * 8, 128), F32),
+            pltpu.VMEM((NZ, 8, 64, 128), F32),
+            pltpu.VMEM((20, 64, 128), F32),
             pltpu.VMEM((16 * 80, 128), F32),
             pltpu.VMEM((14 * 64, 128), F32),
             pltpu.VMEM((256, 128), F32),
+            pltpu.SemaphoreType.DMA((NZ,)),
+            pltpu.SemaphoreType.DMA((18,)),
         ],
         compiler_params=params(),
         cost_estimate=cost(100_000_000, 20_000_000),
-        name="diffuse_source",
-    )(
-        conductivity_lookup, substance_of_slab, source.reshape(4096, 128), base,
-        s_low, s_high, s_front, s_back, s_corner_low, s_corner_high,
-    )
+        name="diffuse_outer",
+    )(*parts, coef, base, s_low, s_high, s_front, s_back, s_corner_low, s_corner_high)
     thermal_state = (
         new_state.reshape(NZ, 8, 8, 8, 128).transpose(0, 1, 3, 2, 4).reshape(NZ, NY, 1024)
     )

time: 121 us -> 122 us (level)
  local copies, waits for them, and re-layouts: 4.84 us -> 6.66 us
  waiting for transfers between devices: 28.6 us -> 26.8 us
    unnamed x25 -> x33, local copies, waits for them, and re-layouts: 4.57 us -> 6.39 us
    ppermute x8, waiting for transfers between devices: 9.34 us -> 7.61 us  [shift(): lax.ppermute(value, axis, [(i, (i + by) % count) for i in range(count)])]
    pallas_call x2 -> x3, Pallas kernels: 23.9 us -> 25.5 us  [the longest x1 11.6 us: per_device(): pl.pallas_call(temperature_kernel, out_shape=[shape((NZ * NY * 8, 128), F...]
  transfers between devices with their start and end apart: 9 -> 9, of which waited for: 5 -> 4; matrix products, arithmetic and copies ran while one was open for 0% -> 0% of each run, Pallas kernels for 17% -> 18%
where the time goes in v4:
time: 122 us
  Pallas kernels  39.9 us (33%)
  starting transfers between devices  28.7 us (24%)
  waiting for transfers between devices  26.8 us (22%)
  blocking collectives  18 us (15%)
  local copies, waits for them, and re-layouts  6.66 us (5%)
  between operations  1.56 us (1%)
    all_to_all x1, waiting for transfers between devices, per_device(): got = lax.all_to_all(packed, both, split_axis=0, concat_axis=0, tiled=True)  19.2 us
    all_to_all x1, blocking collectives, per_device(): lax.all_to_all(coarse, both, split_axis=0, concat_axis=0, tiled=True)  18 us
    ppermute x8, starting transfers between devices, shift(): lax.ppermute(value, axis, [(i, (i + by) % count) for i in range(count)])  17.5 us
    pallas_call x1, Pallas kernels, per_device(): pl.pallas_call(temperature_kernel, out_shape=[shape((NZ * NY * 8, 128), F...  11.6 us
    pallas_call x1, Pallas kernels, per_device(): pl.pallas_call(outer_kernel, out_shape=[pltpu.HBM((NZ, 8, 64, 128), F32),...  11.5 us
    all_to_all x1, starting transfers between devices, per_device(): got = lax.all_to_all(packed, both, split_axis=0, concat_axis=0, tiled=True)  11.2 us
    pallas_call x1, Pallas kernels, per_device(): pl.pallas_call(pack_kernel, out_shape=pltpu.HBM((DEV, ROWS, 128), BF16),...  7.83 us
    ppermute x8, waiting for transfers between devices, shift(): lax.ppermute(value, axis, [(i, (i + by) % count) for i in range(count)])  7.61 us
  transfers between devices with their start and end apart: 9, of which 4 were waited for; matrix products, arithmetic and copies ran while one was open for 0% of the time, Pallas kernels for 18%

profile of v4, /device:TPU:1, one launch (start us, length us, event | category | flops | bytes accessed | tf_op | source)
XLA Modules:
  0.0 121.7 jit_solution(9066302854551667779)
XLA Ops:
  0.6 1.6 %copy-done = f32[8,64,1024]{2,1,0:T(8,128)S(1)} copy-done((f32[8,64,1024]{2,1,0:T(8,128)S(1)}, f32[8,64,1024]{2,1,0:T(8,128)}, u32[]{:S(2)}) %copy-start) | copy-done | bytes 2097176
  2.2 0.2 edges.1
  2.5 2.1 %collective-permute-start = (bf16[4,64,1024]{2,1,0:T(8,128)(2,1)S(1)}, bf16[4,64,1024]{2,1,0:T(8,128)(2,1)S(1)}, u32[]{:S(2)}, u32[]{:S(2)}) collective-permute-start(bf16[4,64,1024]{2,1,0:T(8,128)(2,1)S(1)} %get-tuple-element.26), channel_id=1, source_target_pairs={{0,1},{1,2},{2,3},{3,4},{4,5},{5,6},{6,7},{7,8},{8,9},{9,10},{10,1... | collective-permute-start | bytes 1572872 | tf_op jit(solution)/shard_map/ppermute | solution.py:545
  4.6 3.8 %collective-permute-start.1 = (bf16[4,64,1024]{2,1,0:T(8,128)(2,1)S(1)}, bf16[4,64,1024]{2,1,0:T(8,128)(2,1)S(1)}, u32[]{:S(2)}, u32[]{:S(2)}) collective-permute-start(bf16[4,64,1024]{2,1,0:T(8,128)(2,1)S(1)} %get-tuple-element.27), channel_id=1, source_target_pairs={{0,15},{1,0},{2,1},{3,2},{4,3},{5,4},{6,5},{7,6},{8,7},{9,8},{10,9... | collective-permute-start | bytes 1572872 | tf_op jit(solution)/shard_map/ppermute | solution.py:545
  9.1 7.8 %pack.1 = bf16[128,72,128]{2,1,0:T(8,128)(2,1)} custom-call(s32[1]{0:T(128)S(6)} %copy.24.count_ref, s32[1,2048]{1,0:T(1,128)S(1)} %bitcast.29, s32[1,2048]{1,0:T(1,128)S(1)} %bitcast.30, f32[1,2048]{1,0:T(1,128)S(1)} %bitcast.31, f32[128,128]{1,0:T(8,128)S(1)} %bitcast.28, bf16[2048,256]{1,0:T(8,128)(2,1)S(1)} %copy-done.5), custom_call_target="tpu_custom_call" | custom-call | flops 5000000000 | bytes 4000000 | tf_op jit(solution)/shard_map/pack/pallas_call | solution.py:588
  17.0 2.9 %collective-permute-done.low_ref = bf16[4,64,1024]{2,1,0:T(8,128)(2,1)S(1)} collective-permute-done((bf16[4,64,1024]{2,1,0:T(8,128)(2,1)S(1)}, bf16[4,64,1024]{2,1,0:T(8,128)(2,1)S(1)}, u32[]{:S(2)}, u32[]{:S(2)}) %collective-permute-start) | collective-permute-done | bytes 524320 | tf_op jit(solution)/shard_map/ppermute | solution.py:545
  19.9 11.2 %all-to-all-start = ((bf16[128,72,128]{2,1,0:T(8,128)(2,1)}), bf16[128,72,128]{2,1,0:T(8,128)(2,1)}, u32[]{:S(2)}, u32[]{:S(2)}) async-start(bf16[128,72,128]{2,1,0:T(8,128)(2,1)} %pack.1), calls=%async_computation | async-start | bytes 4718592 | tf_op jit(solution)/shard_map/all_to_all | solution.py:620
  31.2 11.6 %diffuse_temperature.1 = (f32[4096,128]{1,0:T(8,128)S(1)}, f32[16,6,8,128]{3,2,1,0:T(8,128)S(1)}) custom-call(f32[8,3]{1,0:T(8,128)S(1)} %copy.17.table_ref, s32[128]{0:T(128)S(1)} %copy-done.4, f32[8,64,1024]{2,1,0:T(8,128)S(1)} %copy-done.1, bf16[4,64,1024]{2,1,0:T(8,128)(2,1)S(1)} %collective-permute-done.low_ref, ...), custom_call_target="tpu_custom_call" | custom-call | flops 100000000 | bytes 20000000 | tf_op jit(solution)/shard_map/diffuse_temperature/pallas_call | solution.py:622
  42.8 1.3 %copy-done.2 = f32[4096,128]{1,0:T(8,128)} copy-done((f32[4096,128]{1,0:T(8,128)}, f32[4096,128]{1,0:T(8,128)S(1)}, u32[]{:S(2)}) %copy-start.2) | copy-done | bytes 2097176
  44.1 19.2 %all-to-all-done.got_ref = bf16[128,72,128]{2,1,0:T(8,128)(2,1)} async-done(((bf16[128,72,128]{2,1,0:T(8,128)(2,1)}), bf16[128,72,128]{2,1,0:T(8,128)(2,1)}, u32[]{:S(2)}, u32[]{:S(2)}) %all-to-all-start) | async-done | bytes 2359328 | tf_op jit(solution)/shard_map/all_to_all | solution.py:620
  63.3 0.9 copy-done.7
  64.2 0.9 copy-done.9
  65.1 6.3 %place_tiles.1 = (f32[64,8,8,128]{3,2,1,0:T(8,128)S(1)}, bf16[12,8,16,128]{3,2,1,0:T(8,128)(2,1)S(1)}, bf16[12,8,16,128]{3,2,1,0:T(8,128)(2,1)S(1)}, bf16[8,8,8,...) custom-call(bf16[128,72,128]{2,1,0:T(8,128)(2,1)} %all-to-all-done.got_ref, bf16[8,8,8,128]{3,2,1,0:T(8,128)(2,1)S(1)} %bitcast.26, ...), custom_call_target="tpu_custom_call" | custom-call | flops 5000000000 | bytes 6000000 | tf_op jit(solution)/shard_map/place_tiles/pallas_call | solution.py:638
  71.5 0.4 collective-permute-start.2
  71.9 4.5 %collective-permute-start.3 = (bf16[12,8,16,128]{3,2,1,0:T(8,128)(2,1)S(1)}, bf16[12,8,16,128]{3,2,1,0:T(8,128)(2,1)S(1)}, u32[]{:S(2)}, u32[]{:S(2)}) collective-permute-start(bf16[12,8,16,128]{3,2,1,0:T(8,128)(2,1)S(1)} %get-tuple-element.43), channel_id=1, source_target_pairs={{0,15},{1,0},{2,1},{3,2},{4,3},{5,4},{6,5},{7,6},{8,7},{9,8},{10,9... | collective-permute-start | bytes 1179656 | tf_op jit(solution)/shard_map/ppermute | solution.py:545
  76.4 1.9 %collective-permute-start.4 = (bf16[8,8,8,128]{3,2,1,0:T(8,128)(2,1)S(1)}, bf16[8,8,8,128]{3,2,1,0:T(8,128)(2,1)S(1)}, u32[]{:S(2)}, u32[]{:S(2)}) collective-permute-start(bf16[8,8,8,128]{3,2,1,0:T(8,128)(2,1)S(1)} %get-tuple-element.44), channel_id=1, source_target_pairs={{0,16},{16,32},{32,48},{48,64},{64,80},{80,96},{96,112},{112,0},{1... | collective-permute-start | bytes 393224 | tf_op jit(solution)/shard_map/ppermute | solution.py:545
  78.2 1.9 %collective-permute-done.4.front_ref = bf16[8,8,8,128]{3,2,1,0:T(8,128)(2,1)S(1)} collective-permute-done((bf16[8,8,8,128]{3,2,1,0:T(8,128)(2,1)S(1)}, bf16[8,8,8,128]{3,2,1,0:T(8,128)(2,1)S(1)}, u32[]{:S(2)}, u32[]{:S(2)}) %collective-permute-start.4) | collective-permute-done | bytes 131104 | tf_op jit(solution)/shard_map/ppermute | solution.py:545
  80.2 2.7 %collective-permute-done.5.back_ref = bf16[8,8,8,128]{3,2,1,0:T(8,128)(2,1)S(1)} collective-permute-done((bf16[8,8,8,128]{3,2,1,0:T(8,128)(2,1)S(1)}, bf16[8,8,8,128]{3,2,1,0:T(8,128)(2,1)S(1)}, u32[]{:S(2)}, u32[]{:S(2)}) %collective-permute-start.5) | collective-permute-done | bytes 131104 | tf_op jit(solution)/shard_map/ppermute | solution.py:545
  83.0 4.8 %collective-permute-start.7 = (bf16[3,8,16,128]{3,2,1,0:T(8,128)(2,1)S(1)}, bf16[3,8,16,128]{3,2,1,0:T(8,128)(2,1)S(1)}, u32[]{:S(2)}, u32[]{:S(2)}) collective-permute-start(bf16[3,8,16,128]{3,2,1,0:T(8,128)(2,1)S(1)} %get-tuple-element.47), channel_id=1, source_target_pairs={{0,15},{1,0},{2,1},{3,2},{4,3},{5,4},{6,5},{7,6},{8,7},{9,8},{10,9... | collective-permute-start | bytes 294920 | tf_op jit(solution)/shard_map/ppermute | solution.py:545
  87.8 2.4 %diffuse_inner.1 = (f32[8064,128]{1,0:T(8,128)S(1)}, f32[8064,128]{1,0:T(8,128)S(1)}, f32[8064,128]{1,0:T(8,128)S(1)}) custom-call(f32[16,6,8,128]{3,2,1,0:T(8,128)S(1)} %get-tuple-element.33.coef_ref, f32[4096,128]{1,0:T(8,128)S(1)} %bitcast.24), custom_call_target="tpu_custom_call" | custom-call | flops 20000000 | bytes 10000000 | tf_op jit(solution)/shard_map/diffuse_inner/pallas_call | solution.py:671
  90.3 11.5 %diffuse_outer.1 = (f32[8,8,64,128]{3,2,1,0:T(8,128)}, f32[128,128]{1,0:T(8,128)S(1)}) custom-call(f32[8064,128]{1,0:T(8,128)S(1)} %get-tuple-element.38.s_in, f32[8064,128]{1,0:T(8,128)S(1)} %get-tuple-element.39.a_in, f32[8064,128]{1,0:T(8,128)S(1)} %get-tuple-element.40.b_in, f32[16,6,8,128]{3,2,1,0:T(8,128)S(1)} %get-tuple-element.33.coef_ref, ...), custom_call_target="tpu_custom_call" | custom-call | flops 100000000 | bytes 20000000 | tf_op jit(solution)/shard_map/diffuse_outer/pallas_call | solution.py:680
  101.8 18.0 %all_to_all.14 = f32[128,1,128]{2,1,0:T(1,128)S(1)} all-to-all(f32[128,1,128]{2,1,0:T(1,128)S(1)} %bitcast.25), channel_id=1, replica_groups=mesh['logic'=8,'slab'=16] {'logic','slab'}, dimensions={0} | all-to-all | bytes 131072 | tf_op jit(solution)/shard_map/all_to_all | solution.py:704
  120.1 0.4 copy.22
  120.5 1.1 reshape.51
  (37 shorter events, 0.5 us)
Async XLA Ops:
  0.6 1.6 %copy-start = (f32[8,64,1024]{2,1,0:T(8,128)S(1)}, f32[8,64,1024]{2,1,0:T(8,128)}, u32[]{:S(2)}) copy-start(f32[8,64,1024]{2,1,0:T(8,128)} %state_ref.1) | copy-start | bytes 6291460
  2.2 6.9 %copy-start.5 = (bf16[2048,256]{1,0:T(8,128)(2,1)S(1)}, bf16[2048,256]{1,0:T(8,128)(2,1)}, u32[]{:S(2)}) copy-start(bf16[2048,256]{1,0:T(8,128)(2,1)} %watt_hbm.1) | copy-start | bytes 3145732
  2.2 6.9 %copy-start.10 = (f32[128,32,4]{0,2,1:T(4,128)S(1)}, f32[128,32,4]{0,2,1:T(4,128)}, u32[]{:S(2)}) copy-start(f32[128,32,4]{0,2,1:T(4,128)} %param.15) | copy-start | bytes 196612
  2.2 6.9 %copy-start.11 = (s32[2048,1]{0,1:T(1,128)S(1)}, s32[2048,1]{0,1:T(1,128)}, u32[]{:S(2)}) copy-start(s32[2048,1]{0,1:T(1,128)} %param.12) | copy-start | bytes 24580
  2.2 6.9 %copy-start.12 = (s32[2048]{0:T(1024)S(1)}, s32[2048]{0:T(1024)}, u32[]{:S(2)}) copy-start(s32[2048]{0:T(1024)} %param.13) | copy-start | bytes 24580
  2.2 6.9 %copy-start.13 = (f32[2048]{0:T(1024)S(1)}, f32[2048]{0:T(1024)}, u32[]{:S(2)}) copy-start(f32[2048]{0:T(1024)} %param.11) | copy-start | bytes 24580
  2.5 14.5 %copy-start.6 = (bf16[2,4,8,8,128]{4,3,2,1,0:T(8,128)(2,1)}, bf16[2,4,8,8,128]{4,3,2,1,0:T(8,128)(2,1)S(1)}, u32[]{:S(2)}) copy-start(bf16[2,4,8,8,128]{4,3,2,1,0:T(8,128)(2,1)S(1)} %get-tuple-element.35) | copy-start | bytes 393220
  2.5 14.5 %copy-start.8 = (bf16[2,4,8,8,128]{4,3,2,1,0:T(8,128)(2,1)}, bf16[2,4,8,8,128]{4,3,2,1,0:T(8,128)(2,1)S(1)}, u32[]{:S(2)}) copy-start(bf16[2,4,8,8,128]{4,3,2,1,0:T(8,128)(2,1)S(1)} %get-tuple-element.36) | copy-start | bytes 393220
  2.5 17.4 %collective-permute-start = (bf16[4,64,1024]{2,1,0:T(8,128)(2,1)S(1)}, bf16[4,64,1024]{2,1,0:T(8,128)(2,1)S(1)}, u32[]{:S(2)}, u32[]{:S(2)}) collective-permute-start(bf16[4,64,1024]{2,1,0:T(8,128)(2,1)S(1)} %get-tuple-element.26), channel_id=1, source_target_pairs={{0,1},{1,2},{2,3},{3,4},{4,5},{5,6},{6,7},{7,8},{8,9},{9,10},{10,1... | collective-permute-start | bytes 1572872 | tf_op jit(solution)/shard_map/ppermute | solution.py:545
  4.6 15.3 %collective-permute-start.1 = (bf16[4,64,1024]{2,1,0:T(8,128)(2,1)S(1)}, bf16[4,64,1024]{2,1,0:T(8,128)(2,1)S(1)}, u32[]{:S(2)}, u32[]{:S(2)}) collective-permute-start(bf16[4,64,1024]{2,1,0:T(8,128)(2,1)S(1)} %get-tuple-element.27), channel_id=1, source_target_pairs={{0,15},{1,0},{2,1},{3,2},{4,3},{5,4},{6,5},{7,6},{8,7},{9,8},{10,9... | collective-permute-start | bytes 1572872 | tf_op jit(solution)/shard_map/ppermute | solution.py:545
  17.0 14.1 %copy-start.14 = (f32[8,3]{0,1:T(4,128)S(1)}, f32[8,3]{0,1:T(4,128)}, u32[]{:S(2)}) copy-start(f32[8,3]{0,1:T(4,128)} %param.16) | copy-start | bytes 292
  17.0 14.2 %copy-start.1 = (f32[8,64,1024]{2,1,0:T(8,128)S(1)}, f32[8,64,1024]{2,1,0:T(8,128)}, u32[]{:S(2)}) copy-start(f32[8,64,1024]{2,1,0:T(8,128)} %state_ref.1) | copy-start | bytes 6291460
  17.0 14.2 %copy-start.4 = (s32[128]{0:T(128)S(1)}, s32[128]{0:T(128)}, u32[]{:S(2)}) copy-start(s32[128]{0:T(128)} %label_ref.1) | copy-start | bytes 1540
  19.9 43.4 %all-to-all-start = ((bf16[128,72,128]{2,1,0:T(8,128)(2,1)}), bf16[128,72,128]{2,1,0:T(8,128)(2,1)}, u32[]{:S(2)}, u32[]{:S(2)}) async-start(bf16[128,72,128]{2,1,0:T(8,128)(2,1)} %pack.1), calls=%async_computation | async-start | bytes 4718592 | tf_op jit(solution)/shard_map/all_to_all | solution.py:620
  42.8 1.3 %copy-start.2 = (f32[4096,128]{1,0:T(8,128)}, f32[4096,128]{1,0:T(8,128)S(1)}, u32[]{:S(2)}) copy-start(f32[4096,128]{1,0:T(8,128)S(1)} %get-tuple-element.41.base_ref) | copy-start | bytes 6291460
  63.3 0.9 copy-start.7
  64.2 0.9 copy-start.9
  71.5 18.8 %copy-start.3 = (f32[4096,128]{1,0:T(8,128)S(1)}, f32[4096,128]{1,0:T(8,128)}, u32[]{:S(2)}) copy-start(f32[4096,128]{1,0:T(8,128)} %copy-done.2) | copy-start | bytes 6291460
  71.5 18.8 %collective-permute-start.2 = (bf16[12,8,16,128]{3,2,1,0:T(8,128)(2,1)S(1)}, bf16[12,8,16,128]{3,2,1,0:T(8,128)(2,1)S(1)}, u32[]{:S(2)}, u32[]{:S(2)}) collective-permute-start(bf16[12,8,16,128]{3,2,1,0:T(8,128)(2,1)S(1)} %get-tuple-element.42), channel_id=1, source_target_pairs={{0,1},{1,2},{2,3},{3,4},{4,5},{5,6},{6,7},{7,8},{8,9},{9,10},{10,1... | collective-permute-start | bytes 1179656 | tf_op jit(solution)/shard_map/ppermute | solution.py:545
  71.9 18.4 %collective-permute-start.3 = (bf16[12,8,16,128]{3,2,1,0:T(8,128)(2,1)S(1)}, bf16[12,8,16,128]{3,2,1,0:T(8,128)(2,1)S(1)}, u32[]{:S(2)}, u32[]{:S(2)}) collective-permute-start(bf16[12,8,16,128]{3,2,1,0:T(8,128)(2,1)S(1)} %get-tuple-element.43), channel_id=1, source_target_pairs={{0,15},{1,0},{2,1},{3,2},{4,3},{5,4},{6,5},{7,6},{8,7},{9,8},{10,9... | collective-permute-start | bytes 1179656 | tf_op jit(solution)/shard_map/ppermute | solution.py:545
  76.4 3.8 %collective-permute-start.4 = (bf16[8,8,8,128]{3,2,1,0:T(8,128)(2,1)S(1)}, bf16[8,8,8,128]{3,2,1,0:T(8,128)(2,1)S(1)}, u32[]{:S(2)}, u32[]{:S(2)}) collective-permute-start(bf16[8,8,8,128]{3,2,1,0:T(8,128)(2,1)S(1)} %get-tuple-element.44), channel_id=1, source_target_pairs={{0,16},{16,32},{32,48},{48,64},{64,80},{80,96},{96,112},{112,0},{1... | collective-permute-start | bytes 393224 | tf_op jit(solution)/shard_map/ppermute | solution.py:545
  78.2 4.7 %collective-permute-start.5 = (bf16[8,8,8,128]{3,2,1,0:T(8,128)(2,1)S(1)}, bf16[8,8,8,128]{3,2,1,0:T(8,128)(2,1)S(1)}, u32[]{:S(2)}, u32[]{:S(2)}) collective-permute-start(bf16[8,8,8,128]{3,2,1,0:T(8,128)(2,1)S(1)} %get-tuple-element.45), channel_id=1, source_target_pairs={{0,112},{16,0},{32,16},{48,32},{64,48},{80,64},{96,80},{112,96},{1... | collective-permute-start | bytes 393224 | tf_op jit(solution)/shard_map/ppermute | solution.py:545
  83.0 7.3 %collective-permute-start.6 = (bf16[3,8,16,128]{3,2,1,0:T(8,128)(2,1)S(1)}, bf16[3,8,16,128]{3,2,1,0:T(8,128)(2,1)S(1)}, u32[]{:S(2)}, u32[]{:S(2)}) collective-permute-start(bf16[3,8,16,128]{3,2,1,0:T(8,128)(2,1)S(1)} %get-tuple-element.46), channel_id=1, source_target_pairs={{0,1},{1,2},{2,3},{3,4},{4,5},{5,6},{6,7},{7,8},{8,9},{9,10},{10,1... | collective-permute-start | bytes 294920 | tf_op jit(solution)/shard_map/ppermute | solution.py:545
  83.0 7.2 %collective-permute-start.7 = (bf16[3,8,16,128]{3,2,1,0:T(8,128)(2,1)S(1)}, bf16[3,8,16,128]{3,2,1,0:T(8,128)(2,1)S(1)}, u32[]{:S(2)}, u32[]{:S(2)}) collective-permute-start(bf16[3,8,16,128]{3,2,1,0:T(8,128)(2,1)S(1)} %get-tuple-element.47), channel_id=1, source_target_pairs={{0,15},{1,0},{2,1},{3,2},{4,3},{5,4},{6,5},{7,6},{8,7},{9,8},{10,9... | collective-permute-start | bytes 294920 | tf_op jit(solution)/shard_map/ppermute | solution.py:545

commit v5 on v4

--- a/solution.py
+++ b/solution.py
@@ -30,9 +30,27 @@
     return lax.broadcasted_iota(I32, shape, dim)
 
 
-def edge_kernel(lower_ref, upper_ref, to_high_ref, to_low_ref, first_ref, last_ref):
-    to_low_ref[...] = lower_ref[...].astype(BF16)
-    to_high_ref[...] = upper_ref[...].astype(BF16)
+def edge_kernel(
+    lower_ref, upper_ref, to_high_ref, to_low_ref, far_high_ref, far_low_ref, first_ref, last_ref
+):
+    step = pl.program_id(0)
+
+    @pl.when(step < 3)
+    def _():
+        to_low_ref[...] = lower_ref[...].astype(BF16)
+
+    @pl.when(step == 3)
+    def _():
+        far_low_ref[...] = lower_ref[...].astype(BF16)
+
+    @pl.when(step > 0)
+    def _():
+        to_high_ref[...] = upper_ref[...].astype(BF16)
+
+    @pl.when(step == 0)
+    def _():
+        far_high_ref[...] = upper_ref[...].astype(BF16)
+
     for half, ref in ((0, lower_ref), (1, upper_ref)):
         for xb in range(8):
             cols = slice(128 * xb, 128 * xb + 128)
@@ -151,8 +169,15 @@
 
 
 def scatter_kernel(
-    got_ref, first_ref, last_ref, source_ref, low_ref, high_ref, front_ref, back_ref, label_ref,
+    got_ref, first_hbm, last_hbm, source_ref, low_ref, high_ref, front_ref, back_ref,
+    label_ref, first_ref, last_ref, sems,
 ):
+    loads = [
+        pltpu.make_async_copy(first_hbm, first_ref, sems.at[0]),
+        pltpu.make_async_copy(last_hbm, last_ref, sems.at[1]),
+    ]
+    for load in loads:
+        load.start()
     labels = got_ref[:, 64:72, :].reshape(DEV * 8, 128)
     row = iota((DEV * 8, 128), 0)
     lane = iota((DEV * 8, 128), 1)
@@ -168,6 +193,8 @@
     both = jnp.concatenate([left, right], axis=1)
     wanted = iota((512, 128), 0) * 4
     upper = iota((8, 128), 0) < 4
+    for load in loads:
+        load.wait()
     for c in range(4):
         chosen = jnp.concatenate(
             [
@@ -252,7 +279,9 @@
                 before, cell = cell, after
         return 0
 
-    lax.fori_loop(layers[0], layers[1], layer, 0)
+    count = layers[1] - layers[0]
+    unroll = 2 if count % 2 == 0 else 3 if count % 3 == 0 else 1
+    lax.fori_loop(layers[0], layers[1], layer, 0, unroll=unroll)
 
 
 def edges(axis, count):
@@ -288,6 +317,9 @@
         return 0
 
     lax.fori_loop(0, NZ + 2 * halo, clear, 0)
+    for z in (0, NZ + 2 * halo - 1):
+        for y in range(NY):
+            a_ref[row_of(z, y, halo), :] = jnp.zeros((8, 128), F32)
 
     def own(z, _):
         for block in range(8):
@@ -300,7 +332,7 @@
     below, above = edges("slab", SLABS)
 
     def outer(z, _):
-        for base, body, keep in ((0, low_ref, below), (12, high_ref, above)):
+        for base, body, keep in ((1, low_ref, below), (12, high_ref, above)):
             for block in range(4):
                 two = body[z, 16 * block : 16 * block + 16, :].astype(F32)
                 spread(z + base, 2 * block, two[:8])
@@ -308,7 +340,7 @@
             gather(z + base, keep)
         return 0
 
-    lax.fori_loop(0, halo, outer, 0)
+    lax.fori_loop(0, halo - 1, outer, 0)
     low, high = edges("logic", LOGICS)
     bufs = (a_ref, b_ref)
     for step in range(4):
@@ -366,21 +398,13 @@
 
 
 def outer_kernel(
-    s_in, a_in, b_in, coef_ref, base_ref, low_ref, high_ref, front_ref, back_ref,
-    corner_low_ref, corner_high_ref, out_hbm, coarse_ref,
-    s_ref, a_ref, b_ref, out_ref, cells_ref, rim_ref, edge_ref, sums_ref, sems, in_sems,
+    _s, _a, _b, coef_ref, base_ref, far_low_ref, far_high_ref, low_ref, high_ref, front_ref, back_ref,
+    corner_low_ref, corner_high_ref, out_hbm, coarse_ref, s_ref, a_ref, b_ref,
+    out_ref, cells_ref, rim_ref, edge_ref, sums_ref, sems,
 ):
     halo = 3
     zero = jnp.zeros((8, 128), F32)
     coef = lambda z, j: coef_ref[z + 1, j]
-    loads = []
-    for step, (src, dst) in enumerate(((s_in, s_ref), (a_in, a_ref), (b_in, b_ref))):
-        skip = (0, 2, 3)[step]
-        for z in range(halo + step, halo + NZ - step):
-            rows = pl.ds((z * (NY + 8) + 4 + skip) * 8, (NY - 2 * skip) * 8)
-            loads.append(pltpu.make_async_copy(src.at[rows], dst.at[rows], in_sems.at[len(loads)]))
-    for load in loads:
-        load.start()
 
     def rim_at(z, y):
         slot = y + 4 if y < 1 else y - NY + 6
@@ -449,8 +473,20 @@
         return 0
 
     lax.fori_loop(0, halo, outer, 0)
-    for load in loads[:8]:
-        load.wait()
+    for side, (z, j, body, keep) in enumerate(((0, 5, far_low_ref, below), (13, 4, far_high_ref, above))):
+        factor = coef(z, j) * keep
+        for block in range(4):
+            slot = 8 * side + 2 * block
+            two = body[0, 16 * block : 16 * block + 16, :].astype(F32)
+            for xb in range(8):
+                part = two[:, 128 * xb : 128 * xb + 128]
+                cells_ref[slot, pl.ds(xb * 8, 8), :] = part[:8]
+                cells_ref[slot + 1, pl.ds(xb * 8, 8), :] = part[8:]
+            for y in range(16):
+                at = row_of(z, 16 * block + y, halo)
+                s_ref[at, :] = (
+                    s_ref[at, :] + factor * cells_ref[slot + y // 8, pl.ds(y % 8, 8, stride=8), :]
+                )
 
     def read_rim(z, y):
         return rim_ref[rim_at(z, y), :]
@@ -489,8 +525,6 @@
     diffuse(coef, first, to(a_ref), (1, 4), every(2), low, high)
     diffuse(coef, first, to(a_ref), (10, 13), every(2), low, high)
     diffuse(coef, first, to(a_ref), (4, 10), [(-2, 2), (NY - 2, NY + 2)], low, high)
-    for load in loads[8:]:
-        load.wait()
     diffuse(coef, second, to(b_ref), (2, 5), every(1), low, high)
     diffuse(coef, second, to(b_ref), (9, 12), every(1), low, high)
     diffuse(coef, second, to(b_ref), (5, 9), [(-1, 3), (NY - 3, NY + 1)], low, high)
@@ -559,12 +593,14 @@
     state = initial_heat_state
     both = ("logic", "slab")
     shape = jax.ShapeDtypeStruct
-    to_high, to_low, t_first, t_last = pl.pallas_call(
+    to_high, to_low, far_high, far_low, t_first, t_last = pl.pallas_call(
         edge_kernel,
         grid=(NZ // 2,),
         out_shape=[
-            shape((4, NY, 1024), BF16),
-            shape((4, NY, 1024), BF16),
+            shape((3, NY, 1024), BF16),
+            shape((3, NY, 1024), BF16),
+            shape((1, NY, 1024), BF16),
+            shape((1, NY, 1024), BF16),
             shape((2, 4, 8, 8, 128), BF16),
             shape((2, 4, 8, 8, 128), BF16),
         ],
@@ -573,8 +609,10 @@
             pl.BlockSpec((1, NY, 1024), lambda i: (i + NZ // 2, 0, 0)),
         ],
         out_specs=[
-            pl.BlockSpec((1, NY, 1024), lambda i: (i, 0, 0)),
-            pl.BlockSpec((1, NY, 1024), lambda i: (i, 0, 0)),
+            pl.BlockSpec((1, NY, 1024), lambda i: (jnp.maximum(i - 1, 0), 0, 0)),
+            pl.BlockSpec((1, NY, 1024), lambda i: (jnp.minimum(i, 2), 0, 0)),
+            pl.BlockSpec((1, NY, 1024), lambda i: (0, 0, 0)),
+            pl.BlockSpec((1, NY, 1024), lambda i: (0, 0, 0)),
             pl.BlockSpec((2, 1, 8, 8, 128), lambda i: (0, i, 0, 0, 0)),
             pl.BlockSpec((2, 1, 8, 8, 128), lambda i: (0, i, 0, 0, 0)),
         ],
@@ -616,7 +654,11 @@
         prior_reduced_heat_map.transpose(1, 2, 0).reshape(128, LAYERS),
         dynamic_wattage,
     )
-    packed, low, high = lax.optimization_barrier((packed, low, high))
+    packed, low, high, far_high, far_low = lax.optimization_barrier(
+        (packed, low, high, far_high, far_low)
+    )
+    t_low = shift(far_high, "slab", 1)
+    t_high = shift(far_low, "slab", -1)
     got = lax.all_to_all(packed, both, split_axis=0, concat_axis=0, tiled=True)
 
     base, coef = pl.pallas_call(
@@ -644,13 +686,25 @@
             shape((NZ, 8, 8, 128), BF16),
             shape((NZ, 8, 8, 128), BF16),
         ],
-        in_specs=vmem(3),
+        in_specs=vmem(1) + [pl.BlockSpec(memory_space=pltpu.HBM)] * 2,
         out_specs=vmem(5),
-        scratch_shapes=[pltpu.VMEM((32, 128), I32)],
+        scratch_shapes=[
+            pltpu.VMEM((32, 128), I32),
+            pltpu.VMEM((NZ, 8, 8, 128), BF16),
+            pltpu.VMEM((NZ, 8, 8, 128), BF16),
+            pltpu.SemaphoreType.DMA((2,)),
+        ],
         compiler_params=params(),
         cost_estimate=cost(5_000_000_000, 6_000_000),
         name="place_tiles",
-    )(got, t_first.reshape(NZ, 8, 8, 128), t_last.reshape(NZ, 8, 8, 128))
+    )(
+        got,
+        pltpu.with_memory_space_constraint(t_first.reshape(NZ, 8, 8, 128), pltpu.HBM),
+        pltpu.with_memory_space_constraint(t_last.reshape(NZ, 8, 8, 128), pltpu.HBM),
+    )
+    lower, upper, first, last, t_low, t_high = lax.optimization_barrier(
+        (lower, upper, first, last, t_low, t_high)
+    )
     s_low = shift(upper, "slab", 1)
     s_high = shift(lower, "slab", -1)
     s_front = shift(last, "logic", 1)
@@ -667,7 +721,7 @@
     s_corner_low = shift(to_high, "slab", 1)
     s_corner_high = shift(to_low, "slab", -1)
 
-    rows = shape((14 * 72 * 8, 128), F32)
+    rows = pltpu.VMEM((14 * 72 * 8, 128), F32)
     parts = pl.pallas_call(
         inner_kernel,
         out_shape=[rows] * 3,
@@ -677,27 +731,24 @@
         cost_estimate=cost(20_000_000, 10_000_000),
         name="diffuse_inner",
     )(coef, source.reshape(4096, 128))
-    new_state, coarse = pl.pallas_call(
+    new_state, coarse, *_ = pl.pallas_call(
         outer_kernel,
-        out_shape=[pltpu.HBM((NZ, 8, 64, 128), F32), shape((DEV, 128), F32)],
-        in_specs=[pl.BlockSpec(memory_space=pl.ANY)] * 3 + vmem(8),
-        out_specs=[pl.BlockSpec(memory_space=pltpu.HBM)] + vmem(1),
+        out_shape=[pltpu.HBM((NZ, 8, 64, 128), F32), shape((DEV, 128), F32)] + [rows] * 3,
+        in_specs=vmem(13),
+        out_specs=[pl.BlockSpec(memory_space=pltpu.HBM)] + vmem(4),
+        input_output_aliases={0: 2, 1: 3, 2: 4},
         scratch_shapes=[
-            pltpu.VMEM((14 * 72 * 8, 128), F32),
-            pltpu.VMEM((14 * 72 * 8, 128), F32),
-            pltpu.VMEM((14 * 72 * 8, 128), F32),
             pltpu.VMEM((NZ, 8, 64, 128), F32),
             pltpu.VMEM((20, 64, 128), F32),
             pltpu.VMEM((16 * 80, 128), F32),
             pltpu.VMEM((14 * 64, 128), F32),
             pltpu.VMEM((256, 128), F32),
             pltpu.SemaphoreType.DMA((NZ,)),
-            pltpu.SemaphoreType.DMA((18,)),
         ],
         compiler_params=params(),
         cost_estimate=cost(100_000_000, 20_000_000),
         name="diffuse_outer",
-    )(*parts, coef, base, s_low, s_high, s_front, s_back, s_corner_low, s_corner_high)
+    )(*parts, coef, base, t_low, t_high, s_low, s_high, s_front, s_back, s_corner_low, s_corner_high)
     thermal_state = (
         new_state.reshape(NZ, 8, 8, 8, 128).transpose(0, 1, 3, 2, 4).reshape(NZ, NY, 1024)
     )

time: 122 us -> 114 us (0.934)
  Pallas kernels: 39.9 us -> 34.4 us
  waiting for transfers between devices: 26.8 us -> 21.6 us
  starting transfers between devices: 28.7 us -> 33 us
  local copies, waits for them, and re-layouts: 6.66 us -> 4.86 us
    pallas_call x1, Pallas kernels: 11.5 us -> 6.38 us  [per_device(): pl.pallas_call(outer_kernel, out_shape=[pltpu.HBM((NZ, 8, 64, 128), F32),...]
    ppermute x8 -> x10, starting transfers between devices: 17.5 us -> 21.9 us  [shift(): lax.ppermute(value, axis, [(i, (i + by) % count) for i in range(count)])]
    all_to_all x1, waiting for transfers between devices: 19.2 us -> 16.5 us  [per_device(): got = lax.all_to_all(packed, both, split_axis=0, concat_axis=0, tiled=True)]
    ppermute x8 -> x10, waiting for transfers between devices: 7.61 us -> 5.13 us  [shift(): lax.ppermute(value, axis, [(i, (i + by) % count) for i in range(count)])]
    unnamed x33 -> x29, local copies, waits for them, and re-layouts: 6.39 us -> 4.58 us
    pallas_call x1, Pallas kernels: 11.6 us -> 9.87 us  [per_device(): pl.pallas_call(temperature_kernel, out_shape=[shape((NZ * NY * 8, 128), F...]
  transfers between devices with their start and end apart: 9 -> 11, of which waited for: 4 -> 5; matrix products, arithmetic and copies ran while one was open for 0% -> 0% of each run, Pallas kernels for 18% -> 24%
where the time goes in v5:
time: 114 us; the launch traced here: 113 us
  Pallas kernels  34.4 us (30%)
  starting transfers between devices  33 us (29%)
  waiting for transfers between devices  21.6 us (19%)
  blocking collectives  18.1 us (16%)
  local copies, waits for them, and re-layouts  4.86 us (4%)
  between operations  1.53 us (1%)
    ppermute x10, starting transfers between devices, shift(): lax.ppermute(value, axis, [(i, (i + by) % count) for i in range(count)])  21.9 us
    all_to_all x1, blocking collectives, per_device(): lax.all_to_all(coarse, both, split_axis=0, concat_axis=0, tiled=True)  18.1 us
    all_to_all x1, waiting for transfers between devices, per_device(): got = lax.all_to_all(packed, both, split_axis=0, concat_axis=0, tiled=True)  16.5 us
    all_to_all x1, starting transfers between devices, per_device(): got = lax.all_to_all(packed, both, split_axis=0, concat_axis=0, tiled=True)  11.2 us
    pallas_call x1, Pallas kernels, per_device(): pl.pallas_call(temperature_kernel, out_shape=[shape((NZ * NY * 8, 128), F...  9.87 us
    pallas_call x1, Pallas kernels, per_device(): pl.pallas_call(pack_kernel, out_shape=pltpu.HBM((DEV, ROWS, 128), BF16),...  7.83 us
    pallas_call x1, Pallas kernels, per_device(): pl.pallas_call(scatter_kernel, out_shape=[shape((64, 8, 8, 128), F32), sh...  7.14 us
    pallas_call x1, Pallas kernels, per_device(): pl.pallas_call(outer_kernel, out_shape=[pltpu.HBM((NZ, 8, 64, 128), F32),...  6.38 us
  transfers between devices with their start and end apart: 11, of which 5 were waited for; matrix products, arithmetic and copies ran while one was open for 0% of the time, Pallas kernels for 24%

profile of v5, /device:TPU:1, one launch (start us, length us, event | category | flops | bytes accessed | tf_op | source)
XLA Modules:
  0.0 113.5 jit_solution(8145685310318630282)
XLA Ops:
  0.6 1.6 %copy-done = f32[8,64,1024]{2,1,0:T(8,128)S(1)} copy-done((f32[8,64,1024]{2,1,0:T(8,128)S(1)}, f32[8,64,1024]{2,1,0:T(8,128)}, u32[]{:S(2)}) %copy-start) | copy-done | bytes 2097176
  2.2 1.0 edges.1
  3.3 2.0 %collective-permute-start = (bf16[3,64,1024]{2,1,0:T(8,128)(2,1)S(1)}, bf16[3,64,1024]{2,1,0:T(8,128)(2,1)S(1)}, u32[]{:S(2)}, u32[]{:S(2)}) collective-permute-start(bf16[3,64,1024]{2,1,0:T(8,128)(2,1)S(1)} %get-tuple-element.36), channel_id=1, source_target_pairs={{0,1},{1,2},{2,3},{3,4},{4,5},{5,6},{6,7},{7,8},{8,9},{9,10},{10,1... | collective-permute-start | bytes 1179656 | tf_op jit(solution)/shard_map/ppermute | solution.py:579
  5.3 3.8 %collective-permute-start.1 = (bf16[3,64,1024]{2,1,0:T(8,128)(2,1)S(1)}, bf16[3,64,1024]{2,1,0:T(8,128)(2,1)S(1)}, u32[]{:S(2)}, u32[]{:S(2)}) collective-permute-start(bf16[3,64,1024]{2,1,0:T(8,128)(2,1)S(1)} %get-tuple-element.37), channel_id=1, source_target_pairs={{0,15},{1,0},{2,1},{3,2},{4,3},{5,4},{6,5},{7,6},{8,7},{9,8},{10,9... | collective-permute-start | bytes 1179656 | tf_op jit(solution)/shard_map/ppermute | solution.py:579
  9.8 7.8 %pack.1 = bf16[128,72,128]{2,1,0:T(8,128)(2,1)} custom-call(s32[1]{0:T(128)S(6)} %copy.30.count_ref, s32[1,2048]{1,0:T(1,128)S(1)} %bitcast.29, s32[1,2048]{1,0:T(1,128)S(1)} %bitcast.30, f32[1,2048]{1,0:T(1,128)S(1)} %bitcast.31, f32[128,128]{1,0:T(8,128)S(1)} %bitcast.28, bf16[2048,256]{1,0:T(8,128)(2,1)S(1)} %copy-done.5), custom_call_target="tpu_custom_call" | custom-call | flops 5000000000 | bytes 4000000 | tf_op jit(solution)/shard_map/pack/pallas_call | solution.py:626
  17.8 11.2 %all-to-all-start = ((bf16[128,72,128]{2,1,0:T(8,128)(2,1)}), bf16[128,72,128]{2,1,0:T(8,128)(2,1)}, u32[]{:S(2)}, u32[]{:S(2)}) async-start(bf16[128,72,128]{2,1,0:T(8,128)(2,1)} %pack.1), calls=%async_computation | async-start | bytes 4718592 | tf_op jit(solution)/shard_map/all_to_all | solution.py:662
  29.1 1.4 %collective-permute-start.2 = (bf16[1,64,1024]{2,1,0:T(8,128)(2,1)}, bf16[1,64,1024]{2,1,0:T(8,128)(2,1)S(1)}, u32[]{:S(2)}, u32[]{:S(2)}) collective-permute-start(bf16[1,64,1024]{2,1,0:T(8,128)(2,1)} %get-tuple-element.58), channel_id=1, source_target_pairs={{0,1},{1,2},{2,3},{3,4},{4,5},{5,6},{6,7},{7,8},{8,9},{9,10},{10,1... | collective-permute-start | bytes 393224 | tf_op jit(solution)/shard_map/ppermute | solution.py:579
  30.4 3.5 %collective-permute-start.3 = (bf16[1,64,1024]{2,1,0:T(8,128)(2,1)}, bf16[1,64,1024]{2,1,0:T(8,128)(2,1)S(1)}, u32[]{:S(2)}, u32[]{:S(2)}) collective-permute-start(bf16[1,64,1024]{2,1,0:T(8,128)(2,1)} %get-tuple-element.59), channel_id=1, source_target_pairs={{0,15},{1,0},{2,1},{3,2},{4,3},{5,4},{6,5},{7,6},{8,7},{9,8},{10,9... | collective-permute-start | bytes 393224 | tf_op jit(solution)/shard_map/ppermute | solution.py:579
  34.0 9.9 %diffuse_temperature.1 = (f32[4096,128]{1,0:T(8,128)S(1)}, f32[16,6,8,128]{3,2,1,0:T(8,128)S(1)}) custom-call(f32[8,3]{1,0:T(8,128)S(1)} %copy.20.table_ref, s32[128]{0:T(128)S(1)} %copy-done.4, f32[8,64,1024]{2,1,0:T(8,128)S(1)} %copy-done.1, bf16[3,64,1024]{2,1,0:T(8,128)(2,1)S(1)} %collective-permute-done.low_ref, ...), custom_call_target="tpu_custom_call" | custom-call | flops 100000000 | bytes 20000000 | tf_op jit(solution)/shard_map/diffuse_temperature/pallas_call | solution.py:664
  43.8 1.3 %copy-done.2 = f32[4096,128]{1,0:T(8,128)} copy-done((f32[4096,128]{1,0:T(8,128)}, f32[4096,128]{1,0:T(8,128)S(1)}, u32[]{:S(2)}) %copy-start.2) | copy-done | bytes 2097176
  45.2 16.5 %all-to-all-done.got_ref = bf16[128,72,128]{2,1,0:T(8,128)(2,1)} async-done(((bf16[128,72,128]{2,1,0:T(8,128)(2,1)}), bf16[128,72,128]{2,1,0:T(8,128)(2,1)}, u32[]{:S(2)}, u32[]{:S(2)}) %all-to-all-start) | async-done | bytes 2359328 | tf_op jit(solution)/shard_map/all_to_all | solution.py:662
  61.7 7.1 %place_tiles.1 = (f32[64,8,8,128]{3,2,1,0:T(8,128)S(1)}, bf16[12,8,16,128]{3,2,1,0:T(8,128)(2,1)S(1)}, bf16[12,8,16,128]{3,2,1,0:T(8,128)(2,1)S(1)}, bf16[8,8,8,...) custom-call(bf16[128,72,128]{2,1,0:T(8,128)(2,1)} %all-to-all-done.got_ref, bf16[8,8,8,128]{3,2,1,0:T(8,128)(2,1)} %bitcast.26, ...), custom_call_target="tpu_custom_call" | custom-call | flops 5000000000 | bytes 6000000 | tf_op jit(solution)/shard_map/place_tiles/pallas_call | solution.py:680
  68.8 0.6 collective-permute-start.4
  69.5 4.2 %collective-permute-start.5 = (bf16[12,8,16,128]{3,2,1,0:T(8,128)(2,1)S(1)}, bf16[12,8,16,128]{3,2,1,0:T(8,128)(2,1)S(1)}, u32[]{:S(2)}, u32[]{:S(2)}) collective-permute-start(bf16[12,8,16,128]{3,2,1,0:T(8,128)(2,1)S(1)} %get-tuple-element.63), channel_id=1, source_target_pairs={{0,15},{1,0},{2,1},{3,2},{4,3},{5,4},{6,5},{7,6},{8,7},{9,8},{10,9... | collective-permute-start | bytes 1179656 | tf_op jit(solution)/shard_map/ppermute | solution.py:579
  73.7 1.4 %collective-permute-start.6 = (bf16[8,8,8,128]{3,2,1,0:T(8,128)(2,1)S(1)}, bf16[8,8,8,128]{3,2,1,0:T(8,128)(2,1)S(1)}, u32[]{:S(2)}, u32[]{:S(2)}) collective-permute-start(bf16[8,8,8,128]{3,2,1,0:T(8,128)(2,1)S(1)} %get-tuple-element.64), channel_id=1, source_target_pairs={{0,16},{16,32},{32,48},{48,64},{64,80},{80,96},{96,112},{112,0},{1... | collective-permute-start | bytes 393224 | tf_op jit(solution)/shard_map/ppermute | solution.py:579
  75.2 1.9 %collective-permute-done.6.front_ref = bf16[8,8,8,128]{3,2,1,0:T(8,128)(2,1)S(1)} collective-permute-done((bf16[8,8,8,128]{3,2,1,0:T(8,128)(2,1)S(1)}, bf16[8,8,8,128]{3,2,1,0:T(8,128)(2,1)S(1)}, u32[]{:S(2)}, u32[]{:S(2)}) %collective-permute-start.6) | collective-permute-done | bytes 131104 | tf_op jit(solution)/shard_map/ppermute | solution.py:579
  77.1 2.7 %collective-permute-done.7.back_ref = bf16[8,8,8,128]{3,2,1,0:T(8,128)(2,1)S(1)} collective-permute-done((bf16[8,8,8,128]{3,2,1,0:T(8,128)(2,1)S(1)}, bf16[8,8,8,128]{3,2,1,0:T(8,128)(2,1)S(1)}, u32[]{:S(2)}, u32[]{:S(2)}) %collective-permute-start.7) | collective-permute-done | bytes 131104 | tf_op jit(solution)/shard_map/ppermute | solution.py:579
  80.0 4.8 %collective-permute-start.9 = (bf16[3,8,16,128]{3,2,1,0:T(8,128)(2,1)S(1)}, bf16[3,8,16,128]{3,2,1,0:T(8,128)(2,1)S(1)}, u32[]{:S(2)}, u32[]{:S(2)}) collective-permute-start(bf16[3,8,16,128]{3,2,1,0:T(8,128)(2,1)S(1)} %get-tuple-element.67), channel_id=1, source_target_pairs={{0,15},{1,0},{2,1},{3,2},{4,3},{5,4},{6,5},{7,6},{8,7},{9,8},{10,9... | collective-permute-start | bytes 294920 | tf_op jit(solution)/shard_map/ppermute | solution.py:579
  84.7 2.1 %diffuse_inner.1 = (f32[8064,128]{1,0:T(8,128)S(1)}, f32[8064,128]{1,0:T(8,128)S(1)}, f32[8064,128]{1,0:T(8,128)S(1)}) custom-call(f32[16,6,8,128]{3,2,1,0:T(8,128)S(1)} %get-tuple-element.45.coef_ref, f32[4096,128]{1,0:T(8,128)S(1)} %bitcast.24), custom_call_target="tpu_custom_call" | custom-call | flops 20000000 | bytes 10000000 | tf_op jit(solution)/shard_map/diffuse_inner/pallas_call | solution.py:725
  86.8 0.3 collective-permute-done.8.corner_low_ref
  87.2 6.4 %diffuse_outer.1 = (f32[8,8,64,128]{3,2,1,0:T(8,128)}, f32[128,128]{1,0:T(8,128)S(1)}, f32[8064,128]{1,0:T(8,128)S(1)}, f32[8064,128]{1,0:T(8,128)S(1)}, f32[8064,128]{1,0:T(8,128)S(1)}) custom-call(f32[8064,128]{1,0:T(8,128)S(1)} %get-tuple-element.50._s, ...), custom_call_target="tpu_custom_call", output_to_operand_aliasing={{2}: (0, {}), {3}: (1, {}), {4}: (2, {})} | custom-call | flops 100000000 | bytes 20000000 | tf_op jit(solution)/shard_map/diffuse_outer/pallas_call | solution.py:734
  93.6 18.1 %all_to_all.14 = f32[128,1,128]{2,1,0:T(1,128)S(1)} all-to-all(f32[128,1,128]{2,1,0:T(1,128)S(1)} %bitcast.25), channel_id=1, replica_groups=mesh['logic'=8,'slab'=16] {'logic','slab'}, dimensions={0} | all-to-all | bytes 131072 | tf_op jit(solution)/shard_map/all_to_all | solution.py:755
  111.9 0.4 copy.25
  112.3 1.1 reshape.51
  (37 shorter events, 0.7 us)
Async XLA Ops:
  0.6 1.6 %copy-start = (f32[8,64,1024]{2,1,0:T(8,128)S(1)}, f32[8,64,1024]{2,1,0:T(8,128)}, u32[]{:S(2)}) copy-start(f32[8,64,1024]{2,1,0:T(8,128)} %state_ref.1) | copy-start | bytes 6291460
  2.2 7.5 %copy-start.5 = (bf16[2048,256]{1,0:T(8,128)(2,1)S(1)}, bf16[2048,256]{1,0:T(8,128)(2,1)}, u32[]{:S(2)}) copy-start(bf16[2048,256]{1,0:T(8,128)(2,1)} %watt_hbm.1) | copy-start | bytes 3145732
  2.2 7.5 %copy-start.8 = (f32[128,32,4]{0,2,1:T(4,128)S(1)}, f32[128,32,4]{0,2,1:T(4,128)}, u32[]{:S(2)}) copy-start(f32[128,32,4]{0,2,1:T(4,128)} %param.15) | copy-start | bytes 196612
  2.2 7.5 %copy-start.9 = (s32[2048,1]{0,1:T(1,128)S(1)}, s32[2048,1]{0,1:T(1,128)}, u32[]{:S(2)}) copy-start(s32[2048,1]{0,1:T(1,128)} %param.12) | copy-start | bytes 24580
  2.2 7.5 %copy-start.10 = (s32[2048]{0:T(1024)S(1)}, s32[2048]{0:T(1024)}, u32[]{:S(2)}) copy-start(s32[2048]{0:T(1024)} %param.13) | copy-start | bytes 24580
  2.2 7.5 %copy-start.11 = (f32[2048]{0:T(1024)S(1)}, f32[2048]{0:T(1024)}, u32[]{:S(2)}) copy-start(f32[2048]{0:T(1024)} %param.11) | copy-start | bytes 24580
  3.3 14.4 %copy-start.6 = (bf16[2,4,8,8,128]{4,3,2,1,0:T(8,128)(2,1)}, bf16[2,4,8,8,128]{4,3,2,1,0:T(8,128)(2,1)S(1)}, u32[]{:S(2)}) copy-start(bf16[2,4,8,8,128]{4,3,2,1,0:T(8,128)(2,1)S(1)} %get-tuple-element.47) | copy-start | bytes 393220
  3.3 14.4 %copy-start.7 = (bf16[2,4,8,8,128]{4,3,2,1,0:T(8,128)(2,1)}, bf16[2,4,8,8,128]{4,3,2,1,0:T(8,128)(2,1)S(1)}, u32[]{:S(2)}) copy-start(bf16[2,4,8,8,128]{4,3,2,1,0:T(8,128)(2,1)S(1)} %get-tuple-element.48) | copy-start | bytes 393220
  3.3 14.5 %collective-permute-start = (bf16[3,64,1024]{2,1,0:T(8,128)(2,1)S(1)}, bf16[3,64,1024]{2,1,0:T(8,128)(2,1)S(1)}, u32[]{:S(2)}, u32[]{:S(2)}) collective-permute-start(bf16[3,64,1024]{2,1,0:T(8,128)(2,1)S(1)} %get-tuple-element.36), channel_id=1, source_target_pairs={{0,1},{1,2},{2,3},{3,4},{4,5},{5,6},{6,7},{7,8},{8,9},{9,10},{10,1... | collective-permute-start | bytes 1179656 | tf_op jit(solution)/shard_map/ppermute | solution.py:579
  5.3 12.5 %collective-permute-start.1 = (bf16[3,64,1024]{2,1,0:T(8,128)(2,1)S(1)}, bf16[3,64,1024]{2,1,0:T(8,128)(2,1)S(1)}, u32[]{:S(2)}, u32[]{:S(2)}) collective-permute-start(bf16[3,64,1024]{2,1,0:T(8,128)(2,1)S(1)} %get-tuple-element.37), channel_id=1, source_target_pairs={{0,15},{1,0},{2,1},{3,2},{4,3},{5,4},{6,5},{7,6},{8,7},{9,8},{10,9... | collective-permute-start | bytes 1179656 | tf_op jit(solution)/shard_map/ppermute | solution.py:579
  17.6 11.3 %copy-start.12 = (f32[8,3]{0,1:T(4,128)S(1)}, f32[8,3]{0,1:T(4,128)}, u32[]{:S(2)}) copy-start(f32[8,3]{0,1:T(4,128)} %param.16) | copy-start | bytes 292
  17.7 16.3 %copy-start.1 = (f32[8,64,1024]{2,1,0:T(8,128)S(1)}, f32[8,64,1024]{2,1,0:T(8,128)}, u32[]{:S(2)}) copy-start(f32[8,64,1024]{2,1,0:T(8,128)} %state_ref.1) | copy-start | bytes 6291460
  17.7 16.3 %copy-start.4 = (s32[128]{0:T(128)S(1)}, s32[128]{0:T(128)}, u32[]{:S(2)}) copy-start(s32[128]{0:T(128)} %label_ref.1) | copy-start | bytes 1540
  17.8 43.9 %all-to-all-start = ((bf16[128,72,128]{2,1,0:T(8,128)(2,1)}), bf16[128,72,128]{2,1,0:T(8,128)(2,1)}, u32[]{:S(2)}, u32[]{:S(2)}) async-start(bf16[128,72,128]{2,1,0:T(8,128)(2,1)} %pack.1), calls=%async_computation | async-start | bytes 4718592 | tf_op jit(solution)/shard_map/all_to_all | solution.py:662
  29.1 39.8 %collective-permute-start.2 = (bf16[1,64,1024]{2,1,0:T(8,128)(2,1)}, bf16[1,64,1024]{2,1,0:T(8,128)(2,1)S(1)}, u32[]{:S(2)}, u32[]{:S(2)}) collective-permute-start(bf16[1,64,1024]{2,1,0:T(8,128)(2,1)} %get-tuple-element.58), channel_id=1, source_target_pairs={{0,1},{1,2},{2,3},{3,4},{4,5},{5,6},{6,7},{7,8},{8,9},{9,10},{10,1... | collective-permute-start | bytes 393224 | tf_op jit(solution)/shard_map/ppermute | solution.py:579
  30.4 38.4 %collective-permute-start.3 = (bf16[1,64,1024]{2,1,0:T(8,128)(2,1)}, bf16[1,64,1024]{2,1,0:T(8,128)(2,1)S(1)}, u32[]{:S(2)}, u32[]{:S(2)}) collective-permute-start(bf16[1,64,1024]{2,1,0:T(8,128)(2,1)} %get-tuple-element.59), channel_id=1, source_target_pairs={{0,15},{1,0},{2,1},{3,2},{4,3},{5,4},{6,5},{7,6},{8,7},{9,8},{10,9... | collective-permute-start | bytes 393224 | tf_op jit(solution)/shard_map/ppermute | solution.py:579
  43.8 1.3 %copy-start.2 = (f32[4096,128]{1,0:T(8,128)}, f32[4096,128]{1,0:T(8,128)S(1)}, u32[]{:S(2)}) copy-start(f32[4096,128]{1,0:T(8,128)S(1)} %get-tuple-element.53.base_ref) | copy-start | bytes 6291460
  68.8 18.4 %copy-start.3 = (f32[4096,128]{1,0:T(8,128)S(1)}, f32[4096,128]{1,0:T(8,128)}, u32[]{:S(2)}) copy-start(f32[4096,128]{1,0:T(8,128)} %copy-done.2) | copy-start | bytes 6291460
  68.8 18.3 %collective-permute-start.4 = (bf16[12,8,16,128]{3,2,1,0:T(8,128)(2,1)S(1)}, bf16[12,8,16,128]{3,2,1,0:T(8,128)(2,1)S(1)}, u32[]{:S(2)}, u32[]{:S(2)}) collective-permute-start(bf16[12,8,16,128]{3,2,1,0:T(8,128)(2,1)S(1)} %get-tuple-element.62), channel_id=1, source_target_pairs={{0,1},{1,2},{2,3},{3,4},{4,5},{5,6},{6,7},{7,8},{8,9},{9,10},{10,1... | collective-permute-start | bytes 1179656 | tf_op jit(solution)/shard_map/ppermute | solution.py:579
  69.5 17.7 %collective-permute-start.5 = (bf16[12,8,16,128]{3,2,1,0:T(8,128)(2,1)S(1)}, bf16[12,8,16,128]{3,2,1,0:T(8,128)(2,1)S(1)}, u32[]{:S(2)}, u32[]{:S(2)}) collective-permute-start(bf16[12,8,16,128]{3,2,1,0:T(8,128)(2,1)S(1)} %get-tuple-element.63), channel_id=1, source_target_pairs={{0,15},{1,0},{2,1},{3,2},{4,3},{5,4},{6,5},{7,6},{8,7},{9,8},{10,9... | collective-permute-start | bytes 1179656 | tf_op jit(solution)/shard_map/ppermute | solution.py:579
  73.7 3.4 %collective-permute-start.6 = (bf16[8,8,8,128]{3,2,1,0:T(8,128)(2,1)S(1)}, bf16[8,8,8,128]{3,2,1,0:T(8,128)(2,1)S(1)}, u32[]{:S(2)}, u32[]{:S(2)}) collective-permute-start(bf16[8,8,8,128]{3,2,1,0:T(8,128)(2,1)S(1)} %get-tuple-element.64), channel_id=1, source_target_pairs={{0,16},{16,32},{32,48},{48,64},{64,80},{80,96},{96,112},{112,0},{1... | collective-permute-start | bytes 393224 | tf_op jit(solution)/shard_map/ppermute | solution.py:579
  75.1 4.7 %collective-permute-start.7 = (bf16[8,8,8,128]{3,2,1,0:T(8,128)(2,1)S(1)}, bf16[8,8,8,128]{3,2,1,0:T(8,128)(2,1)S(1)}, u32[]{:S(2)}, u32[]{:S(2)}) collective-permute-start(bf16[8,8,8,128]{3,2,1,0:T(8,128)(2,1)S(1)} %get-tuple-element.65), channel_id=1, source_target_pairs={{0,112},{16,0},{32,16},{48,32},{64,48},{80,64},{96,80},{112,96},{1... | collective-permute-start | bytes 393224 | tf_op jit(solution)/shard_map/ppermute | solution.py:579
  79.9 7.3 %collective-permute-start.8 = (bf16[3,8,16,128]{3,2,1,0:T(8,128)(2,1)S(1)}, bf16[3,8,16,128]{3,2,1,0:T(8,128)(2,1)S(1)}, u32[]{:S(2)}, u32[]{:S(2)}) collective-permute-start(bf16[3,8,16,128]{3,2,1,0:T(8,128)(2,1)S(1)} %get-tuple-element.66), channel_id=1, source_target_pairs={{0,1},{1,2},{2,3},{3,4},{4,5},{5,6},{6,7},{7,8},{8,9},{9,10},{10,1... | collective-permute-start | bytes 294920 | tf_op jit(solution)/shard_map/ppermute | solution.py:579
  80.0 7.2 %collective-permute-start.9 = (bf16[3,8,16,128]{3,2,1,0:T(8,128)(2,1)S(1)}, bf16[3,8,16,128]{3,2,1,0:T(8,128)(2,1)S(1)}, u32[]{:S(2)}, u32[]{:S(2)}) collective-permute-start(bf16[3,8,16,128]{3,2,1,0:T(8,128)(2,1)S(1)} %get-tuple-element.67), channel_id=1, source_target_pairs={{0,15},{1,0},{2,1},{3,2},{4,3},{5,4},{6,5},{7,6},{8,7},{9,8},{10,9... | collective-permute-start | bytes 294920 | tf_op jit(solution)/shard_map/ppermute | solution.py:579

commit v6 on v5

--- a/solution.py
+++ b/solution.py
@@ -705,17 +705,17 @@
     lower, upper, first, last, t_low, t_high = lax.optimization_barrier(
         (lower, upper, first, last, t_low, t_high)
     )
+    s_front = shift(last, "logic", 1)
+    s_back = shift(first, "logic", -1)
     s_low = shift(upper, "slab", 1)
     s_high = shift(lower, "slab", -1)
-    s_front = shift(last, "logic", 1)
-    s_back = shift(first, "logic", -1)
     to_high, to_low = pl.pallas_call(
         corner_kernel,
         out_shape=[shape((3, 8, 16, 128), BF16)] * 2,
         in_specs=vmem(2),
         out_specs=vmem(2),
         compiler_params=params(),
-        cost_estimate=cost(1_000_000, 1_000_000),
+        cost_estimate=cost(8_000_000_000, 1_000_000),
         name="corners",
     )(s_front, s_back)
     s_corner_low = shift(to_high, "slab", 1)

time: 114 us -> 112 us (0.982)
  waiting for transfers between devices: 21.6 us -> 18.4 us
  blocking collectives: 18.1 us -> 20.6 us
    ppermute x10, waiting for transfers between devices: 5.13 us -> 1.87 us  [shift(): lax.ppermute(value, axis, [(i, (i + by) % count) for i in range(count)])]
    all_to_all x1, blocking collectives: 18.1 us -> 20.6 us  [per_device(): lax.all_to_all(coarse, both, split_axis=0, concat_axis=0, tiled=True)]
  transfers between devices with their start and end apart: 11 -> 11, of which waited for: 5 -> 3; matrix products, arithmetic and copies ran while one was open for 0% -> 0% of each run, Pallas kernels for 24% -> 24%
where the time goes in v6:
time: 112 us
  Pallas kernels  34.4 us (31%)
  starting transfers between devices  32.4 us (29%)
  blocking collectives  20.6 us (18%)
  waiting for transfers between devices  18.4 us (16%)
  local copies, waits for them, and re-layouts  4.86 us (4%)
  between operations  1.52 us (1%)
    ppermute x10, starting transfers between devices, shift(): lax.ppermute(value, axis, [(i, (i + by) % count) for i in range(count)])  21.3 us
    all_to_all x1, blocking collectives, per_device(): lax.all_to_all(coarse, both, split_axis=0, concat_axis=0, tiled=True)  20.6 us
    all_to_all x1, waiting for transfers between devices, per_device(): got = lax.all_to_all(packed, both, split_axis=0, concat_axis=0, tiled=True)  16.5 us
    all_to_all x1, starting transfers between devices, per_device(): got = lax.all_to_all(packed, both, split_axis=0, concat_axis=0, tiled=True)  11.2 us
    pallas_call x1, Pallas kernels, per_device(): pl.pallas_call(temperature_kernel, out_shape=[shape((NZ * NY * 8, 128), F...  9.87 us
    pallas_call x1, Pallas kernels, per_device(): pl.pallas_call(pack_kernel, out_shape=pltpu.HBM((DEV, ROWS, 128), BF16),...  7.83 us
    pallas_call x1, Pallas kernels, per_device(): pl.pallas_call(scatter_kernel, out_shape=[shape((64, 8, 8, 128), F32), sh...  7.14 us
    pallas_call x1, Pallas kernels, per_device(): pl.pallas_call(outer_kernel, out_shape=[pltpu.HBM((NZ, 8, 64, 128), F32),...  6.38 us
  transfers between devices with their start and end apart: 11, of which 3 were waited for; matrix products, arithmetic and copies ran while one was open for 0% of the time, Pallas kernels for 24%

profile of v6, /device:TPU:1, one launch (start us, length us, event | category | flops | bytes accessed | tf_op | source)
XLA Modules:
  0.0 112.1 jit_solution(6839345757434419819)
XLA Ops:
  0.6 1.6 %copy-done = f32[8,64,1024]{2,1,0:T(8,128)S(1)} copy-done((f32[8,64,1024]{2,1,0:T(8,128)S(1)}, f32[8,64,1024]{2,1,0:T(8,128)}, u32[]{:S(2)}) %copy-start) | copy-done | bytes 2097176
  2.2 1.0 edges.1
  3.3 2.0 %collective-permute-start = (bf16[3,64,1024]{2,1,0:T(8,128)(2,1)S(1)}, bf16[3,64,1024]{2,1,0:T(8,128)(2,1)S(1)}, u32[]{:S(2)}, u32[]{:S(2)}) collective-permute-start(bf16[3,64,1024]{2,1,0:T(8,128)(2,1)S(1)} %get-tuple-element.36), channel_id=1, source_target_pairs={{0,1},{1,2},{2,3},{3,4},{4,5},{5,6},{6,7},{7,8},{8,9},{9,10},{10,1... | collective-permute-start | bytes 1179656 | tf_op jit(solution)/shard_map/ppermute | solution.py:579
  5.3 3.8 %collective-permute-start.1 = (bf16[3,64,1024]{2,1,0:T(8,128)(2,1)S(1)}, bf16[3,64,1024]{2,1,0:T(8,128)(2,1)S(1)}, u32[]{:S(2)}, u32[]{:S(2)}) collective-permute-start(bf16[3,64,1024]{2,1,0:T(8,128)(2,1)S(1)} %get-tuple-element.37), channel_id=1, source_target_pairs={{0,15},{1,0},{2,1},{3,2},{4,3},{5,4},{6,5},{7,6},{8,7},{9,8},{10,9... | collective-permute-start | bytes 1179656 | tf_op jit(solution)/shard_map/ppermute | solution.py:579
  9.8 7.8 %pack.1 = bf16[128,72,128]{2,1,0:T(8,128)(2,1)} custom-call(s32[1]{0:T(128)S(6)} %copy.30.count_ref, s32[1,2048]{1,0:T(1,128)S(1)} %bitcast.29, s32[1,2048]{1,0:T(1,128)S(1)} %bitcast.30, f32[1,2048]{1,0:T(1,128)S(1)} %bitcast.31, f32[128,128]{1,0:T(8,128)S(1)} %bitcast.28, bf16[2048,256]{1,0:T(8,128)(2,1)S(1)} %copy-done.5), custom_call_target="tpu_custom_call" | custom-call | flops 5000000000 | bytes 4000000 | tf_op jit(solution)/shard_map/pack/pallas_call | solution.py:626
  17.8 11.2 %all-to-all-start = ((bf16[128,72,128]{2,1,0:T(8,128)(2,1)}), bf16[128,72,128]{2,1,0:T(8,128)(2,1)}, u32[]{:S(2)}, u32[]{:S(2)}) async-start(bf16[128,72,128]{2,1,0:T(8,128)(2,1)} %pack.1), calls=%async_computation | async-start | bytes 4718592 | tf_op jit(solution)/shard_map/all_to_all | solution.py:662
  29.1 1.4 %collective-permute-start.2 = (bf16[1,64,1024]{2,1,0:T(8,128)(2,1)}, bf16[1,64,1024]{2,1,0:T(8,128)(2,1)S(1)}, u32[]{:S(2)}, u32[]{:S(2)}) collective-permute-start(bf16[1,64,1024]{2,1,0:T(8,128)(2,1)} %get-tuple-element.58), channel_id=1, source_target_pairs={{0,1},{1,2},{2,3},{3,4},{4,5},{5,6},{6,7},{7,8},{8,9},{9,10},{10,1... | collective-permute-start | bytes 393224 | tf_op jit(solution)/shard_map/ppermute | solution.py:579
  30.4 3.5 %collective-permute-start.3 = (bf16[1,64,1024]{2,1,0:T(8,128)(2,1)}, bf16[1,64,1024]{2,1,0:T(8,128)(2,1)S(1)}, u32[]{:S(2)}, u32[]{:S(2)}) collective-permute-start(bf16[1,64,1024]{2,1,0:T(8,128)(2,1)} %get-tuple-element.59), channel_id=1, source_target_pairs={{0,15},{1,0},{2,1},{3,2},{4,3},{5,4},{6,5},{7,6},{8,7},{9,8},{10,9... | collective-permute-start | bytes 393224 | tf_op jit(solution)/shard_map/ppermute | solution.py:579
  34.0 9.9 %diffuse_temperature.1 = (f32[4096,128]{1,0:T(8,128)S(1)}, f32[16,6,8,128]{3,2,1,0:T(8,128)S(1)}) custom-call(f32[8,3]{1,0:T(8,128)S(1)} %copy.20.table_ref, s32[128]{0:T(128)S(1)} %copy-done.4, f32[8,64,1024]{2,1,0:T(8,128)S(1)} %copy-done.1, bf16[3,64,1024]{2,1,0:T(8,128)(2,1)S(1)} %collective-permute-done.low_ref, ...), custom_call_target="tpu_custom_call" | custom-call | flops 100000000 | bytes 20000000 | tf_op jit(solution)/shard_map/diffuse_temperature/pallas_call | solution.py:664
  43.8 1.3 %copy-done.2 = f32[4096,128]{1,0:T(8,128)} copy-done((f32[4096,128]{1,0:T(8,128)}, f32[4096,128]{1,0:T(8,128)S(1)}, u32[]{:S(2)}) %copy-start.2) | copy-done | bytes 2097176
  45.2 16.5 %all-to-all-done.got_ref = bf16[128,72,128]{2,1,0:T(8,128)(2,1)} async-done(((bf16[128,72,128]{2,1,0:T(8,128)(2,1)}), bf16[128,72,128]{2,1,0:T(8,128)(2,1)}, u32[]{:S(2)}, u32[]{:S(2)}) %all-to-all-start) | async-done | bytes 2359328 | tf_op jit(solution)/shard_map/all_to_all | solution.py:662
  61.7 7.1 %place_tiles.1 = (f32[64,8,8,128]{3,2,1,0:T(8,128)S(1)}, bf16[12,8,16,128]{3,2,1,0:T(8,128)(2,1)S(1)}, bf16[12,8,16,128]{3,2,1,0:T(8,128)(2,1)S(1)}, bf16[8,8,8,...) custom-call(bf16[128,72,128]{2,1,0:T(8,128)(2,1)} %all-to-all-done.got_ref, bf16[8,8,8,128]{3,2,1,0:T(8,128)(2,1)} %bitcast.26, ...), custom_call_target="tpu_custom_call" | custom-call | flops 5000000000 | bytes 6000000 | tf_op jit(solution)/shard_map/place_tiles/pallas_call | solution.py:680
  68.8 0.9 collective-permute-start.6
  69.7 0.7 collective-permute-start.4
  70.4 4.1 %collective-permute-start.5 = (bf16[12,8,16,128]{3,2,1,0:T(8,128)(2,1)S(1)}, bf16[12,8,16,128]{3,2,1,0:T(8,128)(2,1)S(1)}, u32[]{:S(2)}, u32[]{:S(2)}) collective-permute-start(bf16[12,8,16,128]{3,2,1,0:T(8,128)(2,1)S(1)} %get-tuple-element.63), channel_id=1, source_target_pairs={{0,15},{1,0},{2,1},{3,2},{4,3},{5,4},{6,5},{7,6},{8,7},{9,8},{10,9... | collective-permute-start | bytes 1179656 | tf_op jit(solution)/shard_map/ppermute | solution.py:579
  74.6 0.6 collective-permute-start.8
  75.2 4.2 %collective-permute-start.9 = (bf16[3,8,16,128]{3,2,1,0:T(8,128)(2,1)S(1)}, bf16[3,8,16,128]{3,2,1,0:T(8,128)(2,1)S(1)}, u32[]{:S(2)}, u32[]{:S(2)}) collective-permute-start(bf16[3,8,16,128]{3,2,1,0:T(8,128)(2,1)S(1)} %get-tuple-element.67), channel_id=1, source_target_pairs={{0,15},{1,0},{2,1},{3,2},{4,3},{5,4},{6,5},{7,6},{8,7},{9,8},{10,9... | collective-permute-start | bytes 294920 | tf_op jit(solution)/shard_map/ppermute | solution.py:579
  79.4 2.1 %diffuse_inner.1 = (f32[8064,128]{1,0:T(8,128)S(1)}, f32[8064,128]{1,0:T(8,128)S(1)}, f32[8064,128]{1,0:T(8,128)S(1)}) custom-call(f32[16,6,8,128]{3,2,1,0:T(8,128)S(1)} %get-tuple-element.45.coef_ref, f32[4096,128]{1,0:T(8,128)S(1)} %bitcast.24), custom_call_target="tpu_custom_call" | custom-call | flops 20000000 | bytes 10000000 | tf_op jit(solution)/shard_map/diffuse_inner/pallas_call | solution.py:725
  81.5 1.7 %collective-permute-done.8.corner_low_ref = bf16[3,8,16,128]{3,2,1,0:T(8,128)(2,1)S(1)} collective-permute-done((bf16[3,8,16,128]{3,2,1,0:T(8,128)(2,1)S(1)}, bf16[3,8,16,128]{3,2,1,0:T(8,128)(2,1)S(1)}, u32[]{:S(2)}, u32[]{:S(2)}) %collective-permute-start.8) | collective-permute-done | bytes 98336 | tf_op jit(solution)/shard_map/ppermute | solution.py:579
  83.3 6.4 %diffuse_outer.1 = (f32[8,8,64,128]{3,2,1,0:T(8,128)}, f32[128,128]{1,0:T(8,128)S(1)}, f32[8064,128]{1,0:T(8,128)S(1)}, f32[8064,128]{1,0:T(8,128)S(1)}, f32[8064,128]{1,0:T(8,128)S(1)}) custom-call(f32[8064,128]{1,0:T(8,128)S(1)} %get-tuple-element.50._s, ...), custom_call_target="tpu_custom_call", output_to_operand_aliasing={{2}: (0, {}), {3}: (1, {}), {4}: (2, {})} | custom-call | flops 100000000 | bytes 20000000 | tf_op jit(solution)/shard_map/diffuse_outer/pallas_call | solution.py:734
  89.7 20.6 %all_to_all.14 = f32[128,1,128]{2,1,0:T(1,128)S(1)} all-to-all(f32[128,1,128]{2,1,0:T(1,128)S(1)} %bitcast.25), channel_id=1, replica_groups=mesh['logic'=8,'slab'=16] {'logic','slab'}, dimensions={0} | all-to-all | bytes 131072 | tf_op jit(solution)/shard_map/all_to_all | solution.py:755
  110.4 0.2 reshape.49
  110.6 0.4 copy.25
  111.0 1.1 reshape.51
  (37 shorter events, 0.4 us)
Async XLA Ops:
  0.6 1.6 %copy-start = (f32[8,64,1024]{2,1,0:T(8,128)S(1)}, f32[8,64,1024]{2,1,0:T(8,128)}, u32[]{:S(2)}) copy-start(f32[8,64,1024]{2,1,0:T(8,128)} %state_ref.1) | copy-start | bytes 6291460
  2.2 7.5 %copy-start.5 = (bf16[2048,256]{1,0:T(8,128)(2,1)S(1)}, bf16[2048,256]{1,0:T(8,128)(2,1)}, u32[]{:S(2)}) copy-start(bf16[2048,256]{1,0:T(8,128)(2,1)} %watt_hbm.1) | copy-start | bytes 3145732
  2.2 7.5 %copy-start.8 = (f32[128,32,4]{0,2,1:T(4,128)S(1)}, f32[128,32,4]{0,2,1:T(4,128)}, u32[]{:S(2)}) copy-start(f32[128,32,4]{0,2,1:T(4,128)} %param.15) | copy-start | bytes 196612
  2.2 7.5 %copy-start.9 = (s32[2048,1]{0,1:T(1,128)S(1)}, s32[2048,1]{0,1:T(1,128)}, u32[]{:S(2)}) copy-start(s32[2048,1]{0,1:T(1,128)} %param.12) | copy-start | bytes 24580
  2.2 7.5 %copy-start.10 = (s32[2048]{0:T(1024)S(1)}, s32[2048]{0:T(1024)}, u32[]{:S(2)}) copy-start(s32[2048]{0:T(1024)} %param.13) | copy-start | bytes 24580
  2.2 7.5 %copy-start.11 = (f32[2048]{0:T(1024)S(1)}, f32[2048]{0:T(1024)}, u32[]{:S(2)}) copy-start(f32[2048]{0:T(1024)} %param.11) | copy-start | bytes 24580
  3.3 14.4 %copy-start.6 = (bf16[2,4,8,8,128]{4,3,2,1,0:T(8,128)(2,1)}, bf16[2,4,8,8,128]{4,3,2,1,0:T(8,128)(2,1)S(1)}, u32[]{:S(2)}) copy-start(bf16[2,4,8,8,128]{4,3,2,1,0:T(8,128)(2,1)S(1)} %get-tuple-element.47) | copy-start | bytes 393220
  3.3 14.4 %copy-start.7 = (bf16[2,4,8,8,128]{4,3,2,1,0:T(8,128)(2,1)}, bf16[2,4,8,8,128]{4,3,2,1,0:T(8,128)(2,1)S(1)}, u32[]{:S(2)}) copy-start(bf16[2,4,8,8,128]{4,3,2,1,0:T(8,128)(2,1)S(1)} %get-tuple-element.48) | copy-start | bytes 393220
  3.3 14.5 %collective-permute-start = (bf16[3,64,1024]{2,1,0:T(8,128)(2,1)S(1)}, bf16[3,64,1024]{2,1,0:T(8,128)(2,1)S(1)}, u32[]{:S(2)}, u32[]{:S(2)}) collective-permute-start(bf16[3,64,1024]{2,1,0:T(8,128)(2,1)S(1)} %get-tuple-element.36), channel_id=1, source_target_pairs={{0,1},{1,2},{2,3},{3,4},{4,5},{5,6},{6,7},{7,8},{8,9},{9,10},{10,1... | collective-permute-start | bytes 1179656 | tf_op jit(solution)/shard_map/ppermute | solution.py:579
  5.3 12.5 %collective-permute-start.1 = (bf16[3,64,1024]{2,1,0:T(8,128)(2,1)S(1)}, bf16[3,64,1024]{2,1,0:T(8,128)(2,1)S(1)}, u32[]{:S(2)}, u32[]{:S(2)}) collective-permute-start(bf16[3,64,1024]{2,1,0:T(8,128)(2,1)S(1)} %get-tuple-element.37), channel_id=1, source_target_pairs={{0,15},{1,0},{2,1},{3,2},{4,3},{5,4},{6,5},{7,6},{8,7},{9,8},{10,9... | collective-permute-start | bytes 1179656 | tf_op jit(solution)/shard_map/ppermute | solution.py:579
  17.6 11.3 %copy-start.12 = (f32[8,3]{0,1:T(4,128)S(1)}, f32[8,3]{0,1:T(4,128)}, u32[]{:S(2)}) copy-start(f32[8,3]{0,1:T(4,128)} %param.16) | copy-start | bytes 292
  17.7 16.3 %copy-start.1 = (f32[8,64,1024]{2,1,0:T(8,128)S(1)}, f32[8,64,1024]{2,1,0:T(8,128)}, u32[]{:S(2)}) copy-start(f32[8,64,1024]{2,1,0:T(8,128)} %state_ref.1) | copy-start | bytes 6291460
  17.7 16.3 %copy-start.4 = (s32[128]{0:T(128)S(1)}, s32[128]{0:T(128)}, u32[]{:S(2)}) copy-start(s32[128]{0:T(128)} %label_ref.1) | copy-start | bytes 1540
  17.8 43.9 %all-to-all-start = ((bf16[128,72,128]{2,1,0:T(8,128)(2,1)}), bf16[128,72,128]{2,1,0:T(8,128)(2,1)}, u32[]{:S(2)}, u32[]{:S(2)}) async-start(bf16[128,72,128]{2,1,0:T(8,128)(2,1)} %pack.1), calls=%async_computation | async-start | bytes 4718592 | tf_op jit(solution)/shard_map/all_to_all | solution.py:662
  29.1 39.8 %collective-permute-start.2 = (bf16[1,64,1024]{2,1,0:T(8,128)(2,1)}, bf16[1,64,1024]{2,1,0:T(8,128)(2,1)S(1)}, u32[]{:S(2)}, u32[]{:S(2)}) collective-permute-start(bf16[1,64,1024]{2,1,0:T(8,128)(2,1)} %get-tuple-element.58), channel_id=1, source_target_pairs={{0,1},{1,2},{2,3},{3,4},{4,5},{5,6},{6,7},{7,8},{8,9},{9,10},{10,1... | collective-permute-start | bytes 393224 | tf_op jit(solution)/shard_map/ppermute | solution.py:579
  30.4 38.4 %collective-permute-start.3 = (bf16[1,64,1024]{2,1,0:T(8,128)(2,1)}, bf16[1,64,1024]{2,1,0:T(8,128)(2,1)S(1)}, u32[]{:S(2)}, u32[]{:S(2)}) collective-permute-start(bf16[1,64,1024]{2,1,0:T(8,128)(2,1)} %get-tuple-element.59), channel_id=1, source_target_pairs={{0,15},{1,0},{2,1},{3,2},{4,3},{5,4},{6,5},{7,6},{8,7},{9,8},{10,9... | collective-permute-start | bytes 393224 | tf_op jit(solution)/shard_map/ppermute | solution.py:579
  43.8 1.3 %copy-start.2 = (f32[4096,128]{1,0:T(8,128)}, f32[4096,128]{1,0:T(8,128)S(1)}, u32[]{:S(2)}) copy-start(f32[4096,128]{1,0:T(8,128)S(1)} %get-tuple-element.53.base_ref) | copy-start | bytes 6291460
  68.8 14.5 %copy-start.3 = (f32[4096,128]{1,0:T(8,128)S(1)}, f32[4096,128]{1,0:T(8,128)}, u32[]{:S(2)}) copy-start(f32[4096,128]{1,0:T(8,128)} %copy-done.2) | copy-start | bytes 6291460
  68.8 5.7 %collective-permute-start.6 = (bf16[8,8,8,128]{3,2,1,0:T(8,128)(2,1)S(1)}, bf16[8,8,8,128]{3,2,1,0:T(8,128)(2,1)S(1)}, u32[]{:S(2)}, u32[]{:S(2)}) collective-permute-start(bf16[8,8,8,128]{3,2,1,0:T(8,128)(2,1)S(1)} %get-tuple-element.64), channel_id=1, source_target_pairs={{0,16},{16,32},{32,48},{48,64},{64,80},{80,96},{96,112},{112,0},{1... | collective-permute-start | bytes 393224 | tf_op jit(solution)/shard_map/ppermute | solution.py:579
  69.7 4.8 %collective-permute-start.7 = (bf16[8,8,8,128]{3,2,1,0:T(8,128)(2,1)S(1)}, bf16[8,8,8,128]{3,2,1,0:T(8,128)(2,1)S(1)}, u32[]{:S(2)}, u32[]{:S(2)}) collective-permute-start(bf16[8,8,8,128]{3,2,1,0:T(8,128)(2,1)S(1)} %get-tuple-element.65), channel_id=1, source_target_pairs={{0,112},{16,0},{32,16},{48,32},{64,48},{80,64},{96,80},{112,96},{1... | collective-permute-start | bytes 393224 | tf_op jit(solution)/shard_map/ppermute | solution.py:579
  69.7 13.5 %collective-permute-start.4 = (bf16[12,8,16,128]{3,2,1,0:T(8,128)(2,1)S(1)}, bf16[12,8,16,128]{3,2,1,0:T(8,128)(2,1)S(1)}, u32[]{:S(2)}, u32[]{:S(2)}) collective-permute-start(bf16[12,8,16,128]{3,2,1,0:T(8,128)(2,1)S(1)} %get-tuple-element.62), channel_id=1, source_target_pairs={{0,1},{1,2},{2,3},{3,4},{4,5},{5,6},{6,7},{7,8},{8,9},{9,10},{10,1... | collective-permute-start | bytes 1179656 | tf_op jit(solution)/shard_map/ppermute | solution.py:579
  70.4 12.9 %collective-permute-start.5 = (bf16[12,8,16,128]{3,2,1,0:T(8,128)(2,1)S(1)}, bf16[12,8,16,128]{3,2,1,0:T(8,128)(2,1)S(1)}, u32[]{:S(2)}, u32[]{:S(2)}) collective-permute-start(bf16[12,8,16,128]{3,2,1,0:T(8,128)(2,1)S(1)} %get-tuple-element.63), channel_id=1, source_target_pairs={{0,15},{1,0},{2,1},{3,2},{4,3},{5,4},{6,5},{7,6},{8,7},{9,8},{10,9... | collective-permute-start | bytes 1179656 | tf_op jit(solution)/shard_map/ppermute | solution.py:579
  74.6 8.7 %collective-permute-start.8 = (bf16[3,8,16,128]{3,2,1,0:T(8,128)(2,1)S(1)}, bf16[3,8,16,128]{3,2,1,0:T(8,128)(2,1)S(1)}, u32[]{:S(2)}, u32[]{:S(2)}) collective-permute-start(bf16[3,8,16,128]{3,2,1,0:T(8,128)(2,1)S(1)} %get-tuple-element.66), channel_id=1, source_target_pairs={{0,1},{1,2},{2,3},{3,4},{4,5},{5,6},{6,7},{7,8},{8,9},{9,10},{10,1... | collective-permute-start | bytes 294920 | tf_op jit(solution)/shard_map/ppermute | solution.py:579
  75.2 8.1 %collective-permute-start.9 = (bf16[3,8,16,128]{3,2,1,0:T(8,128)(2,1)S(1)}, bf16[3,8,16,128]{3,2,1,0:T(8,128)(2,1)S(1)}, u32[]{:S(2)}, u32[]{:S(2)}) collective-permute-start(bf16[3,8,16,128]{3,2,1,0:T(8,128)(2,1)S(1)} %get-tuple-element.67), channel_id=1, source_target_pairs={{0,15},{1,0},{2,1},{3,2},{4,3},{5,4},{6,5},{7,6},{8,7},{9,8},{10,9... | collective-permute-start | bytes 294920 | tf_op jit(solution)/shard_map/ppermute | solution.py:579

commit v7 on v6

--- a/solution.py
+++ b/solution.py
@@ -30,22 +30,17 @@
     return lax.broadcasted_iota(I32, shape, dim)
 
 
-def edge_kernel(
-    lower_ref, upper_ref, to_high_ref, to_low_ref, far_high_ref, far_low_ref, first_ref, last_ref
-):
+def edge_kernel(lower_ref, upper_ref, to_high_ref, to_low_ref):
+    to_low_ref[...] = lower_ref[...].astype(BF16)
+    to_high_ref[...] = upper_ref[...].astype(BF16)
+
+
+def far_kernel(lower_ref, upper_ref, far_high_ref, far_low_ref, first_ref, last_ref):
     step = pl.program_id(0)
-
-    @pl.when(step < 3)
-    def _():
-        to_low_ref[...] = lower_ref[...].astype(BF16)
 
     @pl.when(step == 3)
     def _():
         far_low_ref[...] = lower_ref[...].astype(BF16)
-
-    @pl.when(step > 0)
-    def _():
-        to_high_ref[...] = upper_ref[...].astype(BF16)
 
     @pl.when(step == 0)
     def _():
@@ -280,7 +275,7 @@
         return 0
 
     count = layers[1] - layers[0]
-    unroll = 2 if count % 2 == 0 else 3 if count % 3 == 0 else 1
+    unroll = 4 if count % 4 == 0 else 2 if count % 2 == 0 else 3 if count % 3 == 0 else 1
     lax.fori_loop(layers[0], layers[1], layer, 0, unroll=unroll)
 
 
@@ -593,12 +588,25 @@
     state = initial_heat_state
     both = ("logic", "slab")
     shape = jax.ShapeDtypeStruct
-    to_high, to_low, far_high, far_low, t_first, t_last = pl.pallas_call(
+    to_high, to_low = pl.pallas_call(
         edge_kernel,
+        grid=(3,),
+        out_shape=[shape((3, NY, 1024), BF16)] * 2,
+        in_specs=[
+            pl.BlockSpec((1, NY, 1024), lambda i: (i, 0, 0)),
+            pl.BlockSpec((1, NY, 1024), lambda i: (i + 5, 0, 0)),
+        ],
+        out_specs=[pl.BlockSpec((1, NY, 1024), lambda i: (i, 0, 0))] * 2,
+        compiler_params=params(),
+        cost_estimate=cost(1_000_000, 3_000_000),
+        name="edges",
+    )(state, state)
+    low = shift(to_high, "slab", 1)
+    high = shift(to_low, "slab", -1)
+    far_high, far_low, t_first, t_last = pl.pallas_call(
+        far_kernel,
         grid=(NZ // 2,),
         out_shape=[
-            shape((3, NY, 1024), BF16),
-            shape((3, NY, 1024), BF16),
             shape((1, NY, 1024), BF16),
             shape((1, NY, 1024), BF16),
             shape((2, 4, 8, 8, 128), BF16),
@@ -609,8 +617,6 @@
             pl.BlockSpec((1, NY, 1024), lambda i: (i + NZ // 2, 0, 0)),
         ],
         out_specs=[
-            pl.BlockSpec((1, NY, 1024), lambda i: (jnp.maximum(i - 1, 0), 0, 0)),
-            pl.BlockSpec((1, NY, 1024), lambda i: (jnp.minimum(i, 2), 0, 0)),
             pl.BlockSpec((1, NY, 1024), lambda i: (0, 0, 0)),
             pl.BlockSpec((1, NY, 1024), lambda i: (0, 0, 0)),
             pl.BlockSpec((2, 1, 8, 8, 128), lambda i: (0, i, 0, 0, 0)),
@@ -618,10 +624,8 @@
         ],
         compiler_params=params(),
         cost_estimate=cost(1_000_000, 5_000_000),
-        name="edges",
+        name="far_edges",
     )(state, state)
-    low = shift(to_high, "slab", 1)
-    high = shift(to_low, "slab", -1)
 
     packed = pl.pallas_call(
         pack_kernel,
@@ -654,9 +658,7 @@
         prior_reduced_heat_map.transpose(1, 2, 0).reshape(128, LAYERS),
         dynamic_wattage,
     )
-    packed, low, high, far_high, far_low = lax.optimization_barrier(
-        (packed, low, high, far_high, far_low)
-    )
+    packed, low, high = lax.optimization_barrier((packed, low, high))
     t_low = shift(far_high, "slab", 1)
     t_high = shift(far_low, "slab", -1)
     got = lax.all_to_all(packed, both, split_axis=0, concat_axis=0, tiled=True)

time: 112 us -> 111 us (level)
  waiting for transfers between devices: 18.4 us -> 16.7 us
  local copies, waits for them, and re-layouts: 4.86 us -> 6.16 us
    all_to_all x1, waiting for transfers between devices: 16.5 us -> 14.7 us  [per_device(): got = lax.all_to_all(packed, both, split_axis=0, concat_axis=0, tiled=True)]
    unnamed x29, local copies, waits for them, and re-layouts: 4.58 us -> 5.89 us
  transfers between devices with their start and end apart: 11 -> 11, of which waited for: 3 -> 3; matrix products, arithmetic and copies ran while one was open for 0% -> 0% of each run, Pallas kernels for 24% -> 25%
where the time goes in v7:
time: 111 us
  Pallas kernels  33.7 us (30%)
  starting transfers between devices  32.4 us (29%)
  blocking collectives  20.6 us (19%)
  waiting for transfers between devices  16.7 us (15%)
  local copies, waits for them, and re-layouts  6.16 us (6%)
  between operations  1.51 us (1%)
    ppermute x10, starting transfers between devices, shift(): lax.ppermute(value, axis, [(i, (i + by) % count) for i in range(count)])  21.3 us
    all_to_all x1, blocking collectives, per_device(): lax.all_to_all(coarse, both, split_axis=0, concat_axis=0, tiled=True)  20.6 us
    all_to_all x1, waiting for transfers between devices, per_device(): got = lax.all_to_all(packed, both, split_axis=0, concat_axis=0, tiled=True)  14.7 us
    all_to_all x1, starting transfers between devices, per_device(): got = lax.all_to_all(packed, both, split_axis=0, concat_axis=0, tiled=True)  11.2 us
    pallas_call x1, Pallas kernels, per_device(): pl.pallas_call(temperature_kernel, out_shape=[shape((NZ * NY * 8, 128), F...  9.5 us
    pallas_call x1, Pallas kernels, per_device(): pl.pallas_call(pack_kernel, out_shape=pltpu.HBM((DEV, ROWS, 128), BF16),...  7.81 us
    pallas_call x1, Pallas kernels, per_device(): pl.pallas_call(scatter_kernel, out_shape=[shape((64, 8, 8, 128), F32), sh...  7.14 us
    pallas_call x1, Pallas kernels, per_device(): pl.pallas_call(outer_kernel, out_shape=[pltpu.HBM((NZ, 8, 64, 128), F32),...  6.11 us
  transfers between devices with their start and end apart: 11, of which 3 were waited for; matrix products, arithmetic and copies ran while one was open for 0% of the time, Pallas kernels for 25%

profile of v7, /device:TPU:1, one launch (start us, length us, event | category | flops | bytes accessed | tf_op | source)
XLA Modules:
  0.0 111.1 jit_solution(5683636644089659327)
XLA Ops:
  0.6 1.6 %copy-done = f32[8,64,1024]{2,1,0:T(8,128)S(1)} copy-done((f32[8,64,1024]{2,1,0:T(8,128)S(1)}, f32[8,64,1024]{2,1,0:T(8,128)}, u32[]{:S(2)}) %copy-start) | copy-done | bytes 2097176
  2.4 2.1 %collective-permute-start = (bf16[3,64,1024]{2,1,0:T(8,128)(2,1)S(1)}, bf16[3,64,1024]{2,1,0:T(8,128)(2,1)S(1)}, u32[]{:S(2)}, u32[]{:S(2)}) collective-permute-start(bf16[3,64,1024]{2,1,0:T(8,128)(2,1)S(1)} %get-tuple-element.34), channel_id=1, source_target_pairs={{0,1},{1,2},{2,3},{3,4},{4,5},{5,6},{6,7},{7,8},{8,9},{9,10},{10,1... | collective-permute-start | bytes 1179656 | tf_op jit(solution)/shard_map/ppermute | solution.py:574
  4.5 3.8 %collective-permute-start.1 = (bf16[3,64,1024]{2,1,0:T(8,128)(2,1)S(1)}, bf16[3,64,1024]{2,1,0:T(8,128)(2,1)S(1)}, u32[]{:S(2)}, u32[]{:S(2)}) collective-permute-start(bf16[3,64,1024]{2,1,0:T(8,128)(2,1)S(1)} %get-tuple-element.35), channel_id=1, source_target_pairs={{0,15},{1,0},{2,1},{3,2},{4,3},{5,4},{6,5},{7,6},{8,7},{9,8},{10,9... | collective-permute-start | bytes 1179656 | tf_op jit(solution)/shard_map/ppermute | solution.py:574
  9.0 7.8 %pack.1 = bf16[128,72,128]{2,1,0:T(8,128)(2,1)} custom-call(s32[1]{0:T(128)S(6)} %copy.30.count_ref, s32[1,2048]{1,0:T(1,128)S(1)} %bitcast.29, s32[1,2048]{1,0:T(1,128)S(1)} %bitcast.30, f32[1,2048]{1,0:T(1,128)S(1)} %bitcast.31, f32[128,128]{1,0:T(8,128)S(1)} %bitcast.28, bf16[2048,256]{1,0:T(8,128)(2,1)S(1)} %copy-done.5), custom_call_target="tpu_custom_call" | custom-call | flops 5000000000 | bytes 4000000 | tf_op jit(solution)/shard_map/pack/pallas_call | solution.py:630
  17.0 11.2 %all-to-all-start = ((bf16[128,72,128]{2,1,0:T(8,128)(2,1)}), bf16[128,72,128]{2,1,0:T(8,128)(2,1)}, u32[]{:S(2)}, u32[]{:S(2)}) async-start(bf16[128,72,128]{2,1,0:T(8,128)(2,1)} %pack.1), calls=%async_computation | async-start | bytes 4718592 | tf_op jit(solution)/shard_map/all_to_all | solution.py:664
  28.2 0.9 far_edges.1
  29.1 0.7 copy-done.6
  29.8 0.6 copy-done.7
  30.4 1.4 %collective-permute-start.2 = (bf16[1,64,1024]{2,1,0:T(8,128)(2,1)}, bf16[1,64,1024]{2,1,0:T(8,128)(2,1)S(1)}, u32[]{:S(2)}, u32[]{:S(2)}) collective-permute-start(bf16[1,64,1024]{2,1,0:T(8,128)(2,1)} %get-tuple-element.54), channel_id=1, source_target_pairs={{0,1},{1,2},{2,3},{3,4},{4,5},{5,6},{6,7},{7,8},{8,9},{9,10},{10,1... | collective-permute-start | bytes 393224 | tf_op jit(solution)/shard_map/ppermute | solution.py:574
  31.8 3.4 %collective-permute-start.3 = (bf16[1,64,1024]{2,1,0:T(8,128)(2,1)}, bf16[1,64,1024]{2,1,0:T(8,128)(2,1)S(1)}, u32[]{:S(2)}, u32[]{:S(2)}) collective-permute-start(bf16[1,64,1024]{2,1,0:T(8,128)(2,1)} %get-tuple-element.55), channel_id=1, source_target_pairs={{0,15},{1,0},{2,1},{3,2},{4,3},{5,4},{6,5},{7,6},{8,7},{9,8},{10,9... | collective-permute-start | bytes 393224 | tf_op jit(solution)/shard_map/ppermute | solution.py:574
  35.3 9.5 %diffuse_temperature.1 = (f32[4096,128]{1,0:T(8,128)S(1)}, f32[16,6,8,128]{3,2,1,0:T(8,128)S(1)}) custom-call(f32[8,3]{1,0:T(8,128)S(1)} %copy.20.table_ref, s32[128]{0:T(128)S(1)} %copy-done.4, f32[8,64,1024]{2,1,0:T(8,128)S(1)} %copy-done.1, bf16[3,64,1024]{2,1,0:T(8,128)(2,1)S(1)} %collective-permute-done.low_ref, ...), custom_call_target="tpu_custom_call" | custom-call | flops 100000000 | bytes 20000000 | tf_op jit(solution)/shard_map/diffuse_temperature/pallas_call | solution.py:666
  44.8 1.3 %copy-done.2 = f32[4096,128]{1,0:T(8,128)} copy-done((f32[4096,128]{1,0:T(8,128)}, f32[4096,128]{1,0:T(8,128)S(1)}, u32[]{:S(2)}) %copy-start.2) | copy-done | bytes 2097176
  46.1 14.7 %all-to-all-done.got_ref = bf16[128,72,128]{2,1,0:T(8,128)(2,1)} async-done(((bf16[128,72,128]{2,1,0:T(8,128)(2,1)}), bf16[128,72,128]{2,1,0:T(8,128)(2,1)}, u32[]{:S(2)}, u32[]{:S(2)}) %all-to-all-start) | async-done | bytes 2359328 | tf_op jit(solution)/shard_map/all_to_all | solution.py:664
  60.9 7.1 %place_tiles.1 = (f32[64,8,8,128]{3,2,1,0:T(8,128)S(1)}, bf16[12,8,16,128]{3,2,1,0:T(8,128)(2,1)S(1)}, bf16[12,8,16,128]{3,2,1,0:T(8,128)(2,1)S(1)}, bf16[8,8,8,...) custom-call(bf16[128,72,128]{2,1,0:T(8,128)(2,1)} %all-to-all-done.got_ref, bf16[8,8,8,128]{3,2,1,0:T(8,128)(2,1)} %bitcast.26, ...), custom_call_target="tpu_custom_call" | custom-call | flops 5000000000 | bytes 6000000 | tf_op jit(solution)/shard_map/place_tiles/pallas_call | solution.py:682
  68.1 0.9 collective-permute-start.6
  69.0 0.7 collective-permute-start.4
  69.6 4.1 %collective-permute-start.5 = (bf16[12,8,16,128]{3,2,1,0:T(8,128)(2,1)S(1)}, bf16[12,8,16,128]{3,2,1,0:T(8,128)(2,1)S(1)}, u32[]{:S(2)}, u32[]{:S(2)}) collective-permute-start(bf16[12,8,16,128]{3,2,1,0:T(8,128)(2,1)S(1)} %get-tuple-element.59), channel_id=1, source_target_pairs={{0,15},{1,0},{2,1},{3,2},{4,3},{5,4},{6,5},{7,6},{8,7},{9,8},{10,9... | collective-permute-start | bytes 1179656 | tf_op jit(solution)/shard_map/ppermute | solution.py:574
  73.8 0.6 collective-permute-start.8
  74.4 4.2 %collective-permute-start.9 = (bf16[3,8,16,128]{3,2,1,0:T(8,128)(2,1)S(1)}, bf16[3,8,16,128]{3,2,1,0:T(8,128)(2,1)S(1)}, u32[]{:S(2)}, u32[]{:S(2)}) collective-permute-start(bf16[3,8,16,128]{3,2,1,0:T(8,128)(2,1)S(1)} %get-tuple-element.63), channel_id=1, source_target_pairs={{0,15},{1,0},{2,1},{3,2},{4,3},{5,4},{6,5},{7,6},{8,7},{9,8},{10,9... | collective-permute-start | bytes 294920 | tf_op jit(solution)/shard_map/ppermute | solution.py:574
  78.7 2.0 %diffuse_inner.1 = (f32[8064,128]{1,0:T(8,128)S(1)}, f32[8064,128]{1,0:T(8,128)S(1)}, f32[8064,128]{1,0:T(8,128)S(1)}) custom-call(f32[16,6,8,128]{3,2,1,0:T(8,128)S(1)} %get-tuple-element.41.coef_ref, f32[4096,128]{1,0:T(8,128)S(1)} %bitcast.24), custom_call_target="tpu_custom_call" | custom-call | flops 20000000 | bytes 10000000 | tf_op jit(solution)/shard_map/diffuse_inner/pallas_call | solution.py:727
  80.7 1.8 %collective-permute-done.8.corner_low_ref = bf16[3,8,16,128]{3,2,1,0:T(8,128)(2,1)S(1)} collective-permute-done((bf16[3,8,16,128]{3,2,1,0:T(8,128)(2,1)S(1)}, bf16[3,8,16,128]{3,2,1,0:T(8,128)(2,1)S(1)}, u32[]{:S(2)}, u32[]{:S(2)}) %collective-permute-start.8) | collective-permute-done | bytes 98336 | tf_op jit(solution)/shard_map/ppermute | solution.py:574
  82.5 6.1 %diffuse_outer.1 = (f32[8,8,64,128]{3,2,1,0:T(8,128)}, f32[128,128]{1,0:T(8,128)S(1)}, f32[8064,128]{1,0:T(8,128)S(1)}, f32[8064,128]{1,0:T(8,128)S(1)}, f32[8064,128]{1,0:T(8,128)S(1)}) custom-call(f32[8064,128]{1,0:T(8,128)S(1)} %get-tuple-element.46._s, ...), custom_call_target="tpu_custom_call", output_to_operand_aliasing={{2}: (0, {}), {3}: (1, {}), {4}: (2, {})} | custom-call | flops 100000000 | bytes 20000000 | tf_op jit(solution)/shard_map/diffuse_outer/pallas_call | solution.py:736
  88.6 20.6 %all_to_all.14 = f32[128,1,128]{2,1,0:T(1,128)S(1)} all-to-all(f32[128,1,128]{2,1,0:T(1,128)S(1)} %bitcast.25), channel_id=1, replica_groups=mesh['logic'=8,'slab'=16] {'logic','slab'}, dimensions={0} | all-to-all | bytes 131072 | tf_op jit(solution)/shard_map/all_to_all | solution.py:757
  109.9 1.1 %reshape.51 = f32[128,32,4]{0,2,1:T(4,128)} reshape(f32[16,8,8,4,4]{1,0,4,3,2:T(8,128)S(1)} %copy.25) | data formatting | bytes 131072
  (38 shorter events, 1.2 us)
Async XLA Ops:
  0.6 1.6 %copy-start = (f32[8,64,1024]{2,1,0:T(8,128)S(1)}, f32[8,64,1024]{2,1,0:T(8,128)}, u32[]{:S(2)}) copy-start(f32[8,64,1024]{2,1,0:T(8,128)} %upper_ref.3) | copy-start | bytes 6291460
  2.2 6.7 %copy-start.5 = (bf16[2048,256]{1,0:T(8,128)(2,1)S(1)}, bf16[2048,256]{1,0:T(8,128)(2,1)}, u32[]{:S(2)}) copy-start(bf16[2048,256]{1,0:T(8,128)(2,1)} %watt_hbm.1) | copy-start | bytes 3145732
  2.2 6.7 %copy-start.8 = (f32[128,32,4]{0,2,1:T(4,128)S(1)}, f32[128,32,4]{0,2,1:T(4,128)}, u32[]{:S(2)}) copy-start(f32[128,32,4]{0,2,1:T(4,128)} %param.15) | copy-start | bytes 196612
  2.2 6.7 %copy-start.9 = (s32[2048,1]{0,1:T(1,128)S(1)}, s32[2048,1]{0,1:T(1,128)}, u32[]{:S(2)}) copy-start(s32[2048,1]{0,1:T(1,128)} %param.12) | copy-start | bytes 24580
  2.2 6.8 %copy-start.10 = (s32[2048]{0:T(1024)S(1)}, s32[2048]{0:T(1024)}, u32[]{:S(2)}) copy-start(s32[2048]{0:T(1024)} %param.13) | copy-start | bytes 24580
  2.2 6.8 %copy-start.11 = (f32[2048]{0:T(1024)S(1)}, f32[2048]{0:T(1024)}, u32[]{:S(2)}) copy-start(f32[2048]{0:T(1024)} %param.11) | copy-start | bytes 24580
  2.4 14.6 %collective-permute-start = (bf16[3,64,1024]{2,1,0:T(8,128)(2,1)S(1)}, bf16[3,64,1024]{2,1,0:T(8,128)(2,1)S(1)}, u32[]{:S(2)}, u32[]{:S(2)}) collective-permute-start(bf16[3,64,1024]{2,1,0:T(8,128)(2,1)S(1)} %get-tuple-element.34), channel_id=1, source_target_pairs={{0,1},{1,2},{2,3},{3,4},{4,5},{5,6},{6,7},{7,8},{8,9},{9,10},{10,1... | collective-permute-start | bytes 1179656 | tf_op jit(solution)/shard_map/ppermute | solution.py:574
  4.5 12.5 %collective-permute-start.1 = (bf16[3,64,1024]{2,1,0:T(8,128)(2,1)S(1)}, bf16[3,64,1024]{2,1,0:T(8,128)(2,1)S(1)}, u32[]{:S(2)}, u32[]{:S(2)}) collective-permute-start(bf16[3,64,1024]{2,1,0:T(8,128)(2,1)S(1)} %get-tuple-element.35), channel_id=1, source_target_pairs={{0,15},{1,0},{2,1},{3,2},{4,3},{5,4},{6,5},{7,6},{8,7},{9,8},{10,9... | collective-permute-start | bytes 1179656 | tf_op jit(solution)/shard_map/ppermute | solution.py:574
  16.8 11.4 %copy-start.1 = (f32[8,64,1024]{2,1,0:T(8,128)S(1)}, f32[8,64,1024]{2,1,0:T(8,128)}, u32[]{:S(2)}) copy-start(f32[8,64,1024]{2,1,0:T(8,128)} %upper_ref.3) | copy-start | bytes 6291460
  16.8 18.4 %copy-start.12 = (f32[8,3]{0,1:T(4,128)S(1)}, f32[8,3]{0,1:T(4,128)}, u32[]{:S(2)}) copy-start(f32[8,3]{0,1:T(4,128)} %param.16) | copy-start | bytes 292
  16.9 18.5 %copy-start.4 = (s32[128]{0:T(128)S(1)}, s32[128]{0:T(128)}, u32[]{:S(2)}) copy-start(s32[128]{0:T(128)} %label_ref.1) | copy-start | bytes 1540
  17.0 43.9 %all-to-all-start = ((bf16[128,72,128]{2,1,0:T(8,128)(2,1)}), bf16[128,72,128]{2,1,0:T(8,128)(2,1)}, u32[]{:S(2)}, u32[]{:S(2)}) async-start(bf16[128,72,128]{2,1,0:T(8,128)(2,1)} %pack.1), calls=%async_computation | async-start | bytes 4718592 | tf_op jit(solution)/shard_map/all_to_all | solution.py:664
  29.1 0.7 copy-start.6
  29.8 0.7 copy-start.7
  30.4 37.6 %collective-permute-start.2 = (bf16[1,64,1024]{2,1,0:T(8,128)(2,1)}, bf16[1,64,1024]{2,1,0:T(8,128)(2,1)S(1)}, u32[]{:S(2)}, u32[]{:S(2)}) collective-permute-start(bf16[1,64,1024]{2,1,0:T(8,128)(2,1)} %get-tuple-element.54), channel_id=1, source_target_pairs={{0,1},{1,2},{2,3},{3,4},{4,5},{5,6},{6,7},{7,8},{8,9},{9,10},{10,1... | collective-permute-start | bytes 393224 | tf_op jit(solution)/shard_map/ppermute | solution.py:574
  31.8 36.2 %collective-permute-start.3 = (bf16[1,64,1024]{2,1,0:T(8,128)(2,1)}, bf16[1,64,1024]{2,1,0:T(8,128)(2,1)S(1)}, u32[]{:S(2)}, u32[]{:S(2)}) collective-permute-start(bf16[1,64,1024]{2,1,0:T(8,128)(2,1)} %get-tuple-element.55), channel_id=1, source_target_pairs={{0,15},{1,0},{2,1},{3,2},{4,3},{5,4},{6,5},{7,6},{8,7},{9,8},{10,9... | collective-permute-start | bytes 393224 | tf_op jit(solution)/shard_map/ppermute | solution.py:574
  44.8 1.3 %copy-start.2 = (f32[4096,128]{1,0:T(8,128)}, f32[4096,128]{1,0:T(8,128)S(1)}, u32[]{:S(2)}) copy-start(f32[4096,128]{1,0:T(8,128)S(1)} %get-tuple-element.49.base_ref) | copy-start | bytes 6291460
  68.0 14.5 %copy-start.3 = (f32[4096,128]{1,0:T(8,128)S(1)}, f32[4096,128]{1,0:T(8,128)}, u32[]{:S(2)}) copy-start(f32[4096,128]{1,0:T(8,128)} %copy-done.2) | copy-start | bytes 6291460
  68.1 5.7 %collective-permute-start.6 = (bf16[8,8,8,128]{3,2,1,0:T(8,128)(2,1)S(1)}, bf16[8,8,8,128]{3,2,1,0:T(8,128)(2,1)S(1)}, u32[]{:S(2)}, u32[]{:S(2)}) collective-permute-start(bf16[8,8,8,128]{3,2,1,0:T(8,128)(2,1)S(1)} %get-tuple-element.60), channel_id=1, source_target_pairs={{0,16},{16,32},{32,48},{48,64},{64,80},{80,96},{96,112},{112,0},{1... | collective-permute-start | bytes 393224 | tf_op jit(solution)/shard_map/ppermute | solution.py:574
  69.0 4.8 %collective-permute-start.7 = (bf16[8,8,8,128]{3,2,1,0:T(8,128)(2,1)S(1)}, bf16[8,8,8,128]{3,2,1,0:T(8,128)(2,1)S(1)}, u32[]{:S(2)}, u32[]{:S(2)}) collective-permute-start(bf16[8,8,8,128]{3,2,1,0:T(8,128)(2,1)S(1)} %get-tuple-element.61), channel_id=1, source_target_pairs={{0,112},{16,0},{32,16},{48,32},{64,48},{80,64},{96,80},{112,96},{1... | collective-permute-start | bytes 393224 | tf_op jit(solution)/shard_map/ppermute | solution.py:574
  69.0 13.5 %collective-permute-start.4 = (bf16[12,8,16,128]{3,2,1,0:T(8,128)(2,1)S(1)}, bf16[12,8,16,128]{3,2,1,0:T(8,128)(2,1)S(1)}, u32[]{:S(2)}, u32[]{:S(2)}) collective-permute-start(bf16[12,8,16,128]{3,2,1,0:T(8,128)(2,1)S(1)} %get-tuple-element.58), channel_id=1, source_target_pairs={{0,1},{1,2},{2,3},{3,4},{4,5},{5,6},{6,7},{7,8},{8,9},{9,10},{10,1... | collective-permute-start | bytes 1179656 | tf_op jit(solution)/shard_map/ppermute | solution.py:574
  69.6 12.9 %collective-permute-start.5 = (bf16[12,8,16,128]{3,2,1,0:T(8,128)(2,1)S(1)}, bf16[12,8,16,128]{3,2,1,0:T(8,128)(2,1)S(1)}, u32[]{:S(2)}, u32[]{:S(2)}) collective-permute-start(bf16[12,8,16,128]{3,2,1,0:T(8,128)(2,1)S(1)} %get-tuple-element.59), channel_id=1, source_target_pairs={{0,15},{1,0},{2,1},{3,2},{4,3},{5,4},{6,5},{7,6},{8,7},{9,8},{10,9... | collective-permute-start | bytes 1179656 | tf_op jit(solution)/shard_map/ppermute | solution.py:574
  73.8 8.7 %collective-permute-start.8 = (bf16[3,8,16,128]{3,2,1,0:T(8,128)(2,1)S(1)}, bf16[3,8,16,128]{3,2,1,0:T(8,128)(2,1)S(1)}, u32[]{:S(2)}, u32[]{:S(2)}) collective-permute-start(bf16[3,8,16,128]{3,2,1,0:T(8,128)(2,1)S(1)} %get-tuple-element.62), channel_id=1, source_target_pairs={{0,1},{1,2},{2,3},{3,4},{4,5},{5,6},{6,7},{7,8},{8,9},{9,10},{10,1... | collective-permute-start | bytes 294920 | tf_op jit(solution)/shard_map/ppermute | solution.py:574
  74.4 8.1 %collective-permute-start.9 = (bf16[3,8,16,128]{3,2,1,0:T(8,128)(2,1)S(1)}, bf16[3,8,16,128]{3,2,1,0:T(8,128)(2,1)S(1)}, u32[]{:S(2)}, u32[]{:S(2)}) collective-permute-start(bf16[3,8,16,128]{3,2,1,0:T(8,128)(2,1)S(1)} %get-tuple-element.63), channel_id=1, source_target_pairs={{0,15},{1,0},{2,1},{3,2},{4,3},{5,4},{6,5},{7,6},{8,7},{9,8},{10,9... | collective-permute-start | bytes 294920 | tf_op jit(solution)/shard_map/ppermute | solution.py:574
